TPU v7x, 32 devices: a whole 2x2x4 slice. The times are simulated.
32 devices in a mesh: section: 2 (over x), head: 4 (over y, core), ctx: 4 (over z).
Axes of the slice: x: 2, y: 2, z: 4, core: 2. Of those that a mesh axis runs over, the one named last changes fastest.
Arguments:
- tokens: bfloat16 [2, 1024, 1536], P(None, ('head', 'ctx')), may hold values from -6 to 6
- positions: int32 [2, 1024], replicated, may hold values from 0 to 1023, as said below
- norm1_gain: bfloat16 [2, 1536], P('section', ('head', 'ctx')), may hold values from 0.25 to 1.75
- qkv_bias: bfloat16 [2, 2048], P('section', ('head', 'ctx')), may hold values from -3 to 3
- qkv_weight: bfloat16 [2, 1536, 2048], P('section', ('head', 'ctx')), may hold values from -0.15625 to 0.15625
- out_weight: bfloat16 [2, 1536, 1536], P('section', ('head', 'ctx')), may hold values from -1.75 to 1.75
- norm2_gain: bfloat16 [2, 1536], P('section', ('head', 'ctx')), may hold values from 0.25 to 1.75
- gate_up_weight: bfloat16 [2, 1536, 17920], P('section', ('head', 'ctx')), may hold values from -0.15625 to 0.15625
- down_weight: bfloat16 [2, 1536, 8960], P('section', ('head', 'ctx')), may hold values from -0.0625 to 0.0625
- cotangent: bfloat16 [2, 1024, 1536], P(None, ('head', 'ctx')), may hold values from -6 to 6
Outputs:
- activations: bfloat16 [2, 2, 1024, 1536], P('section', None, ('head', 'ctx'))
- input_grads: bfloat16 [2, 2, 1024, 1536], P('section', None, ('head', 'ctx'))
- norm1_gain_grad: float32 [2, 1536], P('section', ('head', 'ctx'))
- query_key_bias_grad: float32 [2, 1792], P('section', ('head', 'ctx'))
- value_bias_grad: float32 [2, 256], P('section', ('head', 'ctx'))
- qkv_weight_grad: float32 [2, 1536, 2048], P('section', ('head', 'ctx'))
- out_weight_grad: float32 [2, 1536, 1536], P('section', ('head', 'ctx'))
- norm2_gain_grad: float32 [2, 1536], P('section', ('head', 'ctx'))
- gate_up_grad: float32 [2, 1536, 17920], P('section', ('head', 'ctx'))
- down_grad: float32 [2, 1536, 8960], P('section', ('head', 'ctx'))
Inputs may be any that keep to these rules, and one draw needn't show every extreme that they name: Each micro-batch's positions are a permutation of 0 to 1023. The 256 tokens stored in the blocks h * 4 + c of 64 tokens, taken over all h in order, are two whole stretches of 128 consecutive positions in order: stretch i and stretch 2 * 4 - 1 - i, where which i belongs to which c is drawn for each micro-batch.
All inputs are finite; a program needn't handle non-finite values.
Results may differ from a plain program's by a relative error of at most 0.033.
Values may be sent and summed in bfloat16 or wider, within the bound.
A program may use at most 512 MiB of HBM per device.

v0:
```python
import math

import jax
import jax.numpy as jnp
from jax import lax
from jax.sharding import PartitionSpec as P

FF = 8960
QUERY_HEADS = 12
KEY_VALUE_HEADS = 2
HEAD_WIDTH_SIZE = 128


EPSILON = 1e-06
THETA = 1000000.0


def from_behind(value, axis, steps):
    count = lax.axis_size(axis)
    first, last = (max(0, -steps), min(count, count - steps))
    return lax.ppermute(value, axis, [(source, source + steps) for source in range(first, last)])


def rope_tables(position_ids, head_width):
    frequencies = THETA ** (-(jnp.arange(head_width // 2).astype(jnp.float32) * 2.0) / head_width)
    angles = position_ids.astype(jnp.float32)[..., None] * frequencies
    angles = jnp.concatenate([angles, angles], axis=-1)
    return (jnp.cos(angles)[..., None, :], jnp.sin(angles)[..., None, :])


def rotate(values, cosine_table, sine_table):
    half_width = values.shape[-1] // 2
    turned = jnp.concatenate([-values[..., half_width:], values[..., :half_width]], axis=-1)
    return values * cosine_table + turned * sine_table


def unrotate(grad_values, cosine_table, sine_table):
    half_width = grad_values.shape[-1] // 2
    scaled = grad_values * sine_table
    return grad_values * cosine_table + jnp.concatenate(
        [scaled[..., half_width:], -scaled[..., :half_width]], axis=-1
    )


def norm_rows(values, gain_row):
    inverse = lax.rsqrt(jnp.mean(values * values, axis=-1, keepdims=True) + EPSILON)
    return (values * inverse * gain_row, inverse)


def norm_back(values, inverse, gain_row, grad_values):
    weighted = grad_values * gain_row
    inner_mean = jnp.mean(weighted * values, axis=-1, keepdims=True)
    input_grad = inverse * weighted - values * inverse**3 * inner_mean
    gain_grad = jnp.sum((grad_values * values * inverse).reshape(-1, values.shape[-1]), axis=0)
    return (input_grad, gain_grad)


def pick(flag, first_tree, second_tree):
    return jax.tree.map(
        lambda left_side, right_side: jnp.where(flag, left_side, right_side),
        first_tree,
        second_tree,
    )


def masked_scores(queries, keys_now, query_pos, key_now):
    score_scale = 1.0 / math.sqrt(queries.shape[-1])
    allowed = (key_now[:, None, :] <= query_pos[:, :, None])[:, :, None, :]
    scores = (
        jnp.einsum("grhd,gkd->grhk", queries, keys_now, preferred_element_type=jnp.float32)
        * score_scale
    )
    return (jnp.where(allowed, scores, -1e30), allowed)


def attend_forward(queries, pair_group, query_pos, key_pos):
    head_width = queries.shape[-1]
    row_shape = queries.shape[:3]
    shard_piece = lax.all_gather(pair_group, "ctx", axis=1, tiled=True)
    running = jnp.full(row_shape, -1e30, jnp.float32)
    keys_now = shard_piece[:, :, 0, :head_width]
    values_now = shard_piece[:, :, 0, head_width:]
    scores, allowed = masked_scores(queries, keys_now, query_pos, key_pos)
    highest = jnp.maximum(running, jnp.max(scores, axis=-1))
    probs_now = jnp.where(allowed, jnp.exp(scores - highest[..., None]), 0.0)
    totals = jnp.sum(probs_now, axis=-1)
    accumulated = jnp.einsum(
        "grhk,gkd->grhd",
        probs_now.astype(jnp.bfloat16),
        values_now,
        preferred_element_type=jnp.float32,
    )
    running, totals, accumulated = (highest, totals, accumulated)
    return (accumulated / totals[..., None], running + jnp.log(totals))


def attend_backward(queries, pair_group, query_pos, key_pos, out_grads, lse_rows, delta_rows):
    head_width = queries.shape[-1]
    score_scale = 1.0 / math.sqrt(head_width)
    shard_piece = lax.all_gather(pair_group, "ctx", axis=1, tiled=True)
    keys_now = shard_piece[:, :, 0, :head_width]
    values_now = shard_piece[:, :, 0, head_width:]
    scores, allowed = masked_scores(queries, keys_now, query_pos, key_pos)
    probs_now = jnp.where(allowed, jnp.exp(scores - lse_rows[..., None]), 0.0)
    prob_grads = jnp.einsum(
        "grhd,gkd->grhk", out_grads, values_now, preferred_element_type=jnp.float32
    )
    score_grads = (probs_now * (prob_grads - delta_rows[..., None])).astype(jnp.bfloat16)
    query_grads = score_scale * jnp.einsum(
        "grhk,gkd->grhd", score_grads, keys_now, preferred_element_type=jnp.float32
    )
    key_part = score_scale * jnp.einsum(
        "grhk,grhd->gkd", score_grads, queries, preferred_element_type=jnp.float32
    )
    value_part = jnp.einsum(
        "grhk,grhd->gkd",
        probs_now.astype(jnp.bfloat16),
        out_grads,
        preferred_element_type=jnp.float32,
    )
    piece_term = jnp.concatenate([key_part, value_part], axis=-1)[:, :, None, :]
    return (query_grads, piece_term)


def layer_forward(inputs, own_pos, query_pos, key_pos, weights, heads_total):
    gain_one, bias_all, w_qkv, w_out, gain_two, w_gate_up, w_down = weights
    batch_length = inputs.shape[0]
    rows_total = inputs.shape[1]
    per_device = QUERY_HEADS // heads_total
    copy_count = heads_total // KEY_VALUE_HEADS
    query_columns = QUERY_HEADS * HEAD_WIDTH_SIZE
    key_columns = KEY_VALUE_HEADS * HEAD_WIDTH_SIZE
    residual = inputs.astype(jnp.float32)
    normed_one, inverse_one = norm_rows(residual, gain_one.astype(jnp.float32))
    normed_low = normed_one.astype(jnp.bfloat16)
    projected_rows = jnp.einsum(
        "grd,dc->grc", normed_low, w_qkv, preferred_element_type=jnp.float32
    ) + bias_all.astype(jnp.float32)
    cosine_table, sine_table = rope_tables(own_pos, HEAD_WIDTH_SIZE)
    queries = rotate(
        projected_rows[..., :query_columns].reshape(
            batch_length, rows_total, QUERY_HEADS, HEAD_WIDTH_SIZE
        ),
        cosine_table,
        sine_table,
    )
    key_row_block = rotate(
        projected_rows[..., query_columns : query_columns + key_columns].reshape(
            batch_length, rows_total, KEY_VALUE_HEADS, HEAD_WIDTH_SIZE
        ),
        cosine_table,
        sine_table,
    )
    value_row_block = projected_rows[..., query_columns + key_columns :].reshape(
        batch_length, rows_total, KEY_VALUE_HEADS, HEAD_WIDTH_SIZE
    )
    pair_rows = jnp.concatenate(
        [
            jnp.repeat(key_row_block, copy_count, axis=2),
            jnp.repeat(value_row_block, copy_count, axis=2),
        ],
        axis=-1,
    ).astype(jnp.bfloat16)
    query_send = queries.astype(jnp.bfloat16).reshape(
        batch_length, rows_total, heads_total, per_device * HEAD_WIDTH_SIZE
    )
    query_group, pair_group = (
        lax.all_to_all(query_send, "head", split_axis=2, concat_axis=1, tiled=True),
        lax.all_to_all(pair_rows, "head", split_axis=2, concat_axis=1, tiled=True),
    )
    group_rows = query_group.shape[1]
    query_group = query_group.reshape(batch_length, group_rows, per_device, HEAD_WIDTH_SIZE)
    attended, lse_rows = attend_forward(query_group, pair_group, query_pos, key_pos)
    out_send = attended.astype(jnp.bfloat16).reshape(
        batch_length, group_rows, 1, per_device * HEAD_WIDTH_SIZE
    )
    out_rows = lax.all_to_all(out_send, "head", split_axis=1, concat_axis=2, tiled=True).reshape(
        batch_length, rows_total, QUERY_HEADS * HEAD_WIDTH_SIZE
    )
    middle = residual + jnp.einsum(
        "grc,dc->grd", out_rows, w_out, preferred_element_type=jnp.float32
    )
    normed_two, inverse_two = norm_rows(middle, gain_two.astype(jnp.float32))
    normed_two_low = normed_two.astype(jnp.bfloat16)
    gate_up = jnp.einsum(
        "grd,dc->grc", normed_two_low, w_gate_up, preferred_element_type=jnp.float32
    )
    hidden_low = (jax.nn.silu(gate_up[..., :FF]) * gate_up[..., FF:]).astype(jnp.bfloat16)
    output = middle + jnp.einsum(
        "grf,df->grd", hidden_low, w_down, preferred_element_type=jnp.float32
    )
    kept_now = (
        residual,
        inverse_one,
        normed_low,
        query_group,
        pair_group,
        attended,
        lse_rows,
        out_rows,
        middle,
        inverse_two,
        normed_two_low,
        gate_up,
        hidden_low,
    )
    return (output, kept_now)


def layer_backward(out_grad, kept_now, own_pos, query_pos, key_pos, weights, heads_total):
    gain_one, bias_all, w_qkv, w_out, gain_two, w_gate_up, w_down = weights
    (
        residual,
        inverse_one,
        normed_low,
        query_group,
        pair_group,
        attended,
        lse_rows,
        out_rows,
        middle,
        inverse_two,
        normed_two_low,
        gate_up,
        hidden_low,
    ) = kept_now
    batch_length = out_grad.shape[0]
    rows_total = out_grad.shape[1]
    per_device = QUERY_HEADS // heads_total
    copy_count = heads_total // KEY_VALUE_HEADS
    branch_low = out_grad.astype(jnp.bfloat16)
    hidden_grad = jnp.einsum("grd,df->grf", branch_low, w_down, preferred_element_type=jnp.float32)
    gate_values = gate_up[..., :FF]
    up_values = gate_up[..., FF:]
    sigmoid_gate = jax.nn.sigmoid(gate_values)
    gate_grad = hidden_grad * up_values * sigmoid_gate * (1.0 + gate_values * (1.0 - sigmoid_gate))
    up_grad = hidden_grad * gate_values * sigmoid_gate
    gate_up_low = jnp.concatenate([gate_grad, up_grad], axis=-1).astype(jnp.bfloat16)
    normed_two_grad = jnp.einsum(
        "grc,dc->grd", gate_up_low, w_gate_up, preferred_element_type=jnp.float32
    )
    middle_part, gain_two_grad = norm_back(
        middle, inverse_two, gain_two.astype(jnp.float32), normed_two_grad
    )
    middle_grad = out_grad + middle_part
    middle_low = middle_grad.astype(jnp.bfloat16)
    out_grad_rows = jnp.einsum(
        "grd,dc->grc", middle_low, w_out, preferred_element_type=jnp.float32
    ).astype(jnp.bfloat16)
    out_grad_rows = out_grad_rows.reshape(
        batch_length, rows_total, heads_total, per_device * HEAD_WIDTH_SIZE
    )
    out_grad_group = lax.all_to_all(out_grad_rows, "head", split_axis=2, concat_axis=1, tiled=True)
    group_rows = out_grad_group.shape[1]
    out_grad_group = out_grad_group.reshape(batch_length, group_rows, per_device, HEAD_WIDTH_SIZE)
    delta_rows = jnp.sum(out_grad_group.astype(jnp.float32) * attended, axis=-1)
    query_grads, key_grads = attend_backward(
        query_group, pair_group, query_pos, key_pos, out_grad_group, lse_rows, delta_rows
    )
    pair_own = lax.psum_scatter(
        key_grads.astype(jnp.bfloat16), "ctx", scatter_dimension=1, tiled=True
    )
    query_send = query_grads.astype(jnp.bfloat16).reshape(
        batch_length, group_rows, 1, per_device * HEAD_WIDTH_SIZE
    )
    query_back, paired_backward = (
        lax.all_to_all(query_send, "head", split_axis=1, concat_axis=2, tiled=True),
        lax.all_to_all(pair_own, "head", split_axis=1, concat_axis=2, tiled=True),
    )
    query_rows = query_back.astype(jnp.float32).reshape(
        batch_length, rows_total, QUERY_HEADS, HEAD_WIDTH_SIZE
    )
    paired_sum = jnp.sum(
        paired_backward.astype(jnp.float32).reshape(
            batch_length, rows_total, KEY_VALUE_HEADS, copy_count, 2 * HEAD_WIDTH_SIZE
        ),
        axis=3,
    )
    cosine_table, sine_table = rope_tables(own_pos, HEAD_WIDTH_SIZE)
    query_pre = unrotate(query_rows, cosine_table, sine_table).reshape(
        batch_length, rows_total, QUERY_HEADS * HEAD_WIDTH_SIZE
    )
    key_pre = unrotate(paired_sum[..., :HEAD_WIDTH_SIZE], cosine_table, sine_table).reshape(
        batch_length, rows_total, KEY_VALUE_HEADS * HEAD_WIDTH_SIZE
    )
    value_before_rotation = paired_sum[..., HEAD_WIDTH_SIZE:].reshape(
        batch_length, rows_total, KEY_VALUE_HEADS * HEAD_WIDTH_SIZE
    )
    projected_low = jnp.concatenate([query_pre, key_pre, value_before_rotation], axis=-1).astype(
        jnp.bfloat16
    )
    bias_grad = jnp.sum(
        projected_low.astype(jnp.float32).reshape(-1, projected_low.shape[-1]), axis=0
    )
    normed_grad = jnp.einsum(
        "grc,dc->grd", projected_low, w_qkv, preferred_element_type=jnp.float32
    )
    input_part, gain_one_grad = norm_back(
        residual, inverse_one, gain_one.astype(jnp.float32), normed_grad
    )
    input_grad = middle_grad + input_part
    pieces = (
        normed_low,
        projected_low,
        middle_low,
        out_rows,
        normed_two_low,
        gate_up_low,
        branch_low,
        hidden_low,
    )
    return (input_grad, pieces, (gain_one_grad, bias_grad, gain_two_grad))


def reduce_block(left_side, columns):
    block_term = jnp.einsum("rd,rc->dc", left_side, columns, preferred_element_type=jnp.float32)
    return lax.psum_scatter(block_term, ("head", "ctx"), scatter_dimension=0, tiled=True)


def local(
    tokens,
    positions,
    norm1_gain,
    qkv_bias,
    qkv_weight,
    out_weight,
    norm2_gain,
    gate_up_weight,
    down_weight,
    cotangent,
):
    heads_total = lax.axis_size("head")
    rank_count = lax.axis_size("ctx")
    batch_count = tokens.shape[0]
    rows_total = tokens.shape[1]
    seq_total = positions.shape[1]
    group_rows = heads_total * rows_total
    section_index = lax.axis_index("section")
    rank_index = lax.axis_index("ctx")
    block_index = lax.axis_index("head") * rank_count + rank_index
    ordered = (
        positions.reshape(batch_count, heads_total, rank_count, rows_total)
        .transpose(0, 2, 1, 3)
        .reshape(batch_count, seq_total)
    )
    group_count = batch_count // batch_count
    tick_count = group_count + 1

    def positions_for(group_index):
        first_row = group_index * batch_count
        own_pos = lax.dynamic_slice(
            positions, (first_row, block_index * rows_total), (batch_count, rows_total)
        )
        query_pos = lax.dynamic_slice_in_dim(ordered, rank_index * group_rows, group_rows, 1)
        return (own_pos, query_pos, ordered)

    shards = (norm1_gain, qkv_bias, qkv_weight, out_weight, norm2_gain, gate_up_weight, down_weight)
    weights = tuple(
        (
            shard_value[0]
            for shard_value in (
                lax.all_gather(shards[0], ("head", "ctx"), axis=1, tiled=True),
                lax.all_gather(shards[1], ("head", "ctx"), axis=1, tiled=True),
                lax.all_gather(shards[2], ("head", "ctx"), axis=1, tiled=True),
                lax.all_gather(shards[3], ("head", "ctx"), axis=1, tiled=True),
                lax.all_gather(shards[4], ("head", "ctx"), axis=1, tiled=True),
                lax.all_gather(shards[5], ("head", "ctx"), axis=1, tiled=True),
                lax.all_gather(shards[6], ("head", "ctx"), axis=1, tiled=True),
            )
        )
    )
    received = jnp.zeros((batch_count, rows_total, tokens.shape[2]), jnp.bfloat16)
    outputs = []
    kept_list = []
    for tick_now in range(tick_count):
        first_row = min(tick_now, group_count - 1) * batch_count
        inputs = jnp.where(section_index == 0, tokens, received)
        own_pos, query_pos, key_pos = positions_for(
            jnp.clip(tick_now - section_index, 0, group_count - 1)
        )
        result, kept_now = layer_forward(inputs, own_pos, query_pos, key_pos, weights, heads_total)
        result_low = result.astype(jnp.bfloat16)
        outputs.append(result_low)
        kept_list.append(kept_now)
        if tick_now + 1 < tick_count:
            received = from_behind(result_low, "section", 1)
    received = jnp.zeros((batch_count, rows_total, tokens.shape[2]), jnp.bfloat16)
    grads_in = []
    piece_list = []
    small_sums = None
    for tick_now in range(tick_count):
        first_row = min(tick_now, group_count - 1) * batch_count
        incoming = jnp.where(section_index == 1, cotangent, received).astype(jnp.float32)
        kept_now = pick(
            section_index == 0,
            kept_list[max(tick_now - 1, 0)],
            kept_list[min(tick_now + 1, tick_count - 1)],
        )
        group_number = tick_now - 1 + section_index
        own_pos, query_pos, key_pos = positions_for(jnp.clip(group_number, 0, group_count - 1))
        input_grad, pieces, smalls = layer_backward(
            incoming, kept_now, own_pos, query_pos, key_pos, weights, heads_total
        )
        valid_flag = jnp.logical_and(group_number >= 0, group_number < group_count)
        smalls = tuple((jnp.where(valid_flag, entry_value, 0.0) for entry_value in smalls))
        if small_sums is None:
            small_sums = smalls
        else:
            small_sums = tuple(
                (left_side + right_side for left_side, right_side in zip(small_sums, smalls))
            )
        grad_low = input_grad.astype(jnp.bfloat16)
        grads_in.append(grad_low)
        piece_list.append(pieces)
        if tick_now + 1 < tick_count:
            received = from_behind(grad_low, "section", -1)
    activations = jnp.where(section_index == 0, outputs[0], outputs[1])[None]
    input_grads = jnp.where(section_index == 0, grads_in[1], grads_in[0])[None]
    chosen = [pick(section_index == 0, piece_list[1], piece_list[0])]
    merged = tuple(
        (
            jnp.concatenate([chosen_set[slot_number] for chosen_set in chosen], axis=0).reshape(
                batch_count * rows_total, -1
            )
            for slot_number in range(8)
        )
    )
    (
        normed_all,
        projected_all,
        middle_all,
        attn_all,
        normed_two_all,
        gate_up_all,
        branch_all,
        hidden_all,
    ) = merged
    pair_list = (
        (normed_all, projected_all),
        (middle_all, attn_all),
        (normed_two_all, gate_up_all),
        (branch_all, hidden_all),
    )
    share_list = []
    for left_side, right_side in pair_list:
        width_total = right_side.shape[1]
        piece_count = width_total // 4480 if width_total % 4480 == 0 else 1
        piece_width = width_total // piece_count
        piece_shares = []
        for piece_number in range(piece_count):
            columns = right_side[:, piece_number * piece_width : (piece_number + 1) * piece_width]
            piece_shares.append(reduce_block(left_side, columns))
        share_list.append(jnp.concatenate(piece_shares, axis=1)[None])
    qkv_weight_grad, out_weight_grad, gate_up_grad, down_grad = share_list
    split_width = (QUERY_HEADS + KEY_VALUE_HEADS) * HEAD_WIDTH_SIZE
    bias_sum = small_sums[1]
    gain_one_share, query_key_share, value_share, gain_two_share = (
        lax.psum_scatter(small_sums[0][None], ("head", "ctx"), scatter_dimension=1, tiled=True),
        lax.psum_scatter(
            bias_sum[None, :split_width], ("head", "ctx"), scatter_dimension=1, tiled=True
        ),
        lax.psum_scatter(
            bias_sum[None, split_width:], ("head", "ctx"), scatter_dimension=1, tiled=True
        ),
        lax.psum_scatter(small_sums[2][None], ("head", "ctx"), scatter_dimension=1, tiled=True),
    )
    return (
        activations,
        input_grads,
        gain_one_share,
        query_key_share,
        value_share,
        qkv_weight_grad,
        out_weight_grad,
        gain_two_share,
        gate_up_grad,
        down_grad,
    )


def solution(mesh):
    placed = (
        P(None, ("head", "ctx"), None),
        P(),
        P("section", ("head", "ctx")),
        P("section", ("head", "ctx")),
        P("section", ("head", "ctx"), None),
        P("section", ("head", "ctx"), None),
        P("section", ("head", "ctx")),
        P("section", ("head", "ctx"), None),
        P("section", ("head", "ctx"), None),
        P(None, ("head", "ctx"), None),
    )
    return jax.shard_map(
        local,
        mesh=mesh,
        in_specs=placed,
        out_specs=(
            P("section", None, ("head", "ctx"), None),
            P("section", None, ("head", "ctx"), None),
            P("section", ("head", "ctx")),
            P("section", ("head", "ctx")),
            P("section", ("head", "ctx")),
            P("section", ("head", "ctx"), None),
            P("section", ("head", "ctx"), None),
            P("section", ("head", "ctx")),
            P("section", ("head", "ctx"), None),
            P("section", ("head", "ctx"), None),
        ),
        check_vma=False,
    )
```

profile of v0, /device:TPU:14, one launch (start us, length us, event | category | flops | bytes accessed | tf_op | source)
XLA Modules:
  0.0 3052.7 jit_solution(2973088783849526908)
XLA Ops:
  8.0 29.2 all_gather.33
  40.8 35.5 %all-reduce.2 = (bf16[1536]{0:T(1024)(128)(2,1)S(1)}, bf16[1536]{0:T(1024)(128)(2,1)}) all-reduce(bf16[1536]{0:T(1024)(128)(2,1)S(1)} %dynamic-update-slice, bf16[1536]{0:T(1024)(128)(2,1)S(1)} %dynamic-update-slice.1), channel_id=1, replica_groups=mesh['section'=2,'head'=4,'ctx'=4] {'head','ctx'}, use_global_device_ids=true, to_apply=%add | all-reduce | flops 3072 | bytes 12288
  82.5 7.8 all_to_all.162
  104.7 5.4 all-to-all-done
  111.1 7.4 all-gather.10.cloned.1.call-done
  131.8 10.3 all-gather.18.cloned.1.call-start
  142.7 31.3 %all-gather.12.cloned.1.call-done = bf16[1,1536,1536]{2,1,0:T(8,128)(2,1)} async-done(((bf16[1,96,1536]{2,1,0:T(8,128)(2,1)}), bf16[1,1536,1536]{2,1,0:T(8,128)(2,1)}) %all-gather.12.cloned.1.call-update) | async-done | bytes 4718608 | tf_op jit(solution)/shard_map/all_gather | solution.py:365
  178.1 281.7 %all-gather.14.cloned.1.call-done = bf16[1,1536,17920]{2,1,0:T(8,128)(2,1)} async-done(((bf16[1,96,17920]{2,1,0:T(8,128)(2,1)}), bf16[1,1536,17920]{2,1,0:T(8,128)(2,1)}) %all-gather.14.cloned.1.call-update) | async-done | bytes 55050256 | tf_op jit(solution)/shard_map/all_gather | solution.py:367
  459.8 23.9 fusion.6
  483.7 125.1 %all-gather.16.cloned.1.call-done = bf16[1,1536,8960]{2,1,0:T(8,128)(2,1)} async-done(((bf16[1,96,8960]{2,1,0:T(8,128)(2,1)}), bf16[1,1536,8960]{2,1,0:T(8,128)(2,1)}) %all-gather.16.cloned.1.call-update) | async-done | bytes 27525136 | tf_op jit(solution)/shard_map/all_gather | solution.py:368
  608.9 15.8 fusion.73
  626.0 12.3 collective-permute-done
  643.5 7.5 all_to_all.163
  657.5 5.1 all-to-all-start.3
  669.4 11.0 all-gather.18.cloned.1.call-done
  705.1 26.7 broadcast_select_fusion
  731.9 16.5 multiply_convert_fusion.5
  748.4 26.5 multiply_reduce_fusion.1
  784.7 6.2 exponential_select_fusion
  812.0 5.6 all-to-all-done.7
  823.9 5.9 reduce-scatter.23.cloned.1.call-done
  840.5 5.4 multiply_reduce_fusion.3
  848.8 8.4 collective-permute-done.1
  858.0 16.5 multiply_convert_fusion.3
  874.4 24.7 multiply_reduce_fusion
  903.3 5.4 all-to-all-start.9
  909.0 5.7 all-to-all-done.9
  928.9 9.9 broadcast_select_fusion.1
  975.5 6.0 multiply_reduce_fusion.2
  985.1 12.4 fusion.118
  997.6 12.3 fusion.120
  1018.7 11.2 fusion.122
  1029.9 12.3 fusion.124
  1042.5 12.4 fusion.126
  1054.9 12.3 fusion.128
  1068.3 6.1 convolution_bitcast_fusion
  1075.6 6.5 convolution_bitcast_fusion.1
  1083.1 15.5 fusion.85
  1103.5 30.5 reduce-scatter.43.cloned.1.call-done
  1135.3 58.8 %reduce-scatter.45.cloned.1.call-done = f32[112,1]{1,0:T(8,128)} async-done(((f32[1792,1]{1,0:T(8,128)}), f32[112,1]{1,0:T(8,128)}) %reduce-scatter.45.cloned.1.call-update) | async-done | bytes 464
  1195.5 263.4 %reduce-scatter.41.cloned.1.call-done = f32[96,4480]{1,0:T(8,128)} async-done(((f32[1536,4480]{1,0:T(8,128)}), f32[96,4480]{1,0:T(8,128)}) %reduce-scatter.41.cloned.1.call-update) | async-done | bytes 1720336 | tf_op jit(solution)/shard_map/reduce_scatter | solution.py:317
  1458.9 265.9 %reduce-scatter.39.cloned.1.call-done = f32[96,4480]{1,0:T(8,128)} async-done(((f32[1536,4480]{1,0:T(8,128)}), f32[96,4480]{1,0:T(8,128)}) %reduce-scatter.39.cloned.1.call-update) | async-done | bytes 1720336 | tf_op jit(solution)/shard_map/reduce_scatter | solution.py:317
  1728.8 262.5 %reduce-scatter.37.cloned.1.call-done = f32[96,4480]{1,0:T(8,128)} async-done(((f32[1536,4480]{1,0:T(8,128)}), f32[96,4480]{1,0:T(8,128)}) %reduce-scatter.37.cloned.1.call-update) | async-done | bytes 1720336 | tf_op jit(solution)/shard_map/reduce_scatter | solution.py:317
  1991.3 265.9 %reduce-scatter.35.cloned.1.call-done = f32[96,4480]{1,0:T(8,128)} async-done(((f32[1536,4480]{1,0:T(8,128)}), f32[96,4480]{1,0:T(8,128)}) %reduce-scatter.35.cloned.1.call-update) | async-done | bytes 1720336 | tf_op jit(solution)/shard_map/reduce_scatter | solution.py:317
  2257.3 266.5 %reduce-scatter.33.cloned.1.call-done = f32[96,4480]{1,0:T(8,128)} async-done(((f32[1536,4480]{1,0:T(8,128)}), f32[96,4480]{1,0:T(8,128)}) %reduce-scatter.33.cloned.1.call-update) | async-done | bytes 1720336 | tf_op jit(solution)/shard_map/reduce_scatter | solution.py:317
  2523.8 266.1 %reduce-scatter.31.cloned.1.call-done = f32[96,4480]{1,0:T(8,128)} async-done(((f32[1536,4480]{1,0:T(8,128)}), f32[96,4480]{1,0:T(8,128)}) %reduce-scatter.31.cloned.1.call-update) | async-done | bytes 1720336 | tf_op jit(solution)/shard_map/reduce_scatter | solution.py:317
  2794.9 112.5 %reduce-scatter.29.cloned.1.call-done = f32[96,1536]{1,0:T(8,128)} async-done(((f32[1536,1536]{1,0:T(8,128)}), f32[96,1536]{1,0:T(8,128)}) %reduce-scatter.29.cloned.1.call-update) | async-done | bytes 589840 | tf_op jit(solution)/shard_map/reduce_scatter | solution.py:317
  2907.4 138.3 %reduce-scatter.27.cloned.1.call-done = f32[96,2048]{1,0:T(8,128)} async-done(((f32[1536,2048]{1,0:T(8,128)}), f32[96,2048]{1,0:T(8,128)}) %reduce-scatter.27.cloned.1.call-update) | async-done | bytes 786448 | tf_op jit(solution)/shard_map/reduce_scatter | solution.py:317
  (413 shorter events, 225.6 us)
Async XLA Ops:
  7.2 70.6 %all-gather.8.cloned.1.call-start = ((), (), s32[]{:S(2)}) async-start(), calls=%async_computation.26 | async-start | bytes 6684672 | tf_op jit(solution)/shard_map/all_gather | solution.py:364
  7.9 110.6 %all-gather.10.cloned.1.call-start = ((), (), s32[]{:S(2)}) async-start(), calls=%async_computation.27 | async-start | bytes 1310720 | tf_op jit(solution)/shard_map/all_gather | solution.py:79
  77.5 565.8 %copy-start.44 = (f32[2,64,128]{2,1,0:T(8,128)}, f32[2,64,128]{2,1,0:T(8,128)S(1)}, u32[]{:S(2)}) copy-start(f32[2,64,128]{2,1,0:T(8,128)S(1)} %get-tuple-element.53) | copy-start | bytes 196612
  77.5 575.9 %copy-start.26 = (f32[2,64,128]{2,1,0:T(8,128)}, f32[2,64,128]{2,1,0:T(8,128)S(1)}, u32[]{:S(2)}) copy-start(f32[2,64,128]{2,1,0:T(8,128)S(1)} %get-tuple-element.54) | copy-start | bytes 196612
  91.1 82.9 %all-gather.12.cloned.1.call-start = ((), (), s32[]{:S(2)}) async-start(), calls=%async_computation.28 | async-start | bytes 5013504 | tf_op jit(solution)/shard_map/all_gather | solution.py:365
  91.8 368.0 %all-gather.14.cloned.1.call-start = ((), (), s32[]{:S(2)}) async-start(), calls=%async_computation.29 | async-start | bytes 58490880 | tf_op jit(solution)/shard_map/all_gather | solution.py:367
  92.4 516.5 %all-gather.16.cloned.1.call-start = ((), (), s32[]{:S(2)}) async-start(), calls=%async_computation.30 | async-start | bytes 29245440 | tf_op jit(solution)/shard_map/all_gather | solution.py:368
  99.2 10.9 all-to-all-start
  104.7 580.8 %copy-start.16 = (pred[2,256,1024]{2,1,0:T(8,128)(4,1)}, pred[2,256,1024]{2,1,0:T(8,128)(4,1)S(1)}, u32[]{:S(2)}) copy-start(pred[2,256,1024]{2,1,0:T(8,128)(4,1)S(1)} %broadcast_compare_fusion) | copy-start | bytes 1572868
  123.6 50.3 %copy-start.5 = (bf16[2,64,1536]{2,1,0:T(8,128)(2,1)S(1)}, bf16[2,64,1536]{2,1,0:T(8,128)(2,1)}, u32[]{:S(2)}) copy-start(bf16[2,64,1536]{2,1,0:T(8,128)(2,1)} %param.10) | copy-start | bytes 1179652
  127.8 14.3 all-to-all-start.2
  131.8 548.6 %all-gather.18.cloned.1.call-start = ((), (), s32[]{:S(2)}) async-start(), calls=%async_computation.31 | async-start | bytes 1310720 | tf_op jit(solution)/shard_map/all_gather | solution.py:79
  142.7 341.1 %copy-start.35 = (bf16[2,64,1536]{2,1,0:T(8,128)(2,1)}, bf16[2,64,1536]{2,1,0:T(8,128)(2,1)S(1)}, u32[]{:S(2)}) copy-start(bf16[2,64,1536]{2,1,0:T(8,128)(2,1)S(1)} %reshape.538) | copy-start | bytes 1179652
  178.0 430.8 %copy-start.17 = (f32[2,64,1536]{2,1,0:T(8,128)}, f32[2,64,1536]{2,1,0:T(8,128)S(1)}, u32[]{:S(2)}) copy-start(f32[2,64,1536]{2,1,0:T(8,128)S(1)} %get-tuple-element.62) | copy-start | bytes 2359300
  178.0 305.7 %copy-start.62 = (f32[2,64]{1,0:T(2,128)}, f32[2,64]{1,0:T(2,128)S(1)}, u32[]{:S(2)}) copy-start(f32[2,64]{1,0:T(2,128)S(1)} %add_rsqrt_fusion.2) | copy-start | bytes 1540
  624.7 13.6 collective-permute-start
  638.6 61.6 %copy-start.13 = (bf16[2,64,1536]{2,1,0:T(8,128)(2,1)}, bf16[2,64,1536]{2,1,0:T(8,128)(2,1)S(1)}, u32[]{:S(2)}) copy-start(bf16[2,64,1536]{2,1,0:T(8,128)(2,1)S(1)} %get-tuple-element.30) | copy-start | bytes 1179652
  657.5 10.9 all-to-all-start.3
  662.6 122.1 %all-gather.20.cloned.1.call-start = ((), (), s32[]{:S(2)}) async-start(), calls=%async_computation.32 | async-start | bytes 1310720 | tf_op jit(solution)/shard_map/all_gather | solution.py:100
  689.7 10.0 all-to-all-start.5
  700.2 31.6 %copy-start.36 = (bf16[2,64,1536]{2,1,0:T(8,128)(2,1)}, bf16[2,64,1536]{2,1,0:T(8,128)(2,1)S(1)}, u32[]{:S(2)}) copy-start(bf16[2,64,1536]{2,1,0:T(8,128)(2,1)S(1)} %reshape.547) | copy-start | bytes 1179652
  704.4 27.4 copy-start.3
  705.1 26.7 copy-start.64
  705.1 26.7 copy-start.50
  731.9 45.5 %slice-start.4 = ((s8[4718592]{0:T(1024)(128)(4,1)}), s8[4194304]{0:T(1024)(128)(4,1)S(1)}, s32[]{:S(2)}) async-start(s8[4718592]{0:T(1024)(128)(4,1)} %bitcast.422), calls=%async_computation.51 | async-start | bytes 8388608
  748.4 29.0 slice-start.5
  779.1 11.7 all-to-all-start.6
  784.2 45.6 %reduce-scatter.23.cloned.1.call-start = ((), (), s32[]{:S(2)}) async-start(), calls=%async_computation.33 | async-start | bytes 1310720 | tf_op jit(solution)/shard_map/reduce_scatter | solution.py:260
  807.6 10.0 all-to-all-start.7
  831.6 8.4 all-to-all-start.8
  846.3 10.9 collective-permute-start.1
  874.4 24.7 copy-start.74
  903.3 11.3 all-to-all-start.9
  908.8 54.8 %reduce-scatter.25.cloned.1.call-start = ((), (), s32[]{:S(2)}) async-start(), calls=%async_computation.34 | async-start | bytes 1310720 | tf_op jit(solution)/shard_map/reduce_scatter | solution.py:260
  943.2 10.9 all-to-all-start.10
  948.3 150.3 %reduce-scatter.49.cloned.1.call-start = ((), (), s32[]{:S(2)}) async-start(), calls=%async_computation.46 | async-start | bytes 835584
  965.5 9.4 all-to-all-start.11
  970.5 131.7 %reduce-scatter.47.cloned.1.call-start = ((), (), s32[]{:S(2)}) async-start(), calls=%async_computation.45 | async-start | bytes 139264
  982.5 151.5 %reduce-scatter.43.cloned.1.call-start = ((), (), s32[]{:S(2)}) async-start(), calls=%async_computation.43 | async-start | bytes 835584
  983.7 210.4 %reduce-scatter.45.cloned.1.call-start = ((), (), s32[]{:S(2)}) async-start(), calls=%async_computation.44 | async-start | bytes 974848
  985.0 473.8 %reduce-scatter.41.cloned.1.call-start = ((), (), s32[]{:S(2)}) async-start(), calls=%async_computation.42 | async-start | bytes 29245440 | tf_op jit(solution)/shard_map/reduce_scatter | solution.py:317
  997.5 727.3 %reduce-scatter.39.cloned.1.call-start = ((), (), s32[]{:S(2)}) async-start(), calls=%async_computation.41 | async-start | bytes 29245440 | tf_op jit(solution)/shard_map/reduce_scatter | solution.py:317
  1009.9 981.4 %reduce-scatter.37.cloned.1.call-start = ((), (), s32[]{:S(2)}) async-start(), calls=%async_computation.40 | async-start | bytes 29245440 | tf_op jit(solution)/shard_map/reduce_scatter | solution.py:317
  1029.9 1227.4 %reduce-scatter.35.cloned.1.call-start = ((), (), s32[]{:S(2)}) async-start(), calls=%async_computation.39 | async-start | bytes 29245440 | tf_op jit(solution)/shard_map/reduce_scatter | solution.py:317
  1042.2 1481.5 %reduce-scatter.33.cloned.1.call-start = ((), (), s32[]{:S(2)}) async-start(), calls=%async_computation.38 | async-start | bytes 29245440 | tf_op jit(solution)/shard_map/reduce_scatter | solution.py:317
  1054.8 1735.0 %reduce-scatter.31.cloned.1.call-start = ((), (), s32[]{:S(2)}) async-start(), calls=%async_computation.37 | async-start | bytes 29245440 | tf_op jit(solution)/shard_map/reduce_scatter | solution.py:317
  1067.2 1840.2 %reduce-scatter.29.cloned.1.call-start = ((), (), s32[]{:S(2)}) async-start(), calls=%async_computation.36 | async-start | bytes 10027008 | tf_op jit(solution)/shard_map/reduce_scatter | solution.py:317
  1074.5 1971.2 %reduce-scatter.27.cloned.1.call-start = ((), (), s32[]{:S(2)}) async-start(), calls=%async_computation.35 | async-start | bytes 13369344 | tf_op jit(solution)/shard_map/reduce_scatter | solution.py:317
  (67 other events, 470.4 us)
Sparse Core Ops, SparseCore 0:
  10.3 63.0 all-gather.7
  91.2 27.3 all-gather.9
  120.9 53.0 all-gather.11
  175.4 284.3 all-gather.13
  461.2 147.6 all-gather.15
  651.8 28.5 all-gather.17
  682.6 27.4 all-gather.19
  803.5 26.2 reduce-scatter.22
  929.0 26.9 reduce-scatter.24
  959.4 57.1 reduce-scatter.48
  1020.5 54.0 reduce-scatter.46
  1078.4 55.5 reduce-scatter.42
  1138.1 55.9 reduce-scatter.44
  1198.6 260.1 reduce-scatter.40
  1462.8 261.9 reduce-scatter.38
  1729.3 261.9 reduce-scatter.36
  1995.3 261.9 reduce-scatter.34
  2261.8 261.9 reduce-scatter.32
  2527.9 261.9 reduce-scatter.30
  2794.9 112.3 reduce-scatter.28
  2912.0 133.6 reduce-scatter.26
where the time goes:
time: 3070 us; the launch traced here: 3050 us
  waiting for transfers between devices  2450 us (80%)
  matrix products  316 us (10%)
  blocking collectives  80 us (3%)
  local copies, waits for them, and re-layouts  65.6 us (2%)
  starting transfers between devices  63.3 us (2%)
  other arithmetic  62.2 us (2%)
    reduce_scatter x8, waiting for transfers between devices, reduce_block(): lax.psum_scatter(block_term, ('head', 'ctx'), scatter_dimension=0, tiled=...  1840 us
    all_gather x1, waiting for transfers between devices, local(): lax.all_gather(shards[5], ('head', 'ctx'), axis=1, tiled=True)  282 us
    all_gather x1, waiting for transfers between devices, local(): lax.all_gather(shards[6], ('head', 'ctx'), axis=1, tiled=True)  125 us
    unnamed x25, waiting for transfers between devices  92 us
    dot_general x8, matrix products, reduce_block(): jnp.einsum('rd,rc->dc', left_side, columns, preferred_element_type=jnp.fl...  85.4 us
  transfers between devices with their start and end apart: 33, of which 26 were waited for; matrix products, arithmetic and copies ran while one was open for 11% of the time, Pallas kernels for 0%

commit v1 on v0

--- a/solution.py
+++ b/solution.py
@@ -1,8 +1,11 @@
+import functools
 import math
 
 import jax
 import jax.numpy as jnp
 from jax import lax
+from jax.experimental import pallas as pl
+from jax.experimental.pallas import tpu as pltpu
 from jax.sharding import PartitionSpec as P
 
 FF = 8960
@@ -478,6 +481,1433 @@
     )
 
 
+MESH_ID = pl.DeviceIdType.MESH
+BF = jnp.bfloat16
+F32 = jnp.float32
+LANES = 128
+HB = 128
+VMEM_LIMIT = 60 * 1024 * 1024
+DMA = pltpu.SemaphoreType.DMA
+NT = (((1,), (1,)), ((), ()))
+TN = (((0,), (0,)), ((), ()))
+NN = (((1,), (0,)), ((), ()))
+
+
+def mm(left_side, right_side, form=NN):
+    return lax.dot_general(left_side, right_side, form, preferred_element_type=F32)
+
+
+def where_am_i():
+    head = lax.axis_index("head")
+    return (lax.axis_index("section"), head // 2, lax.rem(head, 2), lax.axis_index("ctx"))
+
+
+def at(x, y, k, z):
+    return (x, y * 2 + k, z)
+
+
+def remote(source, target, send_sem, recv_sem, device):
+    return pltpu.make_async_remote_copy(
+        src_ref=source,
+        dst_ref=target,
+        send_sem=send_sem,
+        recv_sem=recv_sem,
+        device_id=device,
+        device_id_type=MESH_ID,
+    )
+
+
+def arrived(ref, sem):
+    pltpu.make_async_copy(ref, ref, sem).wait()
+
+
+def greet(devices):
+    barrier = pltpu.get_barrier_semaphore()
+    for device in devices:
+        pl.semaphore_signal(barrier, inc=1, device_id=device, device_id_type=MESH_ID)
+    pl.semaphore_wait(barrier, len(devices))
+
+
+def greet_all(index, total, device_of):
+    barrier = pltpu.get_barrier_semaphore()
+
+    @pl.loop(1, total)
+    def _(step):
+        device = device_of(lax.rem(index + step, total))
+        pl.semaphore_signal(barrier, inc=1, device_id=device, device_id_type=MESH_ID)
+
+    pl.semaphore_wait(barrier, total - 1)
+
+
+def params(collective_id):
+    return pltpu.CompilerParams(
+        collective_id=collective_id, has_side_effects=True, vmem_limit_bytes=VMEM_LIMIT
+    )
+
+
+def vmem():
+    return pl.BlockSpec(memory_space=pltpu.VMEM)
+
+
+def hbm():
+    return pl.BlockSpec(memory_space=pl.ANY)
+
+
+def row_norm(values):
+    return lax.rsqrt(jnp.mean(values * values, axis=-1, keepdims=True) + EPSILON)
+
+
+class Sizes:
+    def __init__(self, mesh, tokens, qkv_weight, gate_up, down):
+        self.ctx = mesh.shape["ctx"]
+        self.group = 4 * self.ctx
+        self.total = 2 * self.group
+        self.batches, self.seq, self.width = tokens.shape
+        self.rows = self.seq // self.group
+        self.ff = down.shape[2]
+        self.owned = self.width // self.group
+        self.blocks = self.ff // HB
+        self.most = -(-self.blocks // self.total)
+        self.least = self.blocks // self.total
+        self.extra = self.blocks % self.total
+        self.hidden = self.most * HB
+        self.per_group = QUERY_HEADS // 4
+        self.qcols = self.per_group * HEAD_WIDTH_SIZE
+        self.kcols = HEAD_WIDTH_SIZE
+        self.acols = self.qcols + 2 * self.kcols
+        self.atot = self.acols + self.qcols
+
+    def fits(self):
+        gathered = self.batches * self.seq * self.width * 2
+        return (
+            self.batches == 2
+            and gathered * 3 < VMEM_LIMIT // 2
+            and self.ff % HB == 0
+            and self.least >= 1
+            and self.owned % 16 == 0
+            and self.rows % 32 == 0
+        )
+
+
+def flat_place(index, group, ctx):
+    inside = lax.rem(index, group)
+    return (index // group, inside // ctx, lax.rem(inside, ctx))
+
+
+def first_column(sz, owner):
+    return pl.multiple_of((owner * sz.least + jnp.minimum(owner, sz.extra)) * HB, HB)
+
+
+def spread_kernel(
+    sz,
+    small,
+    tokens,
+    cotangent,
+    qkv,
+    out_w,
+    gate_up,
+    down,
+    small_all,
+    tok_own,
+    cot_own,
+    att_all,
+    w_all,
+    zeros,
+    s_small,
+    r_small,
+    s_own,
+    r_own,
+    s_att,
+    r_att,
+    s_fwd,
+    r_fwd,
+    s_mlp,
+    r_mlp,
+    z_sem,
+):
+    n = sz.ctx
+    x, y, k, z = where_am_i()
+    me = x * sz.group + (y * 2 + k) * n + z
+    row = pl.multiple_of(((y * 2 + k) * n + z) * sz.owned, 16)
+    rows = pl.ds(row, sz.owned)
+    place = lambda index: flat_place(index, sz.group, n)
+    greet_all(me, sz.total, place)
+
+    @pl.loop(1, sz.total)
+    def _(step):
+        remote(small, small_all.at[me], s_small, r_small, place(lax.rem(me + step, sz.total))).start()
+
+    pltpu.make_async_copy(small, small_all.at[me], s_small).start()
+
+    def owns(begin):
+        @pl.when(x == y)
+        def _():
+            for batch in range(2):
+                pairs = ((tokens, tok_own, 0), (cotangent, cot_own, 1))
+                for source, target, slot in pairs:
+                    own = jnp.logical_and(k == y, k == batch)
+
+                    @pl.when(jnp.logical_not(own))
+                    def _():
+                        copy = remote(
+                            source.at[batch],
+                            target,
+                            s_own.at[batch, slot],
+                            r_own.at[slot],
+                            at(x, k, batch, z),
+                        )
+                        copy.start() if begin else copy.wait_send()
+
+                    if begin:
+
+                        @pl.when(own)
+                        def _():
+                            pltpu.make_async_copy(source.at[batch], target, r_own.at[slot]).start()
+
+    owns(True)
+
+    mine = (2 * x + y) * n + z
+
+    def att_parts(g):
+        kv = g // (4 // KEY_VALUE_HEADS)
+        q0 = pl.multiple_of(g * sz.qcols, HB)
+        k0 = pl.multiple_of(QUERY_HEADS * HEAD_WIDTH_SIZE + kv * sz.kcols, HB)
+        v0 = pl.multiple_of((QUERY_HEADS + KEY_VALUE_HEADS) * HEAD_WIDTH_SIZE + kv * sz.kcols, HB)
+        return (
+            (qkv.at[:, pl.ds(q0, sz.qcols)], att_all.at[x, rows, pl.ds(0, sz.qcols)]),
+            (qkv.at[:, pl.ds(k0, sz.kcols)], att_all.at[x, rows, pl.ds(sz.qcols, sz.kcols)]),
+            (
+                qkv.at[:, pl.ds(v0, sz.kcols)],
+                att_all.at[x, rows, pl.ds(sz.qcols + sz.kcols, sz.kcols)],
+            ),
+            (out_w.at[:, pl.ds(q0, sz.qcols)], att_all.at[x, rows, pl.ds(sz.acols, sz.qcols)]),
+        )
+
+    @pl.loop(1, sz.group)
+    def _(step):
+        index = lax.rem(mine + step, sz.group)
+        g = index // n
+        for source, target in att_parts(g):
+            remote(
+                source, target, s_att, r_att.at[x], at(g // 2, lax.rem(g, 2), k, lax.rem(index, n))
+            ).start()
+
+    for source, target in att_parts(2 * x + y):
+        pltpu.make_async_copy(source, target, s_att).start()
+
+    wide = sz.least * HB
+
+    def moves(owner, offset, width):
+        first = pl.multiple_of(first_column(sz, owner) + offset, HB)
+        up_first = pl.multiple_of(sz.ff + first, HB)
+        cols = pl.ds(offset, width)
+        return (
+            (gate_up.at[:, pl.ds(first, width)], w_all.at[x, 0, rows, cols]),
+            (gate_up.at[:, pl.ds(up_first, width)], w_all.at[x, 1, rows, cols]),
+            (down.at[:, pl.ds(first, width)], w_all.at[x, 2, rows, cols]),
+        )
+
+    @pl.loop(1, sz.total)
+    def _(step):
+        owner = lax.rem(me + step, sz.total)
+        for source, target in moves(owner, 0, wide):
+            remote(source, target, s_mlp.at[0], r_mlp.at[x, 0], place(owner)).start()
+        if sz.extra:
+
+            @pl.when(owner < sz.extra)
+            def _():
+                for source, target in moves(owner, wide, HB):
+                    remote(source, target, s_mlp.at[1], r_mlp.at[x, 1], place(owner)).start()
+
+    for source, target in moves(me, 0, wide):
+        pltpu.make_async_copy(source, target, s_mlp.at[0]).start()
+    if sz.extra:
+
+        @pl.when(me < sz.extra)
+        def _():
+            for source, target in moves(me, wide, HB):
+                pltpu.make_async_copy(source, target, s_mlp.at[1]).start()
+
+        @pl.when(me >= sz.extra)
+        def _():
+            zeros[...] = jnp.zeros_like(zeros)
+            empty = [
+                pltpu.make_async_copy(
+                    zeros, w_all.at[section, part, :, pl.ds(wide, HB)], z_sem.at[section, part]
+                )
+                for section in range(2)
+                for part in range(3)
+            ]
+            for copy in empty:
+                copy.start()
+            for copy in empty:
+                copy.wait()
+
+    half = sz.width // 2
+    stretch = sz.width // 4
+    for section in range(2):
+        for same in (True, False):
+
+            @pl.when((x == section) == same)
+            def _():
+                count = half - sz.owned if same else half
+                arrived(att_all.at[section, pl.ds(0, count)], r_att.at[section])
+
+    arrived(att_all.at[0], s_att)
+    for section in range(2):
+        for part in range(2):
+            span = att_all.at[
+                section, pl.ds(pl.multiple_of((part * 2 + k) * stretch, 16), stretch)
+            ]
+            remote(span, span, s_fwd.at[section, part], r_fwd.at[section, part], at(x, y, 1 - k, z)).start()
+    arrived(small_all.at[pl.ds(0, sz.total - 1)], r_small)
+    arrived(small_all, s_small)
+    arrived(tok_own, r_own.at[0])
+    arrived(cot_own, r_own.at[1])
+    for section in range(2):
+        for part in range(2):
+            span = att_all.at[
+                section, pl.ds(pl.multiple_of((part * 2 + 1 - k) * stretch, 16), stretch)
+            ]
+            arrived(span, r_fwd.at[section, part])
+            arrived(span, s_fwd.at[section, part])
+    for section in range(2):
+        for same in (True, False):
+
+            @pl.when((x == section) == same)
+            def _():
+                count = sz.width - sz.owned if same else sz.width
+                arrived(w_all.at[section, :, pl.ds(0, count), pl.ds(0, wide)], r_mlp.at[section, 0])
+                if sz.extra:
+
+                    @pl.when(me < sz.extra)
+                    def _():
+                        arrived(
+                            w_all.at[section, :, pl.ds(0, count), pl.ds(0, HB)], r_mlp.at[section, 1]
+                        )
+
+    owns(False)
+    arrived(w_all.at[:, :, :, pl.ds(0, wide)], s_mlp.at[0])
+    if sz.extra:
+        arrived(w_all.at[0, :, pl.ds(0, sz.extra * sz.owned), pl.ds(0, HB)], s_mlp.at[1])
+
+
+def spread(sz, small, tokens, cotangent, qkv, out_w, gate_up, down):
+    shapes = (
+        jax.ShapeDtypeStruct((sz.total, 16, LANES), BF),
+        jax.ShapeDtypeStruct((sz.rows, sz.width), BF),
+        jax.ShapeDtypeStruct((sz.rows, sz.width), BF),
+        jax.ShapeDtypeStruct((2, sz.width, sz.atot), BF),
+        jax.ShapeDtypeStruct((2, 3, sz.width, sz.hidden), BF),
+    )
+    return pl.pallas_call(
+        functools.partial(spread_kernel, sz),
+        out_shape=shapes,
+        in_specs=[hbm()] * 7,
+        out_specs=[hbm()] * 5,
+        scratch_shapes=[
+            pltpu.VMEM((sz.width, HB), BF),
+            DMA,
+            DMA,
+            DMA((2, 2)),
+            DMA((2,)),
+            DMA,
+            DMA((2,)),
+            DMA((2, 2)),
+            DMA((2, 2)),
+            DMA((2,)),
+            DMA((2, 2)),
+            DMA((2, 3)),
+        ],
+        compiler_params=params(1),
+        name="spread_weights",
+    )(small, tokens, cotangent, qkv, out_w, gate_up, down)
+
+
+def collect_kernel(
+    sz,
+    dw0,
+    dw1,
+    da0,
+    da1,
+    small,
+    act0,
+    act1,
+    grad0,
+    grad1,
+    w_in,
+    att_in,
+    small_in,
+    act_out,
+    grad_out,
+    got,
+    summed,
+    s_core,
+    r_core,
+    s_mlp,
+    r_mlp,
+    s_att,
+    r_att,
+    s_small,
+    r_small,
+    s_out,
+    r_out,
+):
+    n = sz.ctx
+    x, y, k, z = where_am_i()
+    me = x * sz.group + (y * 2 + k) * n + z
+    place = lambda index: flat_place(index, sz.group, n)
+    greet_all(me, sz.total, place)
+    stretch = sz.width // 4
+    wide = sz.least * HB
+
+    def exchange(section, part):
+        source = (da0, da1)[section]
+        span = source.at[pl.ds(pl.multiple_of((part * 2 + 1 - k) * stretch, 16), stretch)]
+        return remote(
+            span,
+            got.at[section, part],
+            s_core.at[section, part],
+            r_core.at[section, part],
+            at(x, y, 1 - k, z),
+        )
+
+    for section in (1, 0):
+        for part in range(2):
+            exchange(section, part).start()
+
+    def outs(begin):
+        for section in range(2):
+            for slot, (source, target) in enumerate(
+                (((act0, act1)[section], act_out), ((grad0, grad1)[section], grad_out))
+            ):
+                own = jnp.logical_and(x == section, jnp.logical_and(x == y, y == k))
+
+                @pl.when(jnp.logical_not(own))
+                def _():
+                    copy = remote(
+                        source,
+                        target.at[k],
+                        s_out.at[section, slot],
+                        r_out.at[slot, k],
+                        at(section, x, y, z),
+                    )
+                    copy.start() if begin else copy.wait_send()
+
+                if begin:
+
+                    @pl.when(own)
+                    def _():
+                        pltpu.make_async_copy(source, target.at[k], r_out.at[slot, k]).start()
+
+    outs(True)
+
+    cols = pl.ds(first_column(sz, me), wide)
+    more = pl.ds(pl.multiple_of(first_column(sz, me) + wide, HB), HB)
+
+    def block(device, op):
+        inside = lax.rem(device, sz.group)
+        rows = pl.ds(pl.multiple_of(inside * sz.owned, 16), sz.owned)
+        for section, source in enumerate((dw0, dw1)):
+
+            @pl.when(device // sz.group == section)
+            def _():
+                op(source.at[:, rows, pl.ds(0, wide)], w_in.at[:, :, cols], 0)
+                if sz.extra:
+
+                    @pl.when(me < sz.extra)
+                    def _():
+                        op(source.at[:, rows, pl.ds(wide, HB)], w_in.at[:, :, more], 1)
+
+    @pl.loop(1, sz.total)
+    def _(step):
+        device = lax.rem(me + step, sz.total)
+        remote(
+            small.at[device], small_in.at[me], s_small, r_small, place(device)
+        ).start()
+        block(
+            device,
+            lambda source, target, kind: remote(
+                source, target, s_mlp.at[kind], r_mlp.at[kind], place(device)
+            ).start(),
+        )
+
+    pltpu.make_async_copy(small.at[me], small_in.at[me], s_small).start()
+    block(
+        me,
+        lambda source, target, kind: pltpu.make_async_copy(source, target, s_mlp.at[kind]).start(),
+    )
+
+    for section in (1, 0):
+        for part in range(2):
+            exchange(section, part).wait_recv()
+            source = (da0, da1)[section]
+            rows = pl.ds(pl.multiple_of((part * 2 + k) * stretch, 16), stretch)
+            summed[section, part] = (
+                source[rows].astype(F32) + got[section, part].astype(F32)
+            ).astype(BF)
+
+    mine = (2 * x + y) * n + z
+
+    def att_pair(index):
+        section, part, ctx = (index // (2 * n), lax.rem(index // n, 2), lax.rem(index, n))
+        source = summed.at[
+            section, part, pl.ds(pl.multiple_of(ctx * sz.owned, 16), sz.owned)
+        ]
+        return (source, att_in.at[mine], at(section, part, k, ctx))
+
+    @pl.loop(1, sz.group)
+    def _(step):
+        source, target, device = att_pair(lax.rem(mine + step, sz.group))
+        remote(source, target, s_att, r_att, device).start()
+
+    source, target, _ = att_pair(mine)
+    pltpu.make_async_copy(source, target, s_att).start()
+
+    for section in range(2):
+        for part in range(2):
+            exchange(section, part).wait_send()
+    outs(False)
+    for slot, target in enumerate((act_out, grad_out)):
+        for batch in range(2):
+            arrived(target.at[batch], r_out.at[slot, batch])
+    arrived(small_in.at[pl.ds(0, sz.total - 1)], r_small)
+    arrived(small_in, s_small)
+    arrived(att_in.at[pl.ds(0, sz.group - 1)], r_att)
+    arrived(att_in, s_att)
+    arrived(w_in.at[:, :, pl.ds(0, (sz.total - 1) * wide)], r_mlp.at[0])
+    arrived(w_in.at[:, :, pl.ds(0, sz.total * wide)], s_mlp.at[0])
+    if sz.extra:
+
+        @pl.when(me < sz.extra)
+        def _():
+            if sz.extra > 1:
+                arrived(w_in.at[:, :, pl.ds(0, (sz.extra - 1) * HB)], r_mlp.at[1])
+            arrived(w_in.at[:, :, pl.ds(0, sz.total * HB)], s_mlp.at[1])
+
+        @pl.when(me >= sz.extra)
+        def _():
+            arrived(w_in.at[:, :, pl.ds(0, sz.extra * HB)], r_mlp.at[1])
+
+
+def collect(sz, dw, da, small, acts, grads):
+    stretch = sz.width // 4
+    shapes = (
+        jax.ShapeDtypeStruct((3, sz.owned, sz.ff), BF),
+        jax.ShapeDtypeStruct((sz.group, sz.owned, sz.atot), BF),
+        jax.ShapeDtypeStruct((sz.total, 8, LANES), F32),
+        jax.ShapeDtypeStruct((2, sz.rows, sz.width), BF),
+        jax.ShapeDtypeStruct((2, sz.rows, sz.width), BF),
+    )
+    return pl.pallas_call(
+        functools.partial(collect_kernel, sz),
+        out_shape=shapes,
+        in_specs=[hbm()] * 2 + [vmem()] * 2 + [hbm()] * 5,
+        out_specs=[hbm()] * 5,
+        scratch_shapes=[
+            pltpu.VMEM((2, 2, stretch, sz.atot), BF),
+            pltpu.VMEM((2, 2, stretch, sz.atot), BF),
+            DMA((2, 2)),
+            DMA((2, 2)),
+            DMA((2,)),
+            DMA((2,)),
+            DMA,
+            DMA,
+            DMA,
+            DMA,
+            DMA((2, 2)),
+            DMA((2, 2)),
+        ],
+        compiler_params=params(2),
+        name="collect_gradients",
+    )(dw[0], dw[1], da[0], da[1], small, *acts, *grads)
+
+
+def half_turn(values):
+    return pltpu.roll(values, HEAD_WIDTH_SIZE // 2, 1)
+
+
+def pair_peers(x, y, k, z):
+    return (at(1 - x, y, k, z), at(x, 1 - y, k, z), at(1 - x, 1 - y, k, z))
+
+
+def pair_groups(x, y):
+    return (2 * (1 - x) + y, 2 * x + 1 - y, 2 * (1 - x) + 1 - y)
+
+
+def line_peers(n, x, y, k, z):
+    return [at(x, y, k, lax.rem(z + step, n)) for step in range(1, n)]
+
+
+def gather_pair(buffer, place, send, recv):
+    x, y, k, z = place
+    own = buffer.at[2 * x + y]
+    copies = [
+        remote(own, own, send.at[i], recv.at[i], device)
+        for i, device in enumerate(pair_peers(x, y, k, z))
+    ]
+    for copy in copies:
+        copy.start()
+    return copies
+
+
+def gathered_pair(buffer, place, copies, recv):
+    x, y, k, z = place
+    for i, group in enumerate(pair_groups(x, y)):
+        arrived(buffer.at[group], recv.at[i])
+
+
+def scatter_pair(parts, landed, place, send, recv):
+    x, y, k, z = place
+    groups = pair_groups(x, y)
+    copies = [
+        remote(parts.at[groups[i]], landed.at[i], send.at[i], recv.at[i], device)
+        for i, device in enumerate(pair_peers(x, y, k, z))
+    ]
+    for copy in copies:
+        copy.start()
+    return copies
+
+
+def attend_kernel(
+    sz,
+    section,
+    x_ref,
+    gain,
+    bias,
+    watt,
+    cosine,
+    sine,
+    qpos,
+    kpos,
+    h1_out,
+    n1_all,
+    q_out,
+    kv_all,
+    o_out,
+    lse_out,
+    w,
+    parts,
+    landed,
+    w_sem,
+    s_in,
+    r_in,
+    s_kv,
+    r_kv,
+    s_back,
+    r_back,
+):
+    n = sz.ctx
+    place = where_am_i()
+    x, y, k, z = place
+    load = pltpu.make_async_copy(watt.at[section], w, w_sem)
+    load.start()
+    greet(list(pair_peers(x, y, k, z)) + line_peers(n, x, y, k, z))
+    group = 2 * x + y
+    values = x_ref[...].astype(F32)
+    n1_all[group] = (values * row_norm(values) * gain[...]).astype(BF)
+    copies = gather_pair(n1_all, place, s_in, r_in)
+    load.wait()
+    gathered_pair(n1_all, place, copies, r_in)
+    rows = 4 * sz.rows
+    normed = n1_all[...].reshape(rows, sz.width)
+    kv = mm(normed, w[:, sz.qcols : sz.acols]) + bias[:, sz.qcols : sz.acols]
+    cos, sin = cosine[...], sine[...]
+    key = kv[:, : sz.kcols]
+    kv_all[z, :, : sz.kcols] = (key * cos + half_turn(key) * sin).astype(BF)
+    kv_all[z, :, sz.kcols :] = kv[:, sz.kcols :].astype(BF)
+    kv_copies = []
+    for step, device in enumerate(line_peers(n, x, y, k, z)):
+        own = kv_all.at[z]
+        kv_copies.append(remote(own, own, s_kv.at[step], r_kv.at[step], device))
+        kv_copies[-1].start()
+    queries = mm(normed, w[:, : sz.qcols]) + bias[:, : sz.qcols]
+    for head in range(sz.per_group):
+        cols = slice(head * HEAD_WIDTH_SIZE, (head + 1) * HEAD_WIDTH_SIZE)
+        query = queries[:, cols]
+        q_out[:, cols] = (query * cos + half_turn(query) * sin).astype(BF)
+    for step in range(n - 1):
+        arrived(kv_all.at[lax.rem(z + n - 1 - step, n)], r_kv.at[step])
+    keys = kv_all[:, :, : sz.kcols].reshape(n * rows, sz.kcols)
+    vals = kv_all[:, :, sz.kcols :].reshape(n * rows, sz.kcols)
+    allowed = kpos[...] <= qpos[...]
+    scale = 1.0 / math.sqrt(HEAD_WIDTH_SIZE)
+    for head in range(sz.per_group):
+        cols = slice(head * HEAD_WIDTH_SIZE, (head + 1) * HEAD_WIDTH_SIZE)
+        scores = jnp.where(allowed, mm(q_out[:, cols], keys, NT) * scale, -1e30)
+        highest = jnp.max(scores, axis=-1, keepdims=True)
+        weights = jnp.exp(scores - highest)
+        total = jnp.sum(weights, axis=-1, keepdims=True)
+        o_out[:, cols] = mm(weights.astype(BF), vals) / total
+        lse_out[head] = jnp.broadcast_to(highest + jnp.log(total), (rows, LANES))
+    partial = mm(o_out[...].astype(BF), w[:, sz.acols :], NT)
+    parts[...] = partial.astype(BF).reshape(4, sz.rows, sz.width)
+    back = scatter_pair(parts, landed, place, s_back, r_back)
+    for copy in copies + kv_copies:
+        copy.wait_send()
+    out = values + parts[group].astype(F32)
+    for i in range(3):
+        back[i].wait_recv()
+        out = out + landed[i].astype(F32)
+    h1_out[...] = out
+    for copy in back:
+        copy.wait_send()
+
+
+def attend(sz, section, x_own, gain, bias, watt, tables, qpos, kpos):
+    n, rows = sz.ctx, 4 * sz.rows
+    shapes = (
+        jax.ShapeDtypeStruct((sz.rows, sz.width), F32),
+        jax.ShapeDtypeStruct((4, sz.rows, sz.width), BF),
+        jax.ShapeDtypeStruct((rows, sz.qcols), BF),
+        jax.ShapeDtypeStruct((n, rows, 2 * sz.kcols), BF),
+        jax.ShapeDtypeStruct((rows, sz.qcols), F32),
+        jax.ShapeDtypeStruct((sz.per_group, rows, LANES), F32),
+    )
+    return pl.pallas_call(
+        functools.partial(attend_kernel, sz, section),
+        out_shape=shapes,
+        in_specs=[vmem()] * 3 + [hbm()] + [vmem()] * 4,
+        out_specs=[vmem()] * 6,
+        scratch_shapes=[
+            pltpu.VMEM((sz.width, sz.atot), BF),
+            pltpu.VMEM((4, sz.rows, sz.width), BF),
+            pltpu.VMEM((3, sz.rows, sz.width), BF),
+            DMA,
+            DMA((3,)),
+            DMA((3,)),
+            DMA((n,)),
+            DMA((n,)),
+            DMA((3,)),
+            DMA((3,)),
+        ],
+        compiler_params=params(3 + section),
+        name="attend_forward",
+    )(x_own, gain, bias, watt, *tables, qpos, kpos)
+
+
+def attend_back_kernel(
+    sz,
+    section,
+    dh1,
+    x_ref,
+    gain,
+    watt,
+    cosine,
+    sine,
+    qpos,
+    kpos,
+    n1_all,
+    q_in,
+    kv_all,
+    o_in,
+    lse_in,
+    dx_out,
+    dw_out,
+    gain_grad,
+    bias_grad,
+    w,
+    dh_all,
+    dkv,
+    dkv_in,
+    da,
+    parts,
+    landed,
+    w_sem,
+    s_in,
+    r_in,
+    s_kv,
+    r_kv,
+    s_back,
+    r_back,
+):
+    n = sz.ctx
+    place = where_am_i()
+    x, y, k, z = place
+    load = pltpu.make_async_copy(watt.at[section], w, w_sem)
+    load.start()
+    greet(list(pair_peers(x, y, k, z)) + line_peers(n, x, y, k, z))
+    group = 2 * x + y
+    rows = 4 * sz.rows
+    dh_all[group] = dh1[...].astype(BF)
+    copies = gather_pair(dh_all, place, s_in, r_in)
+    load.wait()
+    gathered_pair(dh_all, place, copies, r_in)
+    dh = dh_all[...].reshape(rows, sz.width)
+    dout = mm(dh, w[:, sz.acols :]).astype(BF)
+    keys = kv_all[:, :, : sz.kcols].reshape(n * rows, sz.kcols)
+    vals = kv_all[:, :, sz.kcols :].reshape(n * rows, sz.kcols)
+    allowed = kpos[...] <= qpos[...]
+    scale = 1.0 / math.sqrt(HEAD_WIDTH_SIZE)
+    cos, sin = cosine[...], sine[...]
+    dkeys, dvals = None, None
+    for head in range(sz.per_group):
+        cols = slice(head * HEAD_WIDTH_SIZE, (head + 1) * HEAD_WIDTH_SIZE)
+        query, grad = q_in[:, cols], dout[:, cols]
+        delta = jnp.sum(grad.astype(F32) * o_in[:, cols], axis=-1, keepdims=True)
+        scores = mm(query, keys, NT) * scale
+        probs = jnp.where(allowed, jnp.exp(scores - lse_in[head][:, :1]), 0.0)
+        dscores = (probs * (mm(grad, vals, NT) - delta)).astype(BF)
+        dquery = (mm(dscores, keys) * scale).astype(BF).astype(F32)
+        da[:, cols] = (dquery * cos - half_turn(dquery) * sin).astype(BF)
+        one_key = mm(dscores, query, TN)
+        one_val = mm(probs.astype(BF), grad, TN)
+        dkeys = one_key if dkeys is None else dkeys + one_key
+        dvals = one_val if dvals is None else dvals + one_val
+    dkv[:, :, : sz.kcols] = (dkeys * scale).astype(BF).reshape(n, rows, sz.kcols)
+    dkv[:, :, sz.kcols :] = dvals.astype(BF).reshape(n, rows, sz.kcols)
+    kv_copies = []
+    for step, device in enumerate(line_peers(n, x, y, k, z)):
+        kv_copies.append(
+            remote(
+                dkv.at[lax.rem(z + 1 + step, n)],
+                dkv_in.at[step],
+                s_kv.at[step],
+                r_kv.at[step],
+                device,
+            )
+        )
+        kv_copies[-1].start()
+    dw_out[:, sz.acols :] = mm(dh, o_in[...].astype(BF), TN).astype(BF)
+    total = dkv[z].astype(F32)
+    for step in range(n - 1):
+        kv_copies[step].wait_recv()
+        total = total + dkv_in[step].astype(F32)
+    dkey = total[:, : sz.kcols]
+    da[:, sz.qcols : sz.qcols + sz.kcols] = (dkey * cos - half_turn(dkey) * sin).astype(BF)
+    da[:, sz.qcols + sz.kcols :] = total[:, sz.kcols :].astype(BF)
+    parts[...] = mm(da[...], w[:, : sz.acols], NT).astype(BF).reshape(4, sz.rows, sz.width)
+    back = scatter_pair(parts, landed, place, s_back, r_back)
+    dw_out[:, : sz.acols] = mm(n1_all[...].reshape(rows, sz.width), da[...], TN).astype(BF)
+    bias_grad[...] = jnp.sum(da[...].astype(F32), axis=0, keepdims=True)
+    for copy in copies + kv_copies:
+        copy.wait_send()
+    dn1 = parts[group].astype(F32)
+    for i in range(3):
+        back[i].wait_recv()
+        dn1 = dn1 + landed[i].astype(F32)
+    values = x_ref[...].astype(F32)
+    inverse = row_norm(values)
+    weighted = dn1 * gain[...]
+    inner = jnp.mean(weighted * values, axis=-1, keepdims=True)
+    dx = dh1[...] + inverse * weighted - values * (inverse * inverse * inverse) * inner
+    dx_out[...] = dx.astype(BF)
+    gain_grad[...] = jnp.sum(dn1 * values * inverse, axis=0, keepdims=True)
+    for copy in back:
+        copy.wait_send()
+
+
+def attend_back(sz, section, dh1, x_own, gain, watt, tables, qpos, kpos, kept):
+    n, rows = sz.ctx, 4 * sz.rows
+    shapes = (
+        jax.ShapeDtypeStruct((sz.rows, sz.width), BF),
+        jax.ShapeDtypeStruct((sz.width, sz.atot), BF),
+        jax.ShapeDtypeStruct((1, sz.width), F32),
+        jax.ShapeDtypeStruct((1, sz.acols), F32),
+    )
+    return pl.pallas_call(
+        functools.partial(attend_back_kernel, sz, section),
+        out_shape=shapes,
+        in_specs=[vmem()] * 3 + [hbm()] + [vmem()] * 9,
+        out_specs=[vmem()] * 4,
+        scratch_shapes=[
+            pltpu.VMEM((sz.width, sz.atot), BF),
+            pltpu.VMEM((4, sz.rows, sz.width), BF),
+            pltpu.VMEM((n, rows, 2 * sz.kcols), BF),
+            pltpu.VMEM((n, rows, 2 * sz.kcols), BF),
+            pltpu.VMEM((rows, sz.acols), BF),
+            pltpu.VMEM((4, sz.rows, sz.width), BF),
+            pltpu.VMEM((3, sz.rows, sz.width), BF),
+            DMA,
+            DMA((3,)),
+            DMA((3,)),
+            DMA((n,)),
+            DMA((n,)),
+            DMA((3,)),
+            DMA((3,)),
+        ],
+        compiler_params=params(5 + section),
+        name="attend_backward",
+    )(dh1, x_own, gain, watt, *tables, qpos, kpos, *kept)
+
+
+def tree_peers(n, x, y, k, z):
+    return [at(1 - x, y, k, z), at(x, 1 - y, k, z), at(x, y, 1 - k, z)] + line_peers(n, x, y, k, z)
+
+
+class Gather:
+    SEMS = 12
+
+    @staticmethod
+    def scratch(n):
+        return [DMA((n,))] * 10 + [DMA((4, n))] * 2
+
+    def __init__(self, n, rows, buffer, place, sems):
+        self.n, self.half, self.buffer = n, rows // 2, buffer
+        self.x, self.y, self.k, self.z = place
+        x, y = self.x, self.y
+        self.groups = (2 * x + y, 2 * x + 1 - y, 2 * (1 - x) + y, 2 * (1 - x) + 1 - y)
+        (
+            self.sz,
+            self.rz,
+            self.sy,
+            self.ry,
+            self.sx,
+            self.rx,
+            self.syd,
+            self.ryd,
+            self.sxd,
+            self.rxd,
+            self.sc,
+            self.rc,
+        ) = sems
+
+    def src(self, step):
+        return lax.rem(self.z + self.n - step, self.n)
+
+    def line(self, step):
+        own = self.buffer.at[self.k, self.groups[0], self.z]
+        device = at(self.x, self.y, self.k, lax.rem(self.z + step, self.n))
+        return remote(own, own, self.sz.at[step], self.rz.at[step], device)
+
+    def to_y(self, step):
+        part = self.buffer.at[self.k, self.groups[0], self.src(step)]
+        device = at(self.x, 1 - self.y, self.k, self.z)
+        return remote(part, part, self.sy.at[step], self.ry.at[step], device)
+
+    def to_x(self, step):
+        part = self.buffer.at[self.k, self.groups[0], self.src(step)]
+        device = at(1 - self.x, self.y, self.k, self.z)
+        return remote(part, part, self.sx.at[step], self.rx.at[step], device)
+
+    def on_x(self, step):
+        part = self.buffer.at[self.k, self.groups[1], self.src(step), pl.ds(0, self.half)]
+        device = at(1 - self.x, self.y, self.k, self.z)
+        return remote(part, part, self.sxd.at[step], self.rxd.at[step], device)
+
+    def on_y(self, step):
+        part = self.buffer.at[self.k, self.groups[2], self.src(step), pl.ds(self.half, self.half)]
+        device = at(self.x, 1 - self.y, self.k, self.z)
+        return remote(part, part, self.syd.at[step], self.ryd.at[step], device)
+
+    def core(self, which, step):
+        part = self.buffer.at[self.k, self.groups[which], self.src(step)]
+        device = at(self.x, self.y, 1 - self.k, self.z)
+        return remote(part, part, self.sc.at[which, step], self.rc.at[which, step], device)
+
+    def begin(self):
+        for step in range(1, self.n):
+            self.line(step).start()
+        self.spread(0)
+
+    def spread(self, step):
+        if step:
+            arrived(self.buffer.at[self.k, self.groups[0], self.src(step)], self.rz.at[step])
+        self.to_y(step).start()
+        self.to_x(step).start()
+        self.core(0, step).start()
+
+    def second(self, step):
+        arrived(self.buffer.at[self.k, self.groups[1], self.src(step)], self.ry.at[step])
+        self.on_x(step).start()
+        self.core(1, step).start()
+        arrived(self.buffer.at[self.k, self.groups[2], self.src(step)], self.rx.at[step])
+        self.on_y(step).start()
+        self.core(2, step).start()
+
+    def third(self, step):
+        part = self.buffer.at[self.k, self.groups[3], self.src(step)]
+        arrived(part.at[pl.ds(0, self.half)], self.rxd.at[step])
+        arrived(part.at[pl.ds(self.half, self.half)], self.ryd.at[step])
+        self.core(3, step).start()
+
+    def other(self, which):
+        for step in range(self.n):
+            part = self.buffer.at[1 - self.k, self.groups[which], self.src(step)]
+            arrived(part, self.rc.at[which, step])
+
+    def finish(self):
+        for step in range(self.n):
+            if step:
+                self.line(step).wait_send()
+            self.to_y(step).wait_send()
+            self.to_x(step).wait_send()
+            self.on_x(step).wait_send()
+            self.on_y(step).wait_send()
+            for which in range(4):
+                self.core(which, step).wait_send()
+
+    def run(self, column):
+        k, groups, steps = self.k, self.groups, range(self.n)
+        for step in range(1, self.n):
+            self.spread(step)
+        column(k, 0)
+        for step in steps:
+            self.second(step)
+        self.other(0)
+        column(1 - k, 0)
+        column(k, 1)
+        column(k, 2)
+        for step in steps:
+            self.third(step)
+        self.other(1)
+        column(1 - k, 1)
+        self.other(2)
+        column(1 - k, 2)
+        column(k, 3)
+        self.other(3)
+        column(1 - k, 3)
+
+
+class Scatter:
+    @staticmethod
+    def scratch(n, rows, width):
+        return [
+            pltpu.VMEM((2, 4, n, rows, width), BF),
+            pltpu.VMEM((4, n, rows, width), BF),
+            pltpu.VMEM((2, n, rows // 2, width), BF),
+            pltpu.VMEM((2, n, rows, width), BF),
+            pltpu.VMEM((n, rows, width), BF),
+            DMA((4,)),
+            DMA((4,)),
+            DMA((2, n)),
+            DMA((2, n)),
+            DMA((2, 2, n)),
+            DMA((2, 2, n)),
+            DMA((n,)),
+            DMA((n,)),
+        ]
+
+    def __init__(self, n, rows, place, refs):
+        self.n, self.rows, self.half = n, rows, rows // 2
+        self.x, self.y, self.k, self.z = place
+        x, y = self.x, self.y
+        self.groups = (2 * x + y, 2 * x + 1 - y, 2 * (1 - x) + y, 2 * (1 - x) + 1 - y)
+        (
+            self.parts,
+            self.from_core,
+            self.from_diag,
+            self.from_near,
+            self.from_line,
+            self.s_core,
+            self.r_core,
+            self.s_diag,
+            self.r_diag,
+            self.s_near,
+            self.r_near,
+            self.s_line,
+            self.r_line,
+        ) = refs
+        self.near = (at(x, 1 - y, self.k, self.z), at(1 - x, y, self.k, self.z))
+
+    def slot(self, step):
+        return lax.rem(self.z + step, self.n)
+
+    def order(self):
+        return list(range(1, self.n)) + [0]
+
+    def core(self, which):
+        return remote(
+            self.parts.at[1 - self.k, self.groups[which]],
+            self.from_core.at[which],
+            self.s_core.at[which],
+            self.r_core.at[which],
+            at(self.x, self.y, 1 - self.k, self.z),
+        )
+
+    def diag(self, direction, step):
+        rows = pl.ds(self.half if direction == 0 else 0, self.half)
+        return remote(
+            self.parts.at[self.k, self.groups[3], self.slot(step), rows],
+            self.from_diag.at[direction, step],
+            self.s_diag.at[direction, step],
+            self.r_diag.at[direction, step],
+            self.near[direction],
+        )
+
+    def close(self, direction, part, step):
+        rows = pl.ds(part * self.half, self.half)
+        return remote(
+            self.parts.at[self.k, self.groups[1 + direction], self.slot(step), rows],
+            self.from_near.at[direction, step, rows],
+            self.s_near.at[direction, part, step],
+            self.r_near.at[direction, part, step],
+            self.near[direction],
+        )
+
+    def line(self, step):
+        return remote(
+            self.parts.at[self.k, self.groups[0], self.slot(step)],
+            self.from_line.at[step],
+            self.s_line.at[step],
+            self.r_line.at[step],
+            at(self.x, self.y, self.k, self.slot(step)),
+        )
+
+    def add_core(self, which):
+        self.core(which).wait_recv()
+        group = self.groups[which]
+        self.parts[self.k, group] = (
+            self.parts[self.k, group].astype(F32) + self.from_core[which].astype(F32)
+        ).astype(BF)
+
+    def run(self, fill):
+        fill = list(fill) + [lambda: None] * 4
+        self.add_core(3)
+        for step in self.order():
+            self.diag(1, step).start()
+            self.diag(0, step).start()
+        for direction, part in ((0, 1), (1, 0)):
+            self.add_core(1 + direction)
+            for step in self.order():
+                self.close(direction, part, step).start()
+        self.add_core(0)
+        fill[0]()
+        for step in self.order():
+            slot = self.slot(step)
+            for direction, part in ((0, 0), (1, 1)):
+                came = 1 - direction
+                self.diag(came, step).wait_recv()
+                rows = pl.ds(part * self.half, self.half)
+                group = self.groups[1 + direction]
+                self.parts[self.k, group, slot, rows] = (
+                    self.parts[self.k, group, slot, rows].astype(F32)
+                    + self.from_diag[came, step].astype(F32)
+                ).astype(BF)
+                self.close(direction, part, step).start()
+        fill[1]()
+        group = self.groups[0]
+        result = None
+        for step in self.order():
+            slot = self.slot(step)
+            for direction in range(2):
+                for part in range(2):
+                    self.close(direction, part, step).wait_recv()
+            total = (
+                self.parts[self.k, group, slot].astype(F32)
+                + self.from_near[0, step].astype(F32)
+                + self.from_near[1, step].astype(F32)
+            )
+            if step:
+                self.parts[self.k, group, slot] = total.astype(BF)
+                self.line(step).start()
+            else:
+                result = total
+        fill[2]()
+        for step in range(1, self.n):
+            self.line(step).wait_recv()
+            result = result + self.from_line[step].astype(F32)
+        return result
+
+    def finish(self):
+        for which in range(4):
+            self.core(which).wait_send()
+        for step in range(self.n):
+            for direction in range(2):
+                self.diag(direction, step).wait_send()
+                for part in range(2):
+                    self.close(direction, part, step).wait_send()
+            if step:
+                self.line(step).wait_send()
+
+
+def feed_kernel(sz, section, h1, gain, w_all, act_out, n2_all, gate_out, up_out, hm_out, w, w_sem, *refs):
+    n = sz.ctx
+    place = where_am_i()
+    x, y, k, z = place
+    load = pltpu.make_async_copy(w_all.at[section], w, w_sem)
+    load.start()
+    greet(tree_peers(n, x, y, k, z))
+    gather = Gather(n, sz.rows, n2_all, place, refs[:12])
+    scatter = Scatter(n, sz.rows, place, refs[12:])
+    values = h1[...]
+    n2_all[k, gather.groups[0], z] = (values * row_norm(values) * gain[...]).astype(BF)
+    gather.begin()
+    load.wait()
+    rows = n * sz.rows
+
+    def column(core, which):
+        group = gather.groups[which]
+        normed = n2_all[core, group].reshape(rows, sz.width)
+        gate = mm(normed, w[0])
+        up = mm(normed, w[1])
+        hidden = (gate * jax.nn.sigmoid(gate) * up).astype(BF)
+        gate_out[core, group] = gate.astype(BF)
+        up_out[core, group] = up.astype(BF)
+        hm_out[core, group] = hidden
+        scatter.parts[core, group] = (
+            mm(hidden, w[2], NT).astype(BF).reshape(n, sz.rows, sz.width)
+        )
+
+    def column_and_send(core, which):
+        column(core, which)
+        if core is not k:
+            scatter.core(which).start()
+
+    gather.run(column_and_send)
+    result = scatter.run(())
+    act_out[...] = (values + result).astype(BF)
+    gather.finish()
+    scatter.finish()
+
+
+def feed(sz, section, h1, gain, w_all):
+    n = sz.ctx
+    kept = jax.ShapeDtypeStruct((2, 4, n * sz.rows, sz.hidden), BF)
+    shapes = (
+        jax.ShapeDtypeStruct((sz.rows, sz.width), BF),
+        jax.ShapeDtypeStruct((2, 4, n, sz.rows, sz.width), BF),
+        kept,
+        kept,
+        kept,
+    )
+    return pl.pallas_call(
+        functools.partial(feed_kernel, sz, section),
+        out_shape=shapes,
+        in_specs=[vmem()] * 2 + [hbm()],
+        out_specs=[vmem()] * 5,
+        scratch_shapes=[pltpu.VMEM((3, sz.width, sz.hidden), BF), DMA]
+        + Gather.scratch(n)
+        + Scatter.scratch(n, sz.rows, sz.width),
+        compiler_params=params(7 + section),
+        name="feed_forward",
+    )(h1, gain, w_all)
+
+
+def feed_back_kernel(
+    sz,
+    section,
+    dy,
+    h1,
+    gain,
+    w_all,
+    n2_all,
+    gate_in,
+    up_in,
+    hm_in,
+    dh1_out,
+    dw_out,
+    gain_grad,
+    w,
+    dy_all,
+    dgate_all,
+    dup_all,
+    w_sem,
+    *refs,
+):
+    n = sz.ctx
+    place = where_am_i()
+    x, y, k, z = place
+    load = pltpu.make_async_copy(w_all.at[section], w, w_sem)
+    load.start()
+    greet(tree_peers(n, x, y, k, z))
+    gather = Gather(n, sz.rows, dy_all, place, refs[:12])
+    scatter = Scatter(n, sz.rows, place, refs[12:])
+    dy_all[k, gather.groups[0], z] = dy[...]
+    gather.begin()
+    load.wait()
+    rows = n * sz.rows
+
+    def column(core, which):
+        group = gather.groups[which]
+        dhidden = mm(dy_all[core, group].reshape(rows, sz.width), w[2])
+        gate = gate_in[core, group].astype(F32)
+        up = up_in[core, group].astype(F32)
+        sigmoid = jax.nn.sigmoid(gate)
+        dgate = (dhidden * up * sigmoid * (1.0 + gate * (1.0 - sigmoid))).astype(BF)
+        dup = (dhidden * gate * sigmoid).astype(BF)
+        dgate_all[core, group] = dgate
+        dup_all[core, group] = dup
+        partial = mm(dgate, w[0], NT) + mm(dup, w[1], NT)
+        scatter.parts[core, group] = partial.astype(BF).reshape(n, sz.rows, sz.width)
+        if core is not k:
+            scatter.core(which).start()
+
+    gather.run(column)
+    total = 8 * rows
+    tile = 256 if sz.width % 256 == 0 else 128
+
+    def weight_grad(slot, left, right):
+        def work():
+            grads = right[...].reshape(total, sz.hidden)
+
+            @pl.loop(0, sz.width // tile)
+            def _(step):
+                cols = pl.ds(pl.multiple_of(step * tile, tile), tile)
+                side = left[:, :, :, :, cols].reshape(total, tile)
+                dw_out[slot, cols] = mm(side, grads, TN).astype(BF)
+
+        return work
+
+    dn2 = scatter.run(
+        (
+            weight_grad(0, n2_all, dgate_all),
+            weight_grad(1, n2_all, dup_all),
+            weight_grad(2, dy_all, hm_in),
+        )
+    )
+    values = h1[...]
+    inverse = row_norm(values)
+    weighted = dn2 * gain[...]
+    inner = jnp.mean(weighted * values, axis=-1, keepdims=True)
+    dh1_out[...] = (
+        dy[...].astype(F32) + inverse * weighted - values * (inverse * inverse * inverse) * inner
+    )
+    gain_grad[...] = jnp.sum(dn2 * values * inverse, axis=0, keepdims=True)
+    gather.finish()
+    scatter.finish()
+
+
+def feed_back(sz, section, dy, h1, gain, w_all, kept):
+    n = sz.ctx
+    shapes = (
+        jax.ShapeDtypeStruct((sz.rows, sz.width), F32),
+        jax.ShapeDtypeStruct((3, sz.width, sz.hidden), BF),
+        jax.ShapeDtypeStruct((1, sz.width), F32),
+    )
+    inner = pltpu.VMEM((2, 4, n * sz.rows, sz.hidden), BF)
+    return pl.pallas_call(
+        functools.partial(feed_back_kernel, sz, section),
+        out_shape=shapes,
+        in_specs=[vmem()] * 3 + [hbm()] + [vmem()] * 4,
+        out_specs=[vmem()] * 3,
+        scratch_shapes=[
+            pltpu.VMEM((3, sz.width, sz.hidden), BF),
+            pltpu.VMEM((2, 4, n, sz.rows, sz.width), BF),
+            inner,
+            inner,
+            DMA,
+        ]
+        + Gather.scratch(n)
+        + Scatter.scratch(n, sz.rows, sz.width),
+        compiler_params=params(9 + section),
+        name="feed_backward",
+    )(dy, h1, gain, w_all, *kept)
+
+
+def local_columns(
+    sz,
+    tokens,
+    positions,
+    norm1_gain,
+    qkv_bias,
+    qkv_weight,
+    out_weight,
+    norm2_gain,
+    gate_up_weight,
+    down_weight,
+    cotangent,
+):
+    n, group = sz.ctx, sz.group
+    x, y, k, z = where_am_i()
+    mine = 2 * x + y
+    bias_owned = qkv_bias.shape[1]
+
+    def line(values):
+        return jnp.pad(values, ((0, 0), (0, LANES - values.shape[1])))
+
+    small = jnp.concatenate(
+        [line(norm1_gain), line(norm2_gain), line(qkv_bias), jnp.zeros((13, LANES), BF)], axis=0
+    )
+    small_all, tok_own, cot_own, att_all, w_all = spread(
+        sz, small, tokens, cotangent, qkv_weight[0], out_weight[0], gate_up_weight[0], down_weight[0]
+    )
+    per_section = small_all.reshape(2, group, 16, LANES).astype(F32)
+    gain1 = per_section[:, :, 0, : sz.owned].reshape(2, 1, sz.width)
+    gain2 = per_section[:, :, 1, : sz.owned].reshape(2, 1, sz.width)
+    bias = per_section[:, :, 2, :bias_owned].reshape(2, 1, group * bias_owned)
+    query_columns = QUERY_HEADS * HEAD_WIDTH_SIZE
+    key_columns = KEY_VALUE_HEADS * HEAD_WIDTH_SIZE
+    kv = mine // (4 // KEY_VALUE_HEADS)
+    starts = (
+        (mine * sz.qcols, sz.qcols),
+        (query_columns + kv * sz.kcols, sz.kcols),
+        (query_columns + key_columns + kv * sz.kcols, sz.kcols),
+    )
+    own_bias = jnp.concatenate(
+        [lax.dynamic_slice_in_dim(bias, start, size, 2) for start, size in starts], axis=2
+    )
+    ordered = lax.dynamic_index_in_dim(positions, k, 0, keepdims=False)
+    ordered = ordered.reshape(4, n, sz.rows).transpose(1, 0, 2)
+    own_pos = lax.dynamic_index_in_dim(ordered, z, 0, keepdims=False).reshape(4 * sz.rows)
+    kpos = ordered.reshape(1, sz.seq)
+    qpos = own_pos[:, None]
+    cosine, sine = rope_tables(own_pos, HEAD_WIDTH_SIZE)
+    half = HEAD_WIDTH_SIZE // 2
+    sign = jnp.where(jnp.arange(HEAD_WIDTH_SIZE) < half, -1.0, 1.0)
+    tables = (cosine[:, 0], sine[:, 0] * sign)
+
+    inputs, acts, kept_att, kept_feed, middles = [tok_own], [], [], [], []
+    for section in range(2):
+        h1, *kept = attend(
+            sz, section, inputs[section], gain1[section], own_bias[section], att_all, tables, qpos, kpos
+        )
+        kept_att.append(kept)
+        middles.append(h1)
+        act, *kept = feed(sz, section, h1, gain2[section], w_all)
+        kept_feed.append(kept)
+        acts.append(act)
+        inputs.append(act)
+    grads, dws, das, smalls = [None, None], [None, None], [None, None], [None, None]
+    dy = cot_own
+    for section in (1, 0):
+        dh1, dws[section], gain2_grad = feed_back(
+            sz, section, dy, middles[section], gain2[section], w_all, kept_feed[section]
+        )
+        dy, das[section], gain1_grad, bias_grad = attend_back(
+            sz,
+            section,
+            dh1,
+            inputs[section],
+            gain1[section],
+            att_all,
+            tables,
+            qpos,
+            kpos,
+            kept_att[section],
+        )
+        grads[section] = dy
+        whole_bias = jnp.zeros((1, query_columns + 2 * key_columns), F32)
+        offset = 0
+        for start, size in starts:
+            whole_bias = lax.dynamic_update_slice(
+                whole_bias, bias_grad[:, offset : offset + size], (0, start)
+            )
+            offset += size
+        split = query_columns + key_columns
+        rows = [gain1_grad, gain2_grad, whole_bias[:, :split], whole_bias[:, split:]]
+        rows = [line(row.reshape(group, -1))[:, None] for row in rows]
+        smalls[section] = jnp.concatenate(rows + [jnp.zeros((group, 4, LANES), F32)], axis=1)
+    small_out = jnp.concatenate(smalls, axis=0)
+    w_in, att_in, small_in, act_out, grad_out = collect(sz, dws, das, small_out, acts, grads)
+    small_sum = jnp.sum(small_in, axis=0)
+    gate_up_grad = jnp.concatenate([w_in[0], w_in[1]], axis=1).astype(F32)[None]
+    down_grad = w_in[2].astype(F32)[None]
+    att_sum = jnp.sum(att_in.astype(F32).reshape(4, n, sz.owned, sz.atot), axis=1)
+    q_grad = att_sum[:, :, : sz.qcols].transpose(1, 0, 2).reshape(sz.owned, query_columns)
+    kv_grad = jnp.sum(
+        att_sum[:, :, sz.qcols : sz.acols].reshape(
+            KEY_VALUE_HEADS, 4 // KEY_VALUE_HEADS, sz.owned, 2, sz.kcols
+        ),
+        axis=1,
+    )
+    kv_grad = kv_grad.transpose(1, 2, 0, 3).reshape(sz.owned, 2 * key_columns)
+    qkv_grad = jnp.concatenate([q_grad, kv_grad], axis=1)[None]
+    out_grad = att_sum[:, :, sz.acols :].transpose(1, 0, 2).reshape(1, sz.owned, query_columns)
+    return (
+        act_out[None],
+        grad_out[None],
+        small_sum[0:1, : sz.owned],
+        small_sum[2:3, : (query_columns + key_columns) // group],
+        small_sum[3:4, : key_columns // group],
+        qkv_grad,
+        out_grad,
+        small_sum[1:2, : sz.owned],
+        gate_up_grad,
+        down_grad,
+    )
+
+
 def solution(mesh):
     placed = (
         P(None, ("head", "ctx"), None),
@@ -491,21 +1921,24 @@
         P("section", ("head", "ctx"), None),
         P(None, ("head", "ctx"), None),
     )
-    return jax.shard_map(
-        local,
-        mesh=mesh,
-        in_specs=placed,
-        out_specs=(
-            P("section", None, ("head", "ctx"), None),
-            P("section", None, ("head", "ctx"), None),
-            P("section", ("head", "ctx")),
-            P("section", ("head", "ctx")),
-            P("section", ("head", "ctx")),
-            P("section", ("head", "ctx"), None),
-            P("section", ("head", "ctx"), None),
-            P("section", ("head", "ctx")),
-            P("section", ("head", "ctx"), None),
-            P("section", ("head", "ctx"), None),
-        ),
-        check_vma=False,
-    )
+    returned = (
+        P("section", None, ("head", "ctx"), None),
+        P("section", None, ("head", "ctx"), None),
+        P("section", ("head", "ctx")),
+        P("section", ("head", "ctx")),
+        P("section", ("head", "ctx")),
+        P("section", ("head", "ctx"), None),
+        P("section", ("head", "ctx"), None),
+        P("section", ("head", "ctx")),
+        P("section", ("head", "ctx"), None),
+        P("section", ("head", "ctx"), None),
+    )
+
+    def program(*arrays):
+        sizes = Sizes(mesh, arrays[0], arrays[4], arrays[7], arrays[8])
+        body = functools.partial(local_columns, sizes) if sizes.fits() else local
+        return jax.shard_map(
+            body, mesh=mesh, in_specs=placed, out_specs=returned, check_vma=False
+        )(*arrays)
+
+    return program

time: 3070 us -> 996 us (0.32)
  the two profiles are of different devices: /device:TPU:14 before, /device:TPU:30 now
where the time goes in v1:
time: 996 us; the launch traced here: 986 us
  Pallas kernels  957 us (96%)
  other arithmetic  15.2 us (2%)
  local copies, waits for them, and re-layouts  13.3 us (1%)
    pallas_call x1, Pallas kernels, collect(): pl.pallas_call(functools.partial(collect_kernel, sz), out_shape=shapes, i...  242 us
    pallas_call x1, Pallas kernels, spread(): pl.pallas_call(functools.partial(spread_kernel, sz), out_shape=shapes, in...  185 us
    pallas_call x2, Pallas kernels, feed_back(): pl.pallas_call(functools.partial(feed_back_kernel, sz, section), out_shap...  179 us
    pallas_call x2, Pallas kernels, feed(): pl.pallas_call(functools.partial(feed_kernel, sz, section), out_shape=sha...  163 us
    pallas_call x2, Pallas kernels, attend(): pl.pallas_call(functools.partial(attend_kernel, sz, section), out_shape=s...  93.7 us
    pallas_call x2, Pallas kernels, attend_back(): pl.pallas_call(functools.partial(attend_back_kernel, sz, section), out_sh...  93.7 us

profile of v1, /device:TPU:30, one launch (start us, length us, event | category | flops | bytes accessed | tf_op | source)
XLA Modules:
  0.0 986.5 jit_solution(13164233632965541563)
XLA Ops:
  0.7 0.1 pad.58.clone
  0.8 1.4 fusion.6.small
  2.1 185.0 %spread_weights.1 = (bf16[32,16,128]{2,1,0:T(8,128)(2,1)}, bf16[64,1536]{1,0:T(8,128)(2,1)}, bf16[64,1536]{1,0:T(8,128)(2,1)}, bf16[2,1536,1024]{2,1,0:T(8,128)(2,1)}, bf16[2,3,1536,384]{3,2,1,0:T(8,128)(2,1)}) custom-call(bf16[16,128]{1,0:T(8,128)(2,1)} %fusion.6.small, bf16[2,64,1536]{2,1,0:T(8,128)(2,1)} %tokens.1, bf16[2,64,1536]{2,1,0:T(8,128)(2,1)} %cotangent.1, ...), custom_call_target="tpu_custom_call" | custom-call | tf_op jit(solution)/shard_map/spread_weights/pallas_call | solution.py:803
  187.1 0.9 bitcast_convert_fusion
  188.2 0.6 slice_bitcast_fusion.2
  188.8 0.1 reshape.132
  188.9 0.1 convert_element_type.55
  189.0 0.1 broadcast_multiply_fusion
  189.2 1.2 sine_multiply_fusion
  190.4 0.8 reshape.152.qpos
  191.2 0.7 reshape.134.kpos
  191.9 0.7 squeeze.45.gain
  192.6 46.2 %attend_forward.2 = (f32[64,1536]{1,0:T(8,128)}, bf16[4,64,1536]{2,1,0:T(8,128)(2,1)}, bf16[256,384]{1,0:T(8,128)(2,1)}, bf16[4,256,256]{2,1,0:T(8,128)(2,1)}, f...) custom-call(bf16[64,1536]{1,0:T(8,128)(2,1)} %get-tuple-element.57.x_ref, f32[1,1536]{1,0:T(1,128)} %squeeze.45.gain, ...), custom_call_target="tpu_custom_call" | custom-call | tf_op jit(solution)/shard_map/attend_forward/pallas_call | solution.py:1167
  238.8 0.7 squeeze.47.gain
  239.5 81.6 %feed_forward.2 = (bf16[64,1536]{1,0:T(8,128)(2,1)}, bf16[2,4,4,64,1536]{4,3,2,1,0:T(8,128)(2,1)}, bf16[2,4,256,384]{3,2,1,0:T(8,128)(2,1)}, bf16[2,4,256,384]{3,2,1,0:T(8,128)(2,1)}, bf16[2,4,256,384]{3,2,1,0:T(8,128)(2,1)}) custom-call(f32[64,1536]{1,0:T(8,128)} %get-tuple-element.60.h1, f32[1,1536]{1,0:T(1,128)} %squeeze.47.gain, ...), custom_call_target="tpu_custom_call" | custom-call | tf_op jit(solution)/shard_map/feed_forward/pallas_call | solution.py:1664
  321.0 0.7 squeeze.48.gain
  321.7 47.6 %attend_forward.3 = (f32[64,1536]{1,0:T(8,128)}, bf16[4,64,1536]{2,1,0:T(8,128)(2,1)}, bf16[256,384]{1,0:T(8,128)(2,1)}, bf16[4,256,256]{2,1,0:T(8,128)(2,1)}, f...) custom-call(bf16[64,1536]{1,0:T(8,128)(2,1)} %get-tuple-element.62.x_ref.act0, f32[1,1536]{1,0:T(1,128)} %squeeze.48.gain, ...), custom_call_target="tpu_custom_call" | custom-call | tf_op jit(solution)/shard_map/attend_forward/pallas_call | solution.py:1167
  369.3 0.7 squeeze.50.gain
  370.0 81.4 %feed_forward.3 = (bf16[64,1536]{1,0:T(8,128)(2,1)}, bf16[2,4,4,64,1536]{4,3,2,1,0:T(8,128)(2,1)}, bf16[2,4,256,384]{3,2,1,0:T(8,128)(2,1)}, bf16[2,4,256,384]{3,2,1,0:T(8,128)(2,1)}, bf16[2,4,256,384]{3,2,1,0:T(8,128)(2,1)}) custom-call(f32[64,1536]{1,0:T(8,128)} %get-tuple-element.63.h1, f32[1,1536]{1,0:T(1,128)} %squeeze.50.gain, ...), custom_call_target="tpu_custom_call" | custom-call | tf_op jit(solution)/shard_map/feed_forward/pallas_call | solution.py:1664
  451.4 96.9 %feed_backward.2 = (f32[64,1536]{1,0:T(8,128)}, bf16[3,1536,384]{2,1,0:T(8,128)(2,1)}, f32[1,1536]{1,0:T(1,128)}) custom-call(bf16[64,1536]{1,0:T(8,128)(2,1)} %get-tuple-element.56.dy, f32[64,1536]{1,0:T(8,128)} %get-tuple-element.63.h1, f32[1,1536]{1,0:T(1,128)} %squeeze.50.gain, bf16[2,3,1536,384]{3,2,1,0:T(8,128)(2,1)} %get-tuple-element.61.w_all, ...), custom_call_target="tpu_custom_call" | custom-call | tf_op jit(solution)/shard_map/feed_backward/pallas_call | solution.py:1769
  548.2 46.1 %attend_backward.2 = (bf16[64,1536]{1,0:T(8,128)(2,1)}, bf16[1536,1024]{1,0:T(8,128)(2,1)}, f32[1,1536]{1,0:T(1,128)}, f32[1,640]{1,0:T(1,128)}) custom-call(f32[64,1536]{1,0:T(8,128)} %get-tuple-element.68.dh1, bf16[64,1536]{1,0:T(8,128)(2,1)} %get-tuple-element.62.x_ref.act0, f32[1,1536]{1,0:T(1,128)} %squeeze.48.gain, ...), custom_call_target="tpu_custom_call" | custom-call | tf_op jit(solution)/shard_map/attend_backward/pallas_call | solution.py:1308
  594.4 82.6 %feed_backward.3 = (f32[64,1536]{1,0:T(8,128)}, bf16[3,1536,384]{2,1,0:T(8,128)(2,1)}, f32[1,1536]{1,0:T(1,128)}) custom-call(bf16[64,1536]{1,0:T(8,128)(2,1)} %get-tuple-element.74.dy.grad1, f32[64,1536]{1,0:T(8,128)} %get-tuple-element.60.h1, f32[1,1536]{1,0:T(1,128)} %squeeze.47.gain, bf16[2,3,1536,384]{3,2,1,0:T(8,128)(2,1)} %get-tuple-element.61.w_all, ...), custom_call_target="tpu_custom_call" | custom-call | tf_op jit(solution)/shard_map/feed_backward/pallas_call | solution.py:1769
  677.0 47.6 %attend_backward.3 = (bf16[64,1536]{1,0:T(8,128)(2,1)}, bf16[1536,1024]{1,0:T(8,128)(2,1)}, f32[1,1536]{1,0:T(1,128)}, f32[1,640]{1,0:T(1,128)}) custom-call(f32[64,1536]{1,0:T(8,128)} %get-tuple-element.81.dh1, bf16[64,1536]{1,0:T(8,128)(2,1)} %get-tuple-element.57.x_ref, f32[1,1536]{1,0:T(1,128)} %squeeze.45.gain, ...), custom_call_target="tpu_custom_call" | custom-call | tf_op jit(solution)/shard_map/attend_backward/pallas_call | solution.py:1308
  724.6 0.7 constant_dynamic-update-slice_fusion.5
  725.3 0.6 constant_dynamic-update-slice_fusion.4
  725.9 0.7 constant_dynamic-update-slice_fusion.3
  726.8 0.1 reshape.138
  726.9 0.7 reduce.4
  727.9 0.1 reshape.142
  728.3 0.1 concatenate.35
  728.4 0.7 pad_maximum_fusion.1.small
  729.1 241.7 %collect_gradients.1 = (bf16[3,96,8960]{2,1,0:T(8,128)(2,1)}, bf16[16,96,1024]{2,1,0:T(8,128)(2,1)}, f32[32,8,128]{2,1,0:T(8,128)}, bf16[2,64,1536]{2,1,0:T(8,128)(2,1)}, bf16[2,64,1536]{2,1,0:T(8,128)(2,1)}) custom-call(bf16[3,1536,384]{2,1,0:T(8,128)(2,1)} %get-tuple-element.79.dw0, bf16[3,1536,384]{2,1,0:T(8,128)(2,1)} %get-tuple-element.80.dw1, ...), custom_call_target="tpu_custom_call" | custom-call | tf_op jit(solution)/shard_map/collect_gradients/pallas_call | solution.py:1002
  970.8 4.7 slice_convert_fusion
  975.5 3.5 maximum_convert_fusion
  979.0 0.6 convert_reduce_fusion
  979.7 0.1 slice_bitcast_fusion
  979.9 0.2 reshape.146
  980.1 0.3 reduce_sum.29
  980.4 0.2 copy.54
  980.6 0.2 reshape.147
  980.8 0.9 maximum_bitcast_fusion
  981.7 0.4 copy.55
  982.1 1.1 reshape.148
  983.2 0.5 fusion.9
  983.7 0.5 slice.113
  984.2 0.5 slice.114
  984.7 0.7 copy.81
  985.5 0.7 copy.82
  (63 shorter events, 1.1 us)
Async XLA Ops:
  0.6 188.2 %copy-start = (s32[2,1024]{1,0:T(2,128)S(1)}, s32[2,1024]{1,0:T(2,128)}, u32[]{:S(2)}) copy-start(s32[2,1024]{1,0:T(2,128)} %param.11) | copy-start | bytes 24580
  677.0 49.8 %copy-start.9 = (f32[1,640]{1,0:T(1,128)S(1)}, f32[1,640]{1,0:T(1,128)}, u32[]{:S(2)}) copy-start(f32[1,640]{1,0:T(1,128)} %get-tuple-element.94) | copy-start | bytes 7684
  677.0 50.7 %copy-start.8 = (f32[1,1536]{1,0:T(1,128)S(1)}, f32[1,1536]{1,0:T(1,128)}, u32[]{:S(2)}) copy-start(f32[1,1536]{1,0:T(1,128)} %get-tuple-element.90) | copy-start | bytes 18436
  677.0 51.1 %copy-start.7 = (f32[1,1536]{1,0:T(1,128)S(1)}, f32[1,1536]{1,0:T(1,128)}, u32[]{:S(2)}) copy-start(f32[1,1536]{1,0:T(1,128)} %get-tuple-element.92) | copy-start | bytes 18436
  677.0 51.2 %copy-start.6 = (f32[1,1536]{1,0:T(1,128)S(1)}, f32[1,1536]{1,0:T(1,128)}, u32[]{:S(2)}) copy-start(f32[1,1536]{1,0:T(1,128)} %get-tuple-element.93) | copy-start | bytes 18436
  975.5 3.5 copy-start.2
  979.9 3.3 copy-start.5
  979.9 4.9 copy-start.4
  980.1 5.4 copy-start.3
  980.4 5.8 copy-start.1

commit v2 on v0

--- a/solution.py
+++ b/solution.py
@@ -1,8 +1,11 @@
+import functools
 import math
 
 import jax
 import jax.numpy as jnp
 from jax import lax
+from jax.experimental import pallas as pl
+from jax.experimental.pallas import tpu as pltpu
 from jax.sharding import PartitionSpec as P
 
 FF = 8960
@@ -478,6 +481,1739 @@
     )
 
 
+MESH_ID = pl.DeviceIdType.MESH
+BF = jnp.bfloat16
+F32 = jnp.float32
+LANES = 128
+HB = 128
+VMEM_LIMIT = 60 * 1024 * 1024
+DMA = pltpu.SemaphoreType.DMA
+NT = (((1,), (1,)), ((), ()))
+TN = (((0,), (0,)), ((), ()))
+NN = (((1,), (0,)), ((), ()))
+
+
+def mm(left_side, right_side, form=NN):
+    return lax.dot_general(left_side, right_side, form, preferred_element_type=F32)
+
+
+def where_am_i():
+    head = lax.axis_index("head")
+    return (lax.axis_index("section"), head // 2, lax.rem(head, 2), lax.axis_index("ctx"))
+
+
+def at(x, y, k, z):
+    return (x, y * 2 + k, z)
+
+
+def remote(source, target, send_sem, recv_sem, device):
+    return pltpu.make_async_remote_copy(
+        src_ref=source,
+        dst_ref=target,
+        send_sem=send_sem,
+        recv_sem=recv_sem,
+        device_id=device,
+        device_id_type=MESH_ID,
+    )
+
+
+def arrived(ref, sem):
+    pltpu.make_async_copy(ref, ref, sem).wait()
+
+
+def greet(devices):
+    barrier = pltpu.get_barrier_semaphore()
+    for device in devices:
+        pl.semaphore_signal(barrier, inc=1, device_id=device, device_id_type=MESH_ID)
+    pl.semaphore_wait(barrier, len(devices))
+
+
+def greet_all(index, total, device_of):
+    barrier = pltpu.get_barrier_semaphore()
+
+    @pl.loop(1, total)
+    def _(step):
+        device = device_of(lax.rem(index + step, total))
+        pl.semaphore_signal(barrier, inc=1, device_id=device, device_id_type=MESH_ID)
+
+    pl.semaphore_wait(barrier, total - 1)
+
+
+def params(collective_id):
+    return pltpu.CompilerParams(
+        collective_id=collective_id, has_side_effects=True, vmem_limit_bytes=VMEM_LIMIT
+    )
+
+
+def vmem():
+    return pl.BlockSpec(memory_space=pltpu.VMEM)
+
+
+def hbm():
+    return pl.BlockSpec(memory_space=pl.ANY)
+
+
+def row_norm(values):
+    return lax.rsqrt(jnp.mean(values * values, axis=-1, keepdims=True) + EPSILON)
+
+
+class Sizes:
+    def __init__(self, mesh, tokens, qkv_weight, gate_up, down):
+        self.ctx = mesh.shape["ctx"]
+        self.group = 4 * self.ctx
+        self.total = 2 * self.group
+        self.batches, self.seq, self.width = tokens.shape
+        self.rows = self.seq // self.group
+        self.ff = down.shape[2]
+        self.owned = self.width // self.group
+        self.blocks = self.ff // HB
+        self.most = -(-self.blocks // self.total)
+        self.least = self.blocks // self.total
+        self.extra = self.blocks % self.total
+        self.hidden = self.most * HB
+        self.per_group = QUERY_HEADS // 4
+        self.qcols = self.per_group * HEAD_WIDTH_SIZE
+        self.kcols = HEAD_WIDTH_SIZE
+        self.acols = self.qcols + 2 * self.kcols
+        self.atot = self.acols + self.qcols
+
+    def fits(self):
+        gathered = self.batches * self.seq * self.width * 2
+        return (
+            self.batches == 2
+            and gathered * 3 < VMEM_LIMIT // 2
+            and self.ff % HB == 0
+            and self.least >= 1
+            and self.owned % 16 == 0
+            and self.rows % 32 == 0
+        )
+
+
+def flat_place(index, group, ctx):
+    inside = lax.rem(index, group)
+    return (index // group, inside // ctx, lax.rem(inside, ctx))
+
+
+def first_column(sz, owner):
+    return pl.multiple_of((owner * sz.least + jnp.minimum(owner, sz.extra)) * HB, HB)
+
+
+def plane_blocks(sz, plane):
+    start = plane * sz.group * sz.least + min(plane * sz.group, sz.extra)
+    stop = (plane + 1) * sz.group * sz.least + min((plane + 1) * sz.group, sz.extra)
+    return (start, stop - start)
+
+
+def half_turn(values):
+    return pltpu.roll(values, HEAD_WIDTH_SIZE // 2, 1)
+
+
+def pair_peers(x, y, k, z):
+    return (at(1 - x, y, k, z), at(x, 1 - y, k, z), at(1 - x, 1 - y, k, z))
+
+
+def pair_groups(x, y):
+    return (2 * (1 - x) + y, 2 * x + 1 - y, 2 * (1 - x) + 1 - y)
+
+
+def line_peers(n, x, y, k, z):
+    return [at(x, y, k, lax.rem(z + step, n)) for step in range(1, n)]
+
+
+def tree_peers(n, x, y, k, z):
+    return [at(1 - x, y, k, z), at(x, 1 - y, k, z), at(x, y, 1 - k, z)] + line_peers(n, x, y, k, z)
+
+
+def meet(sz, place, near, across, jobs):
+    x, y, k, z = place
+    n = sz.ctx
+    inside = (y * 2 + k) * n + z
+    reach = max([job.reach for job in jobs], default=0)
+    if reach == 2:
+        greet_all(x * sz.group + inside, sz.total, lambda index: flat_place(index, sz.group, n))
+    elif reach == 1:
+        barrier = pltpu.get_barrier_semaphore()
+        for device in across:
+            pl.semaphore_signal(barrier, inc=1, device_id=device, device_id_type=MESH_ID)
+
+        @pl.loop(1, sz.group)
+        def _(step):
+            device = flat_place(x * sz.group + lax.rem(inside + step, sz.group), sz.group, n)
+            pl.semaphore_signal(barrier, inc=1, device_id=device, device_id_type=MESH_ID)
+
+        pl.semaphore_wait(barrier, sz.group - 1 + len(across))
+    else:
+        greet(near)
+
+
+def run_call(body, ins, outs, scratch, jobs, collective_id, name):
+    fg_in, fg_out, fg_scratch = len(ins), len(outs), len(scratch)
+    ins, outs, scratch = list(ins), list(outs), list(scratch)
+    for job in jobs:
+        ins += [(array, hbm() if spec is None else spec) for array, spec in job.ins]
+        outs += [(shape, hbm()) for shape in job.outs]
+        scratch += job.scratch
+
+    def kernel(*refs):
+        given, made, own = (
+            refs[: len(ins)],
+            refs[len(ins) : len(ins) + len(outs)],
+            refs[len(ins) + len(outs) :],
+        )
+        a, b, c = fg_in, fg_out, fg_scratch
+        for job in jobs:
+            job.bind(
+                given[a : a + len(job.ins)],
+                made[b : b + len(job.outs)],
+                own[c : c + len(job.scratch)],
+            )
+            a, b, c = a + len(job.ins), b + len(job.outs), c + len(job.scratch)
+        body(given[:fg_in], made[:fg_out], own[:fg_scratch], jobs)
+
+    results = pl.pallas_call(
+        kernel,
+        out_shape=tuple(shape for shape, _ in outs),
+        in_specs=[spec for _, spec in ins],
+        out_specs=tuple(spec for _, spec in outs),
+        scratch_shapes=scratch,
+        compiler_params=params(collective_id),
+        name=name,
+    )(*[array for array, _ in ins])
+    at_out, extra = fg_out, []
+    for job in jobs:
+        extra.append(results[at_out : at_out + len(job.outs)])
+        at_out += len(job.outs)
+    return (results[:fg_out], extra)
+
+
+def plane_order(n, place, index):
+    x, y, k, z = place
+    head = y * 2 + k
+    far = 4 * (n - 1)
+    if isinstance(index, int) and index == 4 * n - 1:
+        return head * n + z
+    rest = index - far
+    head_to = lax.rem(head + jnp.where(index < far, index // (n - 1), rest + 1), 4)
+    ctx_to = lax.rem(z + jnp.where(index < far, 1 + lax.rem(index, n - 1), 0), n)
+    return head_to * n + ctx_to
+
+
+def span_of(count, low, high):
+    return (int(count * low), int(count * high))
+
+
+class Columns:
+    reach = 1
+
+    def __init__(self, sz, section, part, gate_up, down, staged):
+        self.sz, self.section, self.part = sz, section, part
+        self.ins = [(down if part == 2 else gate_up, None), (staged, None)]
+        self.outs = [jax.ShapeDtypeStruct((sz.width, sz.hidden), BF)]
+        self.scratch = [DMA((2,)), DMA((2,))]
+
+    def bind(self, ins, outs, scratch):
+        self.source, self.staged = ins
+        self.target = outs[0]
+        self.send, self.recv = scratch
+
+    def begin(self, place, low=0.0, high=1.0):
+        sz = self.sz
+        n = sz.ctx
+        x, y, k, z = place
+        inside = (y * 2 + k) * n + z
+        me = x * sz.group + inside
+        first, stop = span_of(sz.group, low, high)
+        rows = pl.ds(pl.multiple_of(inside * sz.owned, 16), sz.owned)
+        wide = sz.least * HB
+        base = sz.ff if self.part == 1 else 0
+
+        def pair(owner, offset, width, own):
+            target = self.target.at[rows, pl.ds(offset, width)]
+            if own:
+                first = pl.multiple_of(base + first_column(sz, owner) + offset, HB)
+                return (self.source.at[:, pl.ds(first, width)], target)
+            first = first_column(sz, owner) - first_column(sz, x * sz.group) + offset
+            first = pl.multiple_of(first, HB)
+            return (self.staged.at[self.part, :, pl.ds(first, width)], target)
+
+        for own in (True, False):
+
+            @pl.when((x == self.section) == own)
+            def _():
+                @pl.loop(first, min(stop, sz.group - 1))
+                def _(step):
+                    owner = x * sz.group + plane_order(n, place, step)
+                    device = flat_place(owner, sz.group, n)
+                    source, target = pair(owner, 0, wide, own)
+                    remote(source, target, self.send.at[0], self.recv.at[0], device).start()
+                    if sz.extra:
+
+                        @pl.when(owner < sz.extra)
+                        def _():
+                            source, target = pair(owner, wide, HB, own)
+                            remote(source, target, self.send.at[1], self.recv.at[1], device).start()
+
+                if stop < sz.group:
+                    return
+                source, target = pair(me, 0, wide, own)
+                pltpu.make_async_copy(source, target, self.send.at[0]).start()
+                if sz.extra:
+
+                    @pl.when(me < sz.extra)
+                    def _():
+                        source, target = pair(me, wide, HB, own)
+                        pltpu.make_async_copy(source, target, self.send.at[1]).start()
+
+    def middle(self, place):
+        pass
+
+    def finish(self, place):
+        sz = self.sz
+        x, y, k, z = place
+        me = x * sz.group + (y * 2 + k) * sz.ctx + z
+        wide = sz.least * HB
+        arrived(self.target.at[pl.ds(0, sz.width - sz.owned), pl.ds(0, wide)], self.recv.at[0])
+        arrived(self.target.at[:, pl.ds(0, wide)], self.send.at[0])
+        for plane in range(2):
+            count = min(max(sz.extra - plane * sz.group, 0), sz.group)
+            if count:
+
+                @pl.when(x == plane)
+                def _():
+                    arrived(self.target.at[pl.ds(0, count * sz.owned), pl.ds(0, HB)], self.send.at[1])
+
+                    @pl.when(me < sz.extra)
+                    def _():
+                        arrived(
+                            self.target.at[pl.ds(0, sz.width - sz.owned), pl.ds(0, HB)],
+                            self.recv.at[1],
+                        )
+
+
+def head_columns(sz, g, qkv, out_w):
+    kv = g // (4 // KEY_VALUE_HEADS)
+    q0 = pl.multiple_of(g * sz.qcols, HB)
+    k0 = pl.multiple_of(QUERY_HEADS * HEAD_WIDTH_SIZE + kv * sz.kcols, HB)
+    v0 = pl.multiple_of((QUERY_HEADS + KEY_VALUE_HEADS) * HEAD_WIDTH_SIZE + kv * sz.kcols, HB)
+    return (
+        (qkv.at[:, pl.ds(q0, sz.qcols)], pl.ds(0, sz.qcols)),
+        (qkv.at[:, pl.ds(k0, sz.kcols)], pl.ds(sz.qcols, sz.kcols)),
+        (qkv.at[:, pl.ds(v0, sz.kcols)], pl.ds(sz.qcols + sz.kcols, sz.kcols)),
+        (out_w.at[:, pl.ds(q0, sz.qcols)], pl.ds(sz.acols, sz.qcols)),
+    )
+
+
+class Heads:
+    reach = 1
+
+    def __init__(self, sz, section, qkv, out_w, staged):
+        self.sz, self.section = sz, section
+        self.ins = [(qkv, None), (out_w, None), (staged, None)]
+        self.outs = [jax.ShapeDtypeStruct((sz.width, sz.atot), BF)]
+        self.scratch = [DMA, DMA, DMA((2,)), DMA((2,))]
+
+    def bind(self, ins, outs, scratch):
+        self.qkv, self.out_w, self.staged = ins
+        self.target = outs[0]
+        self.send, self.recv, self.s_core, self.r_core = scratch
+
+    def begin(self, place, low=0.0, high=1.0):
+        sz = self.sz
+        n = sz.ctx
+        x, y, k, z = place
+        rows = pl.ds(pl.multiple_of(((y * 2 + k) * n + z) * sz.owned, 16), sz.owned)
+        mine = y * n + z
+
+        def pairs(y_to, own):
+            if own:
+                return [
+                    (source, self.target.at[rows, cols])
+                    for source, cols in head_columns(sz, 2 * x + y_to, self.qkv, self.out_w)
+                ]
+            return [(self.staged.at[y_to], self.target.at[rows])]
+
+        for own in (True, False):
+
+            @pl.when((x == self.section) == own)
+            def _():
+                @pl.loop(1, 2 * n)
+                def _(step):
+                    index = lax.rem(mine + step, 2 * n)
+                    for source, target in pairs(index // n, own):
+                        remote(
+                            source, target, self.send, self.recv, at(x, index // n, k, lax.rem(index, n))
+                        ).start()
+
+                for source, target in pairs(y, own):
+                    pltpu.make_async_copy(source, target, self.send).start()
+
+    def span(self, part, k):
+        stretch = self.sz.width // 4
+        return self.target.at[pl.ds(pl.multiple_of((part * 2 + k) * stretch, 16), stretch)]
+
+    def middle(self, place):
+        sz = self.sz
+        x, y, k, z = place
+        half = sz.width // 2
+        arrived(self.target.at[pl.ds(0, half - sz.owned)], self.recv)
+        arrived(self.target.at[pl.ds(0, half)], self.send)
+        for part in range(2):
+            span = self.span(part, k)
+            remote(span, span, self.s_core.at[part], self.r_core.at[part], at(x, y, 1 - k, z)).start()
+
+    def finish(self, place):
+        x, y, k, z = place
+        for part in range(2):
+            span = self.span(part, 1 - k)
+            arrived(span, self.r_core.at[part])
+            arrived(span, self.s_core.at[part])
+
+
+class Returned:
+    reach = 2
+
+    def __init__(self, sz, section, parts, grads):
+        self.sz, self.section, self.parts = sz, section, parts
+        self.ins = [(grads, None)]
+        self.outs = [jax.ShapeDtypeStruct((sz.owned, sz.ff), BF) for _ in parts]
+        self.scratch = [DMA((2, len(parts))), DMA((2, len(parts)))]
+
+    def bind(self, ins, outs, scratch):
+        self.source, self.targets = ins[0], outs
+        self.send, self.recv = scratch
+
+    def begin(self, place, low=0.0, high=1.0):
+        sz = self.sz
+        n = sz.ctx
+        x, y, k, z = place
+        inside = (y * 2 + k) * n + z
+        me = x * sz.group + inside
+        first, stop = span_of(sz.group, low, high)
+        wide = sz.least * HB
+        cols = pl.ds(first_column(sz, me), wide)
+        more = pl.ds(pl.multiple_of(first_column(sz, me) + wide, HB), HB)
+
+        def moves(device, slot):
+            rows = pl.ds(pl.multiple_of(device * sz.owned, 16), sz.owned)
+            source = self.source.at[self.parts[slot], rows]
+            base = (source.at[:, pl.ds(0, wide)], self.targets[slot].at[:, cols])
+            last = (source.at[:, pl.ds(wide, HB)], self.targets[slot].at[:, more])
+            return (base, last)
+
+        def go(device, local):
+            for slot in range(len(self.parts)):
+                base, last = moves(device, slot)
+
+                def start(pair, kind):
+                    if local:
+                        pltpu.make_async_copy(*pair, self.send.at[kind, slot]).start()
+                    else:
+                        remote(
+                            *pair,
+                            self.send.at[kind, slot],
+                            self.recv.at[kind, slot],
+                            (self.section, device // n, lax.rem(device, n)),
+                        ).start()
+
+                start(base, 0)
+                if sz.extra:
+
+                    @pl.when(me < sz.extra)
+                    def _():
+                        start(last, 1)
+
+        @pl.loop(first, min(stop, sz.group - 1))
+        def _(step):
+            go(plane_order(n, place, step), False)
+
+        if stop < sz.group:
+            return
+        for own in (True, False):
+
+            @pl.when((x == self.section) == own)
+            def _():
+                go(inside, own)
+
+    def middle(self, place):
+        pass
+
+    def finish(self, place):
+        sz = self.sz
+        x, y, k, z = place
+        me = x * sz.group + (y * 2 + k) * sz.ctx + z
+        wide = sz.least * HB
+        for slot, target in enumerate(self.targets):
+            arrived(target.at[:, pl.ds(0, sz.group * wide)], self.send.at[0, slot])
+            if sz.extra:
+
+                @pl.when(me < sz.extra)
+                def _():
+                    arrived(target.at[:, pl.ds(0, sz.group * HB)], self.send.at[1, slot])
+
+            @pl.when(x == self.section)
+            def _():
+                arrived(target.at[:, pl.ds(0, (sz.total - 1) * wide)], self.recv.at[0, slot])
+                if sz.extra:
+
+                    @pl.when(me >= sz.extra)
+                    def _():
+                        arrived(target.at[:, pl.ds(0, sz.extra * HB)], self.recv.at[1, slot])
+
+                    if sz.extra > 1:
+
+                        @pl.when(me < sz.extra)
+                        def _():
+                            arrived(target.at[:, pl.ds(0, (sz.extra - 1) * HB)], self.recv.at[1, slot])
+
+
+class ReturnedHeads:
+    reach = 2
+
+    def __init__(self, sz, section, grads):
+        self.sz, self.section = sz, section
+        stretch = sz.width // 4
+        self.ins = [(grads, vmem())]
+        self.outs = [jax.ShapeDtypeStruct((sz.group, sz.owned, sz.atot), BF)]
+        self.scratch = [
+            pltpu.VMEM((2, stretch, sz.atot), BF),
+            pltpu.VMEM((2, stretch, sz.atot), BF),
+            DMA((2,)),
+            DMA((2,)),
+            DMA,
+            DMA,
+        ]
+
+    def bind(self, ins, outs, scratch):
+        self.source, self.target = ins[0], outs[0]
+        self.got, self.summed, self.s_core, self.r_core, self.send, self.recv = scratch
+
+    def rows(self, part, k):
+        stretch = self.sz.width // 4
+        return pl.ds(pl.multiple_of((part * 2 + k) * stretch, 16), stretch)
+
+    def core(self, place, part):
+        x, y, k, z = place
+        return remote(
+            self.source.at[self.rows(part, 1 - k)],
+            self.got.at[part],
+            self.s_core.at[part],
+            self.r_core.at[part],
+            at(x, y, 1 - k, z),
+        )
+
+    def begin(self, place, low=0.0, high=1.0):
+        for part in range(2):
+            self.core(place, part).start()
+
+    def middle(self, place):
+        sz = self.sz
+        n = sz.ctx
+        x, y, k, z = place
+        for part in range(2):
+            self.core(place, part).wait_recv()
+            total = self.source[self.rows(part, k)].astype(F32) + self.got[part].astype(F32)
+            self.summed[part] = total.astype(BF)
+        slot = (2 * x + y) * n + z
+        mine = y * n + z
+
+        def pair(index):
+            rows = pl.ds(pl.multiple_of(lax.rem(index, n) * sz.owned, 16), sz.owned)
+            return (self.summed.at[index // n, rows], self.target.at[slot])
+
+        def go(index):
+            device = at(self.section, index // n, k, lax.rem(index, n))
+            remote(*pair(index), self.send, self.recv, device).start()
+
+        @pl.loop(1, 2 * n)
+        def _(step):
+            go(lax.rem(mine + step, 2 * n))
+
+        @pl.when(x == self.section)
+        def _():
+            pltpu.make_async_copy(*pair(mine), self.send).start()
+
+        @pl.when(x != self.section)
+        def _():
+            go(mine)
+
+    def finish(self, place):
+        sz = self.sz
+        x, y, k, z = place
+        for part in range(2):
+            self.core(place, part).wait_send()
+        arrived(self.target.at[pl.ds(0, 2 * sz.ctx)], self.send)
+
+        @pl.when(x == self.section)
+        def _():
+            arrived(self.target.at[pl.ds(0, sz.group - 1)], self.recv)
+
+
+def begin(jobs, place, low=0.0, high=1.0):
+    for job in jobs:
+        job.begin(place, low, high)
+
+
+def middle(jobs, place):
+    for job in jobs:
+        job.middle(place)
+
+
+def finish(jobs, place):
+    for job in jobs:
+        job.finish(place)
+
+
+class Gather:
+    SEMS = 12
+
+    @staticmethod
+    def scratch(n):
+        return [DMA((n,))] * 10 + [DMA((4, n))] * 2
+
+    def __init__(self, n, rows, buffer, place, sems):
+        self.n, self.half, self.buffer = n, rows // 2, buffer
+        self.x, self.y, self.k, self.z = place
+        x, y = self.x, self.y
+        self.groups = (2 * x + y, 2 * x + 1 - y, 2 * (1 - x) + y, 2 * (1 - x) + 1 - y)
+        (
+            self.sz,
+            self.rz,
+            self.sy,
+            self.ry,
+            self.sx,
+            self.rx,
+            self.syd,
+            self.ryd,
+            self.sxd,
+            self.rxd,
+            self.sc,
+            self.rc,
+        ) = sems
+
+    def src(self, step):
+        return lax.rem(self.z + self.n - step, self.n)
+
+    def line(self, step):
+        own = self.buffer.at[self.k, self.groups[0], self.z]
+        device = at(self.x, self.y, self.k, lax.rem(self.z + step, self.n))
+        return remote(own, own, self.sz.at[step], self.rz.at[step], device)
+
+    def to_y(self, step):
+        part = self.buffer.at[self.k, self.groups[0], self.src(step)]
+        device = at(self.x, 1 - self.y, self.k, self.z)
+        return remote(part, part, self.sy.at[step], self.ry.at[step], device)
+
+    def to_x(self, step):
+        part = self.buffer.at[self.k, self.groups[0], self.src(step)]
+        device = at(1 - self.x, self.y, self.k, self.z)
+        return remote(part, part, self.sx.at[step], self.rx.at[step], device)
+
+    def on_x(self, step):
+        part = self.buffer.at[self.k, self.groups[1], self.src(step), pl.ds(0, self.half)]
+        device = at(1 - self.x, self.y, self.k, self.z)
+        return remote(part, part, self.sxd.at[step], self.rxd.at[step], device)
+
+    def on_y(self, step):
+        part = self.buffer.at[self.k, self.groups[2], self.src(step), pl.ds(self.half, self.half)]
+        device = at(self.x, 1 - self.y, self.k, self.z)
+        return remote(part, part, self.syd.at[step], self.ryd.at[step], device)
+
+    def core(self, which, step):
+        part = self.buffer.at[self.k, self.groups[which], self.src(step)]
+        device = at(self.x, self.y, 1 - self.k, self.z)
+        return remote(part, part, self.sc.at[which, step], self.rc.at[which, step], device)
+
+    def begin(self):
+        for step in range(1, self.n):
+            self.line(step).start()
+        self.spread(0)
+
+    def spread(self, step):
+        if step:
+            arrived(self.buffer.at[self.k, self.groups[0], self.src(step)], self.rz.at[step])
+        self.to_y(step).start()
+        self.to_x(step).start()
+        self.core(0, step).start()
+
+    def second(self, step):
+        arrived(self.buffer.at[self.k, self.groups[1], self.src(step)], self.ry.at[step])
+        self.on_x(step).start()
+        self.core(1, step).start()
+        arrived(self.buffer.at[self.k, self.groups[2], self.src(step)], self.rx.at[step])
+        self.on_y(step).start()
+        self.core(2, step).start()
+
+    def third(self, step):
+        part = self.buffer.at[self.k, self.groups[3], self.src(step)]
+        arrived(part.at[pl.ds(0, self.half)], self.rxd.at[step])
+        arrived(part.at[pl.ds(self.half, self.half)], self.ryd.at[step])
+        self.core(3, step).start()
+
+    def other(self, which):
+        for step in range(self.n):
+            part = self.buffer.at[1 - self.k, self.groups[which], self.src(step)]
+            arrived(part, self.rc.at[which, step])
+
+    def finish(self):
+        for step in range(self.n):
+            if step:
+                self.line(step).wait_send()
+            self.to_y(step).wait_send()
+            self.to_x(step).wait_send()
+            self.on_x(step).wait_send()
+            self.on_y(step).wait_send()
+            for which in range(4):
+                self.core(which, step).wait_send()
+
+    def run(self, column, nearly):
+        k, steps = self.k, range(self.n)
+        for step in range(1, self.n):
+            self.spread(step)
+        column(k, 0)
+        for step in steps:
+            self.second(step)
+        self.other(0)
+        column(1 - k, 0)
+        column(k, 1)
+        column(k, 2)
+        for step in steps:
+            self.third(step)
+        self.other(1)
+        column(1 - k, 1)
+        self.other(2)
+        column(1 - k, 2)
+        nearly()
+        column(k, 3)
+        self.other(3)
+        column(1 - k, 3)
+
+
+class Scatter:
+    @staticmethod
+    def scratch(n, rows, width):
+        return [
+            pltpu.VMEM((2, 4, n, rows, width), BF),
+            pltpu.VMEM((4, n, rows, width), BF),
+            pltpu.VMEM((2, n, rows // 2, width), BF),
+            pltpu.VMEM((2, n, rows, width), BF),
+            pltpu.VMEM((n, rows, width), BF),
+            DMA((4,)),
+            DMA((4,)),
+            DMA((2, n)),
+            DMA((2, n)),
+            DMA((2, 2, n)),
+            DMA((2, 2, n)),
+            DMA((n,)),
+            DMA((n,)),
+        ]
+
+    def __init__(self, n, rows, place, refs):
+        self.n, self.rows, self.half = n, rows, rows // 2
+        self.x, self.y, self.k, self.z = place
+        x, y = self.x, self.y
+        self.groups = (2 * x + y, 2 * x + 1 - y, 2 * (1 - x) + y, 2 * (1 - x) + 1 - y)
+        (
+            self.parts,
+            self.from_core,
+            self.from_diag,
+            self.from_near,
+            self.from_line,
+            self.s_core,
+            self.r_core,
+            self.s_diag,
+            self.r_diag,
+            self.s_near,
+            self.r_near,
+            self.s_line,
+            self.r_line,
+        ) = refs
+        self.near = (at(x, 1 - y, self.k, self.z), at(1 - x, y, self.k, self.z))
+
+    def slot(self, step):
+        return lax.rem(self.z + step, self.n)
+
+    def order(self):
+        return list(range(1, self.n)) + [0]
+
+    def core(self, which):
+        return remote(
+            self.parts.at[1 - self.k, self.groups[which]],
+            self.from_core.at[which],
+            self.s_core.at[which],
+            self.r_core.at[which],
+            at(self.x, self.y, 1 - self.k, self.z),
+        )
+
+    def diag(self, direction, step):
+        rows = pl.ds(self.half if direction == 0 else 0, self.half)
+        return remote(
+            self.parts.at[self.k, self.groups[3], self.slot(step), rows],
+            self.from_diag.at[direction, step],
+            self.s_diag.at[direction, step],
+            self.r_diag.at[direction, step],
+            self.near[direction],
+        )
+
+    def close(self, direction, part, step):
+        rows = pl.ds(part * self.half, self.half)
+        return remote(
+            self.parts.at[self.k, self.groups[1 + direction], self.slot(step), rows],
+            self.from_near.at[direction, step, rows],
+            self.s_near.at[direction, part, step],
+            self.r_near.at[direction, part, step],
+            self.near[direction],
+        )
+
+    def line(self, step):
+        return remote(
+            self.parts.at[self.k, self.groups[0], self.slot(step)],
+            self.from_line.at[step],
+            self.s_line.at[step],
+            self.r_line.at[step],
+            at(self.x, self.y, self.k, self.slot(step)),
+        )
+
+    def add_core(self, which):
+        self.core(which).wait_recv()
+        group = self.groups[which]
+        self.parts[self.k, group] = (
+            self.parts[self.k, group].astype(F32) + self.from_core[which].astype(F32)
+        ).astype(BF)
+
+    def early(self):
+        for direction, part in ((0, 1), (1, 0)):
+            self.add_core(1 + direction)
+            for step in self.order():
+                self.close(direction, part, step).start()
+
+    def run(self, fill):
+        fill = list(fill) + [lambda: None] * 3
+        self.add_core(3)
+        for step in self.order():
+            self.diag(1, step).start()
+            self.diag(0, step).start()
+        self.add_core(0)
+        fill[0]()
+        for step in self.order():
+            slot = self.slot(step)
+            for direction, part in ((0, 0), (1, 1)):
+                came = 1 - direction
+                self.diag(came, step).wait_recv()
+                rows = pl.ds(part * self.half, self.half)
+                group = self.groups[1 + direction]
+                self.parts[self.k, group, slot, rows] = (
+                    self.parts[self.k, group, slot, rows].astype(F32)
+                    + self.from_diag[came, step].astype(F32)
+                ).astype(BF)
+                self.close(direction, part, step).start()
+        fill[1]()
+        group = self.groups[0]
+        result = None
+        for step in self.order():
+            slot = self.slot(step)
+            for direction in range(2):
+                for part in range(2):
+                    self.close(direction, part, step).wait_recv()
+            total = (
+                self.parts[self.k, group, slot].astype(F32)
+                + self.from_near[0, step].astype(F32)
+                + self.from_near[1, step].astype(F32)
+            )
+            if step:
+                self.parts[self.k, group, slot] = total.astype(BF)
+                self.line(step).start()
+            else:
+                result = total
+        fill[2]()
+        for step in range(1, self.n):
+            self.line(step).wait_recv()
+            result = result + self.from_line[step].astype(F32)
+        return result
+
+    def finish(self):
+        for which in range(4):
+            self.core(which).wait_send()
+        for step in range(self.n):
+            for direction in range(2):
+                self.diag(direction, step).wait_send()
+                for part in range(2):
+                    self.close(direction, part, step).wait_send()
+            if step:
+                self.line(step).wait_send()
+
+
+def spread(sz, small, tokens, cotangent, qkv, out_w, gate_up, down):
+    n = sz.ctx
+    counts = [plane_blocks(sz, plane) for plane in range(2)]
+    staged_cols = max(count for _, count in counts) * HB
+
+    def body(ins, outs, scratch, jobs):
+        small, tokens, cotangent, qkv, out_w, gate_up, down = ins
+        small_all, tok_own, cot_own, heads_x, cols_x = outs
+        s_small, r_small, s_own, r_own, s_hx, r_hx, s_cx, r_cx = scratch
+        place = where_am_i()
+        x, y, k, z = place
+        me = x * sz.group + (y * 2 + k) * n + z
+        everyone = lambda index: flat_place(index, sz.group, n)
+        greet_all(me, sz.total, everyone)
+        across = at(1 - x, y, k, z)
+
+        def heads_over():
+            return [
+                remote(source, heads_x.at[y_to, :, cols], s_hx, r_hx, across)
+                for y_to in range(2)
+                for source, cols in head_columns(sz, 2 * (1 - x) + y_to, qkv, out_w)
+            ]
+
+        for copy in heads_over():
+            copy.start()
+
+        def owns(starting):
+            @pl.when(x == y)
+            def _():
+                for batch in range(2):
+                    pairs = ((tokens, tok_own, 0), (cotangent, cot_own, 1))
+                    for source, target, slot in pairs:
+                        own = jnp.logical_and(k == y, k == batch)
+
+                        @pl.when(jnp.logical_not(own))
+                        def _():
+                            copy = remote(
+                                source.at[batch],
+                                target,
+                                s_own.at[batch, slot],
+                                r_own.at[slot],
+                                at(x, k, batch, z),
+                            )
+                            copy.start() if starting else copy.wait_send()
+
+                        if starting:
+
+                            @pl.when(own)
+                            def _():
+                                pltpu.make_async_copy(
+                                    source.at[batch], target, r_own.at[slot]
+                                ).start()
+
+        owns(True)
+
+        @pl.loop(1, sz.total)
+        def _(step):
+            device = everyone(lax.rem(me + step, sz.total))
+            remote(small, small_all.at[me], s_small, r_small, device).start()
+
+        pltpu.make_async_copy(small, small_all.at[me], s_small).start()
+
+        def columns_over(plane, part):
+            start, count = counts[1 - plane]
+            base = (sz.ff if part == 1 else 0) + start * HB
+            source = (down if part == 2 else gate_up).at[:, pl.ds(base, count * HB)]
+            target = cols_x.at[part, :, pl.ds(0, count * HB)]
+            return remote(source, target, s_cx.at[part], r_cx.at[part], across)
+
+        def for_plane(act):
+            for plane in range(2):
+
+                @pl.when(x == plane)
+                def _():
+                    for part in range(3):
+                        act(plane, part)
+
+        heads, first = jobs
+        heads.use(ins, outs)
+        first.use(ins, outs)
+
+        @pl.when(x == heads.section)
+        def _():
+            heads.begin(place)
+
+        for_plane(lambda plane, part: columns_over(plane, part).start())
+        arrived(heads_x, r_hx)
+
+        @pl.when(x != heads.section)
+        def _():
+            heads.begin(place)
+
+        def came(plane, part):
+            width = counts[plane][1] * HB
+            arrived(cols_x.at[part, :, pl.ds(0, width)], r_cx.at[part])
+
+        for plane in range(2):
+
+            @pl.when(x == plane)
+            def _():
+                came(plane, 0)
+
+        first.begin(place)
+        heads.middle(place)
+        arrived(small_all.at[pl.ds(0, sz.total - 1)], r_small)
+        arrived(small_all, s_small)
+        arrived(tok_own, r_own.at[0])
+        arrived(cot_own, r_own.at[1])
+        owns(False)
+        heads.finish(place)
+
+        def rest(plane, part):
+            if part:
+                came(plane, part)
+            columns_over(plane, part).wait_send()
+
+        for_plane(rest)
+        arrived(heads_x, s_hx)
+        first.finish(place)
+
+    shape = jax.ShapeDtypeStruct
+    outs = [
+        (shape((sz.total, 16, LANES), BF), hbm()),
+        (shape((sz.rows, sz.width), BF), hbm()),
+        (shape((sz.rows, sz.width), BF), hbm()),
+        (shape((2, sz.owned, sz.atot), BF), hbm()),
+        (shape((3, sz.owned, staged_cols), BF), hbm()),
+    ]
+    arrays = (small, tokens, cotangent, qkv, out_w, gate_up, down)
+    scratch = [DMA, DMA, DMA((2, 2)), DMA((2,)), DMA, DMA, DMA((3,)), DMA((3,))]
+    jobs = [OwnHeads(sz, 0, 3, 4, 3), OwnColumns(sz, 0, 0, 5, 4)]
+    return run_call(body, [(a, hbm()) for a in arrays], outs, scratch, jobs, 1, "spread_weights")
+
+
+class OwnHeads(Heads):
+    def __init__(self, sz, section, qkv, out_w, staged):
+        super().__init__(sz, section, None, None, None)
+        self.ins = []
+        self.named = (qkv, out_w, staged)
+
+    def bind(self, ins, outs, scratch):
+        self.target = outs[0]
+        self.send, self.recv, self.s_core, self.r_core = scratch
+
+    def use(self, ins, outs):
+        qkv, out_w, staged = self.named
+        self.qkv, self.out_w, self.staged = ins[qkv], ins[out_w], outs[staged]
+
+
+class OwnColumns(Columns):
+    def __init__(self, sz, section, part, source, staged):
+        super().__init__(sz, section, part, None, None, None)
+        self.ins = []
+        self.named = (source, staged)
+
+    def bind(self, ins, outs, scratch):
+        self.target = outs[0]
+        self.send, self.recv = scratch
+
+    def use(self, ins, outs):
+        source, staged = self.named
+        self.source, self.staged = ins[source], outs[staged]
+
+
+def gather_pair(buffer, place, send, recv):
+    x, y, k, z = place
+    own = buffer.at[2 * x + y]
+    copies = [
+        remote(own, own, send.at[i], recv.at[i], device)
+        for i, device in enumerate(pair_peers(x, y, k, z))
+    ]
+    for copy in copies:
+        copy.start()
+    return copies
+
+
+def gathered_pair(buffer, place, copies, recv):
+    x, y, k, z = place
+    for i, group in enumerate(pair_groups(x, y)):
+        arrived(buffer.at[group], recv.at[i])
+
+
+def scatter_pair(parts, landed, place, send, recv):
+    x, y, k, z = place
+    groups = pair_groups(x, y)
+    copies = [
+        remote(parts.at[groups[i]], landed.at[i], send.at[i], recv.at[i], device)
+        for i, device in enumerate(pair_peers(x, y, k, z))
+    ]
+    for copy in copies:
+        copy.start()
+    return copies
+
+
+def meet_pair(sz, place, jobs):
+    x, y, k, z = place
+    peers = pair_peers(x, y, k, z)
+    meet(sz, place, list(peers) + line_peers(sz.ctx, x, y, k, z), [peers[0], peers[2]], jobs)
+
+
+def attend(sz, section, x_own, gain, bias, watt, tables, qpos, kpos, jobs):
+    n, rows = sz.ctx, 4 * sz.rows
+
+    def body(ins, outs, scratch, jobs):
+        x_ref, gain, bias, watt, cosine, sine, qpos, kpos = ins
+        h1_out, n1_all, q_out, kv_all, o_out, lse_out = outs
+        w, parts, landed, w_sem, s_in, r_in, s_kv, r_kv, s_back, r_back = scratch
+        place = where_am_i()
+        x, y, k, z = place
+        load = pltpu.make_async_copy(watt, w, w_sem)
+        load.start()
+        meet_pair(sz, place, jobs)
+        group = 2 * x + y
+        values = x_ref[...].astype(F32)
+        n1_all[group] = (values * row_norm(values) * gain[...]).astype(BF)
+        copies = gather_pair(n1_all, place, s_in, r_in)
+        begin(jobs, place, 0.0, 0.3)
+        load.wait()
+        gathered_pair(n1_all, place, copies, r_in)
+        normed = n1_all[...].reshape(rows, sz.width)
+        kv = mm(normed, w[:, sz.qcols : sz.acols]) + bias[:, sz.qcols : sz.acols]
+        cos, sin = cosine[...], sine[...]
+        key = kv[:, : sz.kcols]
+        kv_all[z, :, : sz.kcols] = (key * cos + half_turn(key) * sin).astype(BF)
+        kv_all[z, :, sz.kcols :] = kv[:, sz.kcols :].astype(BF)
+        kv_copies = []
+        for step, device in enumerate(line_peers(n, x, y, k, z)):
+            own = kv_all.at[z]
+            kv_copies.append(remote(own, own, s_kv.at[step], r_kv.at[step], device))
+            kv_copies[-1].start()
+        begin(jobs, place, 0.3, 1.0)
+        queries = mm(normed, w[:, : sz.qcols]) + bias[:, : sz.qcols]
+        for head in range(sz.per_group):
+            cols = slice(head * HEAD_WIDTH_SIZE, (head + 1) * HEAD_WIDTH_SIZE)
+            query = queries[:, cols]
+            q_out[:, cols] = (query * cos + half_turn(query) * sin).astype(BF)
+        for step in range(n - 1):
+            arrived(kv_all.at[lax.rem(z + n - 1 - step, n)], r_kv.at[step])
+        keys = kv_all[:, :, : sz.kcols].reshape(n * rows, sz.kcols)
+        vals = kv_all[:, :, sz.kcols :].reshape(n * rows, sz.kcols)
+        allowed = kpos[...] <= qpos[...]
+        scale = 1.0 / math.sqrt(HEAD_WIDTH_SIZE)
+        for head in range(sz.per_group):
+            cols = slice(head * HEAD_WIDTH_SIZE, (head + 1) * HEAD_WIDTH_SIZE)
+            scores = jnp.where(allowed, mm(q_out[:, cols], keys, NT) * scale, -1e30)
+            highest = jnp.max(scores, axis=-1, keepdims=True)
+            weights = jnp.exp(scores - highest)
+            total = jnp.sum(weights, axis=-1, keepdims=True)
+            o_out[:, cols] = mm(weights.astype(BF), vals) / total
+            lse_out[head] = jnp.broadcast_to(highest + jnp.log(total), (rows, LANES))
+        partial = mm(o_out[...].astype(BF), w[:, sz.acols :], NT)
+        parts[...] = partial.astype(BF).reshape(4, sz.rows, sz.width)
+        back = scatter_pair(parts, landed, place, s_back, r_back)
+        middle(jobs, place)
+        for copy in copies + kv_copies:
+            copy.wait_send()
+        out = values + parts[group].astype(F32)
+        for i in range(3):
+            back[i].wait_recv()
+            out = out + landed[i].astype(F32)
+        h1_out[...] = out
+        for copy in back:
+            copy.wait_send()
+        finish(jobs, place)
+
+    shapes = (
+        jax.ShapeDtypeStruct((sz.rows, sz.width), F32),
+        jax.ShapeDtypeStruct((4, sz.rows, sz.width), BF),
+        jax.ShapeDtypeStruct((rows, sz.qcols), BF),
+        jax.ShapeDtypeStruct((n, rows, 2 * sz.kcols), BF),
+        jax.ShapeDtypeStruct((rows, sz.qcols), F32),
+        jax.ShapeDtypeStruct((sz.per_group, rows, LANES), F32),
+    )
+    arrays = (x_own, gain, bias, watt, *tables, qpos, kpos)
+    specs = [vmem()] * 3 + [hbm()] + [vmem()] * 4
+    scratch = [
+        pltpu.VMEM((sz.width, sz.atot), BF),
+        pltpu.VMEM((4, sz.rows, sz.width), BF),
+        pltpu.VMEM((3, sz.rows, sz.width), BF),
+        DMA,
+        DMA((3,)),
+        DMA((3,)),
+        DMA((n,)),
+        DMA((n,)),
+        DMA((3,)),
+        DMA((3,)),
+    ]
+    return run_call(
+        body,
+        list(zip(arrays, specs)),
+        [(shape, vmem()) for shape in shapes],
+        scratch,
+        jobs,
+        3 + section,
+        "attend_forward",
+    )
+
+
+def attend_back(sz, section, dh1, x_own, gain, watt, tables, qpos, kpos, kept, jobs):
+    n, rows = sz.ctx, 4 * sz.rows
+
+    def body(ins, outs, scratch, jobs):
+        dh1, x_ref, gain, watt, cosine, sine, qpos, kpos, n1_all, q_in, kv_all, o_in, lse_in = ins
+        dx_out, dw_out, gain_grad, bias_grad = outs
+        w, dh_all, dkv, dkv_in, da, parts, landed, w_sem, s_in, r_in, s_kv, r_kv, s_back, r_back = scratch
+        place = where_am_i()
+        x, y, k, z = place
+        load = pltpu.make_async_copy(watt, w, w_sem)
+        load.start()
+        meet_pair(sz, place, jobs)
+        group = 2 * x + y
+        dh_all[group] = dh1[...].astype(BF)
+        copies = gather_pair(dh_all, place, s_in, r_in)
+        begin(jobs, place, 0.0, 0.4)
+        load.wait()
+        gathered_pair(dh_all, place, copies, r_in)
+        dh = dh_all[...].reshape(rows, sz.width)
+        dout = mm(dh, w[:, sz.acols :]).astype(BF)
+        keys = kv_all[:, :, : sz.kcols].reshape(n * rows, sz.kcols)
+        vals = kv_all[:, :, sz.kcols :].reshape(n * rows, sz.kcols)
+        allowed = kpos[...] <= qpos[...]
+        scale = 1.0 / math.sqrt(HEAD_WIDTH_SIZE)
+        cos, sin = cosine[...], sine[...]
+        dkeys, dvals = None, None
+        for head in range(sz.per_group):
+            cols = slice(head * HEAD_WIDTH_SIZE, (head + 1) * HEAD_WIDTH_SIZE)
+            query, grad = q_in[:, cols], dout[:, cols]
+            delta = jnp.sum(grad.astype(F32) * o_in[:, cols], axis=-1, keepdims=True)
+            scores = mm(query, keys, NT) * scale
+            probs = jnp.where(allowed, jnp.exp(scores - lse_in[head][:, :1]), 0.0)
+            dscores = (probs * (mm(grad, vals, NT) - delta)).astype(BF)
+            dquery = (mm(dscores, keys) * scale).astype(BF).astype(F32)
+            da[:, cols] = (dquery * cos - half_turn(dquery) * sin).astype(BF)
+            one_key = mm(dscores, query, TN)
+            one_val = mm(probs.astype(BF), grad, TN)
+            dkeys = one_key if dkeys is None else dkeys + one_key
+            dvals = one_val if dvals is None else dvals + one_val
+        dkv[:, :, : sz.kcols] = (dkeys * scale).astype(BF).reshape(n, rows, sz.kcols)
+        dkv[:, :, sz.kcols :] = dvals.astype(BF).reshape(n, rows, sz.kcols)
+        kv_copies = []
+        for step, device in enumerate(line_peers(n, x, y, k, z)):
+            kv_copies.append(
+                remote(
+                    dkv.at[lax.rem(z + 1 + step, n)],
+                    dkv_in.at[step],
+                    s_kv.at[step],
+                    r_kv.at[step],
+                    device,
+                )
+            )
+            kv_copies[-1].start()
+        begin(jobs, place, 0.4, 1.0)
+        dw_out[:, sz.acols :] = mm(dh, o_in[...].astype(BF), TN).astype(BF)
+        total = dkv[z].astype(F32)
+        for step in range(n - 1):
+            kv_copies[step].wait_recv()
+            total = total + dkv_in[step].astype(F32)
+        dkey = total[:, : sz.kcols]
+        da[:, sz.qcols : sz.qcols + sz.kcols] = (dkey * cos - half_turn(dkey) * sin).astype(BF)
+        da[:, sz.qcols + sz.kcols :] = total[:, sz.kcols :].astype(BF)
+        parts[...] = mm(da[...], w[:, : sz.acols], NT).astype(BF).reshape(4, sz.rows, sz.width)
+        back = scatter_pair(parts, landed, place, s_back, r_back)
+        dw_out[:, : sz.acols] = mm(n1_all[...].reshape(rows, sz.width), da[...], TN).astype(BF)
+        bias_grad[...] = jnp.sum(da[...].astype(F32), axis=0, keepdims=True)
+        middle(jobs, place)
+        for copy in copies + kv_copies:
+            copy.wait_send()
+        dn1 = parts[group].astype(F32)
+        for i in range(3):
+            back[i].wait_recv()
+            dn1 = dn1 + landed[i].astype(F32)
+        values = x_ref[...].astype(F32)
+        inverse = row_norm(values)
+        weighted = dn1 * gain[...]
+        inner = jnp.mean(weighted * values, axis=-1, keepdims=True)
+        dx = dh1[...] + inverse * weighted - values * (inverse * inverse * inverse) * inner
+        dx_out[...] = dx.astype(BF)
+        gain_grad[...] = jnp.sum(dn1 * values * inverse, axis=0, keepdims=True)
+        for copy in back:
+            copy.wait_send()
+        finish(jobs, place)
+
+    shapes = (
+        jax.ShapeDtypeStruct((sz.rows, sz.width), BF),
+        jax.ShapeDtypeStruct((sz.width, sz.atot), BF),
+        jax.ShapeDtypeStruct((1, sz.width), F32),
+        jax.ShapeDtypeStruct((1, sz.acols), F32),
+    )
+    arrays = (dh1, x_own, gain, watt, *tables, qpos, kpos, *kept)
+    specs = [vmem()] * 3 + [hbm()] + [vmem()] * 9
+    scratch = [
+        pltpu.VMEM((sz.width, sz.atot), BF),
+        pltpu.VMEM((4, sz.rows, sz.width), BF),
+        pltpu.VMEM((n, rows, 2 * sz.kcols), BF),
+        pltpu.VMEM((n, rows, 2 * sz.kcols), BF),
+        pltpu.VMEM((rows, sz.acols), BF),
+        pltpu.VMEM((4, sz.rows, sz.width), BF),
+        pltpu.VMEM((3, sz.rows, sz.width), BF),
+        DMA,
+        DMA((3,)),
+        DMA((3,)),
+        DMA((n,)),
+        DMA((n,)),
+        DMA((3,)),
+        DMA((3,)),
+    ]
+    return run_call(
+        body,
+        list(zip(arrays, specs)),
+        [(shape, vmem()) for shape in shapes],
+        scratch,
+        jobs,
+        5 + section,
+        "attend_backward",
+    )
+
+
+class HiddenWeights:
+    def __init__(self, sz, place, sources, w, sems):
+        x, y, k, z = place
+        self.sz, self.sources, self.w, self.sems = sz, sources, w, sems
+        self.more = x * sz.group + (y * 2 + k) * sz.ctx + z < sz.extra
+        self.wide = sz.least * HB
+
+    def copies(self, offset, width, kind):
+        cols = pl.ds(offset, width)
+        return [
+            pltpu.make_async_copy(
+                self.sources[part].at[:, cols], self.w.at[part, :, cols], self.sems.at[kind, part]
+            )
+            for part in range(3)
+        ]
+
+    def start(self):
+        for copy in self.copies(0, self.wide, 0):
+            copy.start()
+        if self.sz.extra:
+
+            @pl.when(self.more)
+            def _():
+                for copy in self.copies(self.wide, HB, 1):
+                    copy.start()
+
+            @pl.when(jnp.logical_not(self.more))
+            def _():
+                self.w[:, :, self.wide :] = jnp.zeros((3, self.sz.width, HB), BF)
+
+    def wait(self):
+        for copy in self.copies(0, self.wide, 0):
+            copy.wait()
+        if self.sz.extra:
+
+            @pl.when(self.more)
+            def _():
+                for copy in self.copies(self.wide, HB, 1):
+                    copy.wait()
+
+
+def meet_tree(sz, place, jobs):
+    x, y, k, z = place
+    peers = tree_peers(sz.ctx, x, y, k, z)
+    meet(sz, place, peers, peers[:1], jobs)
+
+
+def feed(sz, section, h1, gain, weights, jobs):
+    n = sz.ctx
+
+    def body(ins, outs, scratch, jobs):
+        h1, gain, *sources = ins
+        act_out, n2_all, gate_out, up_out, hm_out = outs
+        w, w_sems, *refs = scratch
+        place = where_am_i()
+        x, y, k, z = place
+        hidden_weights = HiddenWeights(sz, place, sources, w, w_sems)
+        hidden_weights.start()
+        meet_tree(sz, place, jobs)
+        gather = Gather(n, sz.rows, n2_all, place, refs[:12])
+        scatter = Scatter(n, sz.rows, place, refs[12:])
+        values = h1[...]
+        n2_all[k, gather.groups[0], z] = (values * row_norm(values) * gain[...]).astype(BF)
+        gather.begin()
+        begin(jobs[:1], place)
+        begin(jobs[1:], place, 0.0, 0.75)
+        hidden_weights.wait()
+        rows = n * sz.rows
+
+        def column(core, which):
+            group = gather.groups[which]
+            normed = n2_all[core, group].reshape(rows, sz.width)
+            gate = mm(normed, w[0])
+            up = mm(normed, w[1])
+            hidden = (gate * jax.nn.sigmoid(gate) * up).astype(BF)
+            gate_out[core, group] = gate.astype(BF)
+            up_out[core, group] = up.astype(BF)
+            hm_out[core, group] = hidden
+            scatter.parts[core, group] = (
+                mm(hidden, w[2], NT).astype(BF).reshape(n, sz.rows, sz.width)
+            )
+            if core is not k:
+                scatter.core(which).start()
+
+        gather.run(column, scatter.early)
+
+        def later():
+            begin(jobs[1:], place, 0.75, 1.0)
+            middle(jobs, place)
+
+        result = scatter.run((later,))
+        act_out[...] = (values + result).astype(BF)
+        gather.finish()
+        scatter.finish()
+        finish(jobs, place)
+
+    kept = jax.ShapeDtypeStruct((2, 4, n * sz.rows, sz.hidden), BF)
+    shapes = (
+        jax.ShapeDtypeStruct((sz.rows, sz.width), BF),
+        jax.ShapeDtypeStruct((2, 4, n, sz.rows, sz.width), BF),
+        kept,
+        kept,
+        kept,
+    )
+    scratch = (
+        [pltpu.VMEM((3, sz.width, sz.hidden), BF), DMA((2, 3))]
+        + Gather.scratch(n)
+        + Scatter.scratch(n, sz.rows, sz.width)
+    )
+    return run_call(
+        body,
+        [(h1, vmem()), (gain, vmem())] + [(w, hbm()) for w in weights],
+        [(shape, vmem()) for shape in shapes],
+        scratch,
+        jobs,
+        7 + section,
+        "feed_forward",
+    )
+
+
+def feed_back(sz, section, dy, h1, gain, weights, kept, jobs):
+    n = sz.ctx
+
+    def body(ins, outs, scratch, jobs):
+        dy, h1, gain, *sources = ins[:6]
+        n2_all, gate_in, up_in, hm_in = ins[6:]
+        dh1_out, dw_out, gain_grad = outs
+        w, dy_all, dgate_all, dup_all, w_sems, *refs = scratch
+        place = where_am_i()
+        x, y, k, z = place
+        hidden_weights = HiddenWeights(sz, place, sources, w, w_sems)
+        hidden_weights.start()
+        meet_tree(sz, place, jobs)
+        gather = Gather(n, sz.rows, dy_all, place, refs[:12])
+        scatter = Scatter(n, sz.rows, place, refs[12:])
+        dy_all[k, gather.groups[0], z] = dy[...]
+        gather.begin()
+        begin(jobs[:1], place)
+        hidden_weights.wait()
+        middle(jobs, place)
+        begin(jobs[1:], place)
+        rows = n * sz.rows
+
+        def column(core, which):
+            group = gather.groups[which]
+            dhidden = mm(dy_all[core, group].reshape(rows, sz.width), w[2])
+            gate = gate_in[core, group].astype(F32)
+            up = up_in[core, group].astype(F32)
+            sigmoid = jax.nn.sigmoid(gate)
+            dgate = (dhidden * up * sigmoid * (1.0 + gate * (1.0 - sigmoid))).astype(BF)
+            dup = (dhidden * gate * sigmoid).astype(BF)
+            dgate_all[core, group] = dgate
+            dup_all[core, group] = dup
+            partial = mm(dgate, w[0], NT) + mm(dup, w[1], NT)
+            scatter.parts[core, group] = partial.astype(BF).reshape(n, sz.rows, sz.width)
+            if core is not k:
+                scatter.core(which).start()
+
+        gather.run(column, scatter.early)
+        total = 8 * rows
+        tile = 256 if sz.width % 256 == 0 else 128
+
+        def weight_grad(slot, left, right):
+            grads = right[...].reshape(total, sz.hidden)
+
+            @pl.loop(0, sz.width // tile)
+            def _(step):
+                cols = pl.ds(pl.multiple_of(step * tile, tile), tile)
+                side = left[:, :, :, :, cols].reshape(total, tile)
+                dw_out[slot, cols] = mm(side, grads, TN).astype(BF)
+
+        dn2 = scatter.run(
+            (
+                lambda: weight_grad(0, n2_all, dgate_all),
+                lambda: weight_grad(1, n2_all, dup_all),
+                lambda: weight_grad(2, dy_all, hm_in),
+            )
+        )
+        values = h1[...]
+        inverse = row_norm(values)
+        weighted = dn2 * gain[...]
+        inner = jnp.mean(weighted * values, axis=-1, keepdims=True)
+        dh1_out[...] = (
+            dy[...].astype(F32) + inverse * weighted - values * (inverse * inverse * inverse) * inner
+        )
+        gain_grad[...] = jnp.sum(dn2 * values * inverse, axis=0, keepdims=True)
+        gather.finish()
+        scatter.finish()
+        finish(jobs, place)
+
+    shapes = (
+        jax.ShapeDtypeStruct((sz.rows, sz.width), F32),
+        jax.ShapeDtypeStruct((3, sz.width, sz.hidden), BF),
+        jax.ShapeDtypeStruct((1, sz.width), F32),
+    )
+    inner = pltpu.VMEM((2, 4, n * sz.rows, sz.hidden), BF)
+    scratch = (
+        [
+            pltpu.VMEM((3, sz.width, sz.hidden), BF),
+            pltpu.VMEM((2, 4, n, sz.rows, sz.width), BF),
+            inner,
+            inner,
+            DMA((2, 3)),
+        ]
+        + Gather.scratch(n)
+        + Scatter.scratch(n, sz.rows, sz.width)
+    )
+    arrays = (dy, h1, gain, *weights, *kept)
+    specs = [vmem()] * 3 + [hbm()] * 3 + [vmem()] * 4
+    return run_call(
+        body,
+        list(zip(arrays, specs)),
+        [(shape, vmem()) for shape in shapes],
+        scratch,
+        jobs,
+        9 + section,
+        "feed_backward",
+    )
+
+
+def collect(sz, small, acts, grads, jobs):
+    n = sz.ctx
+
+    def body(ins, outs, scratch, jobs):
+        small, act0, act1, grad0, grad1 = ins
+        small_in, act_out, grad_out = outs
+        s_small, r_small, s_out, r_out = scratch
+        place = where_am_i()
+        x, y, k, z = place
+        me = x * sz.group + (y * 2 + k) * n + z
+        meet(sz, place, [], [], jobs)
+        begin(jobs, place)
+
+        @pl.loop(1, sz.total)
+        def _(step):
+            device = lax.rem(me + step, sz.total)
+            remote(
+                small.at[device], small_in.at[me], s_small, r_small, flat_place(device, sz.group, n)
+            ).start()
+
+        pltpu.make_async_copy(small.at[me], small_in.at[me], s_small).start()
+
+        def results(starting):
+            for section in range(2):
+                for slot, (source, target) in enumerate(
+                    (((act0, act1)[section], act_out), ((grad0, grad1)[section], grad_out))
+                ):
+                    own = jnp.logical_and(x == section, jnp.logical_and(x == y, y == k))
+
+                    @pl.when(jnp.logical_not(own))
+                    def _():
+                        copy = remote(
+                            source,
+                            target.at[k],
+                            s_out.at[section, slot],
+                            r_out.at[slot, k],
+                            at(section, x, y, z),
+                        )
+                        copy.start() if starting else copy.wait_send()
+
+                    if starting:
+
+                        @pl.when(own)
+                        def _():
+                            pltpu.make_async_copy(source, target.at[k], r_out.at[slot, k]).start()
+
+        middle(jobs, place)
+        results(True)
+        results(False)
+        for slot, target in enumerate((act_out, grad_out)):
+            for batch in range(2):
+                arrived(target.at[batch], r_out.at[slot, batch])
+        arrived(small_in.at[pl.ds(0, sz.total - 1)], r_small)
+        arrived(small_in, s_small)
+        finish(jobs, place)
+
+    shapes = (
+        jax.ShapeDtypeStruct((sz.total, 8, LANES), F32),
+        jax.ShapeDtypeStruct((2, sz.rows, sz.width), BF),
+        jax.ShapeDtypeStruct((2, sz.rows, sz.width), BF),
+    )
+    return run_call(
+        body,
+        [(array, hbm()) for array in (small, *acts, *grads)],
+        [(shape, hbm()) for shape in shapes],
+        [DMA, DMA, DMA((2, 2)), DMA((2, 2))],
+        jobs,
+        2,
+        "collect_gradients",
+    )
+
+
+def local_columns(
+    sz,
+    tokens,
+    positions,
+    norm1_gain,
+    qkv_bias,
+    qkv_weight,
+    out_weight,
+    norm2_gain,
+    gate_up_weight,
+    down_weight,
+    cotangent,
+):
+    n, group = sz.ctx, sz.group
+    x, y, k, z = where_am_i()
+    mine = 2 * x + y
+    bias_owned = qkv_bias.shape[1]
+    qkv_weight, out_weight = (qkv_weight[0], out_weight[0])
+    gate_up_weight, down_weight = (gate_up_weight[0], down_weight[0])
+
+    def line(values):
+        return jnp.pad(values, ((0, 0), (0, LANES - values.shape[1])))
+
+    small = jnp.concatenate(
+        [line(norm1_gain), line(norm2_gain), line(qkv_bias), jnp.zeros((13, LANES), BF)], axis=0
+    )
+    (small_all, tok_own, cot_own, heads_x, cols_x), ((att0,), (gate0,)) = spread(
+        sz, small, tokens, cotangent, qkv_weight, out_weight, gate_up_weight, down_weight
+    )
+    per_section = small_all.reshape(2, group, 16, LANES).astype(F32)
+    gain1 = per_section[:, :, 0, : sz.owned].reshape(2, 1, sz.width)
+    gain2 = per_section[:, :, 1, : sz.owned].reshape(2, 1, sz.width)
+    bias = per_section[:, :, 2, :bias_owned].reshape(2, 1, group * bias_owned)
+    query_columns = QUERY_HEADS * HEAD_WIDTH_SIZE
+    key_columns = KEY_VALUE_HEADS * HEAD_WIDTH_SIZE
+    kv = mine // (4 // KEY_VALUE_HEADS)
+    starts = (
+        (mine * sz.qcols, sz.qcols),
+        (query_columns + kv * sz.kcols, sz.kcols),
+        (query_columns + key_columns + kv * sz.kcols, sz.kcols),
+    )
+    own_bias = jnp.concatenate(
+        [lax.dynamic_slice_in_dim(bias, start, size, 2) for start, size in starts], axis=2
+    )
+    ordered = lax.dynamic_index_in_dim(positions, k, 0, keepdims=False)
+    ordered = ordered.reshape(4, n, sz.rows).transpose(1, 0, 2)
+    own_pos = lax.dynamic_index_in_dim(ordered, z, 0, keepdims=False).reshape(4 * sz.rows)
+    kpos = ordered.reshape(1, sz.seq)
+    qpos = own_pos[:, None]
+    cosine, sine = rope_tables(own_pos, HEAD_WIDTH_SIZE)
+    half = HEAD_WIDTH_SIZE // 2
+    sign = jnp.where(jnp.arange(HEAD_WIDTH_SIZE) < half, -1.0, 1.0)
+    tables = (cosine[:, 0], sine[:, 0] * sign)
+
+    def columns(section, part):
+        return Columns(sz, section, part, gate_up_weight, down_weight, cols_x)
+
+    att, gates, weights = [att0, None], [gate0, None], []
+    inputs, acts, kept_att, kept_feed, middles = [tok_own], [], [], [], []
+    for section in range(2):
+        (h1, *kept), ((up,), (down,)) = attend(
+            sz,
+            section,
+            inputs[section],
+            gain1[section],
+            own_bias[section],
+            att[section],
+            tables,
+            qpos,
+            kpos,
+            [columns(section, 1), columns(section, 2)],
+        )
+        kept_att.append(kept)
+        middles.append(h1)
+        weights.append((gates[section], up, down))
+        jobs = []
+        if section == 0:
+            jobs = [Heads(sz, 1, qkv_weight, out_weight, heads_x), columns(1, 0)]
+        (act, *kept), more = feed(sz, section, h1, gain2[section], weights[section], jobs)
+        if section == 0:
+            (att[1],), (gates[1],) = more
+        kept_feed.append(kept)
+        acts.append(act)
+        inputs.append(act)
+    grads, das, smalls = [None, None], [None, None], [None, None]
+    came = [[None] * 3, [None] * 3]
+    came_heads = [None, None]
+    dy = cot_own
+    for section in (1, 0):
+        jobs = []
+        if section == 0:
+            jobs = [ReturnedHeads(sz, 1, das[1]), Returned(sz, 1, (2,), dw)]
+        (dh1, dw, gain2_grad), more = feed_back(
+            sz, section, dy, middles[section], gain2[section], weights[section], kept_feed[section], jobs
+        )
+        if section == 0:
+            (came_heads[1],), (came[1][2],) = more
+        (dy, das[section], gain1_grad, bias_grad), (returned,) = attend_back(
+            sz,
+            section,
+            dh1,
+            inputs[section],
+            gain1[section],
+            att[section],
+            tables,
+            qpos,
+            kpos,
+            kept_att[section],
+            [Returned(sz, section, (0, 1) if section else (0, 1, 2), dw)],
+        )
+        for part, grad in enumerate(returned):
+            came[section][part] = grad
+        grads[section] = dy
+        whole_bias = jnp.zeros((1, query_columns + 2 * key_columns), F32)
+        offset = 0
+        for start, size in starts:
+            whole_bias = lax.dynamic_update_slice(
+                whole_bias, bias_grad[:, offset : offset + size], (0, start)
+            )
+            offset += size
+        split = query_columns + key_columns
+        rows = [gain1_grad, gain2_grad, whole_bias[:, :split], whole_bias[:, split:]]
+        rows = [line(row.reshape(group, -1))[:, None] for row in rows]
+        smalls[section] = jnp.concatenate(rows + [jnp.zeros((group, 4, LANES), F32)], axis=1)
+    small_out = jnp.concatenate(smalls, axis=0)
+    (small_in, act_out, grad_out), ((came_heads[0],),) = collect(
+        sz, small_out, acts, grads, [ReturnedHeads(sz, 0, das[0])]
+    )
+
+    def own(parts):
+        return jnp.where(x == 0, parts[0], parts[1])
+
+    small_sum = jnp.sum(small_in, axis=0)
+    gate_up_grad = jnp.concatenate(
+        [own((came[0][part], came[1][part])).astype(F32) for part in range(2)], axis=1
+    )[None]
+    down_grad = own((came[0][2], came[1][2])).astype(F32)[None]
+    att_in = own(came_heads)
+    att_sum = jnp.sum(att_in.astype(F32).reshape(4, n, sz.owned, sz.atot), axis=1)
+    q_grad = att_sum[:, :, : sz.qcols].transpose(1, 0, 2).reshape(sz.owned, query_columns)
+    kv_grad = jnp.sum(
+        att_sum[:, :, sz.qcols : sz.acols].reshape(
+            KEY_VALUE_HEADS, 4 // KEY_VALUE_HEADS, sz.owned, 2, sz.kcols
+        ),
+        axis=1,
+    )
+    kv_grad = kv_grad.transpose(1, 2, 0, 3).reshape(sz.owned, 2 * key_columns)
+    qkv_grad = jnp.concatenate([q_grad, kv_grad], axis=1)[None]
+    out_grad = att_sum[:, :, sz.acols :].transpose(1, 0, 2).reshape(1, sz.owned, query_columns)
+    return (
+        act_out[None],
+        grad_out[None],
+        small_sum[0:1, : sz.owned],
+        small_sum[2:3, : (query_columns + key_columns) // group],
+        small_sum[3:4, : key_columns // group],
+        qkv_grad,
+        out_grad,
+        small_sum[1:2, : sz.owned],
+        gate_up_grad,
+        down_grad,
+    )
+
+
 def solution(mesh):
     placed = (
         P(None, ("head", "ctx"), None),
@@ -491,21 +2227,24 @@
         P("section", ("head", "ctx"), None),
         P(None, ("head", "ctx"), None),
     )
-    return jax.shard_map(
-        local,
-        mesh=mesh,
-        in_specs=placed,
-        out_specs=(
-            P("section", None, ("head", "ctx"), None),
-            P("section", None, ("head", "ctx"), None),
-            P("section", ("head", "ctx")),
-            P("section", ("head", "ctx")),
-            P("section", ("head", "ctx")),
-            P("section", ("head", "ctx"), None),
-            P("section", ("head", "ctx"), None),
-            P("section", ("head", "ctx")),
-            P("section", ("head", "ctx"), None),
-            P("section", ("head", "ctx"), None),
-        ),
-        check_vma=False,
-    )
+    returned = (
+        P("section", None, ("head", "ctx"), None),
+        P("section", None, ("head", "ctx"), None),
+        P("section", ("head", "ctx")),
+        P("section", ("head", "ctx")),
+        P("section", ("head", "ctx")),
+        P("section", ("head", "ctx"), None),
+        P("section", ("head", "ctx"), None),
+        P("section", ("head", "ctx")),
+        P("section", ("head", "ctx"), None),
+        P("section", ("head", "ctx"), None),
+    )
+
+    def program(*arrays):
+        sizes = Sizes(mesh, arrays[0], arrays[4], arrays[7], arrays[8])
+        body = functools.partial(local_columns, sizes) if sizes.fits() else local
+        return jax.shard_map(
+            body, mesh=mesh, in_specs=placed, out_specs=returned, check_vma=False
+        )(*arrays)
+
+    return program

time: 3070 us -> 914 us (0.30)
  waiting for transfers between devices: 2450 us -> 0 us
  Pallas kernels: 0 us -> 876 us
  matrix products: 316 us -> 0 us
  blocking collectives: 80 us -> 0 us
  starting transfers between devices: 63.3 us -> 0 us
  local copies, waits for them, and re-layouts: 65.6 us -> 13.6 us
  other arithmetic: 62.2 us -> 13.2 us
    reduce_scatter x10 -> x0, waiting for transfers between devices: 1850 us -> none  [the longest x8 1840 us: reduce_block(): lax.psum_scatter(block_term, ('head', 'ctx'), scatter_dimension=0, tiled=...]
    pallas_call x0 -> x10, Pallas kernels: none -> 876 us  [run_call(): pl.pallas_call(kernel, out_shape=tuple((shape for shape, _ in outs)), in_...]
    all_gather x7 -> x0, waiting for transfers between devices: 457 us -> none  [the longest x1 282 us: local(): lax.all_gather(shards[5], ('head', 'ctx'), axis=1, tiled=True)]
    dot_general x37 -> x0, matrix products: 316 us -> none  [the longest x8 85.4 us: reduce_block(): jnp.einsum('rd,rc->dc', left_side, columns, preferred_element_type=jnp.fl...]
    unnamed x25 -> x0, waiting for transfers between devices: 92 us -> none
    all_to_all x10 -> x0, starting transfers between devices: 47.4 us -> none  [the longest x2 10.5 us: layer_backward(): lax.all_to_all(out_grad_rows, 'head', split_axis=2, concat_axis=1, tiled=...]
    unnamed x1 -> x0, blocking collectives: 35.5 us -> none
    all_to_all x10 -> x0, waiting for transfers between devices: 32.7 us -> none  [the longest x2 10.2 us: layer_backward(): lax.all_to_all(query_send, 'head', split_axis=1, concat_axis=2, tiled=True)]
  transfers between devices with their start and end apart: 33 -> 0, of which waited for: 26 -> 0; matrix products, arithmetic and copies ran while one was open for 11% -> 0% of each run, Pallas kernels for 0% -> 0%
where the time goes in v2:
time: 914 us; the launch traced here: 904 us
  Pallas kernels  876 us (96%)
  local copies, waits for them, and re-layouts  13.6 us (1%)
  other arithmetic  13.2 us (1%)
    pallas_call x10, Pallas kernels, run_call(): pl.pallas_call(kernel, out_shape=tuple((shape for shape, _ in outs)), in_...  876 us

profile of v2, /device:TPU:14, one launch (start us, length us, event | category | flops | bytes accessed | tf_op | source)
XLA Modules:
  0.0 903.9 jit_solution(10974534074620741632)
XLA Ops:
  0.7 0.1 pad.58.clone
  0.8 1.4 fusion.7.refs_0_
  2.1 73.8 %spread_weights.1 = (bf16[32,16,128]{2,1,0:T(8,128)(2,1)}, bf16[64,1536]{1,0:T(8,128)(2,1)}, bf16[64,1536]{1,0:T(8,128)(2,1)}, bf16[2,96,1024]{2,1,0:T(8,128)(2,...) custom-call(bf16[16,128]{1,0:T(8,128)(2,1)} %fusion.7.refs_0_, ...), custom_call_target="tpu_custom_call" | custom-call | tf_op jit(solution)/shard_map/spread_weights/pallas_call | solution.py:673
  75.9 0.9 bitcast_convert_fusion.1
  77.0 0.6 slice_bitcast_fusion.2
  77.6 0.1 reshape.107
  77.7 0.1 convert_element_type.44
  77.8 0.1 broadcast_multiply_fusion
  78.0 1.2 sine_multiply_fusion
  79.2 0.8 reshape.129.refs_6_
  80.0 0.7 reshape.109.refs_7_
  80.7 0.7 squeeze.42.refs_1_.refs_2_
  81.4 57.0 %attend_forward.2 = (f32[64,1536]{1,0:T(8,128)}, bf16[4,64,1536]{2,1,0:T(8,128)(2,1)}, bf16[256,384]{1,0:T(8,128)(2,1)}, bf16[4,256,256]{2,1,0:T(8,128)(2,1)}, f...) custom-call(bf16[64,1536]{1,0:T(8,128)(2,1)} %get-tuple-element.71.refs_0_.re, ...), custom_call_target="tpu_custom_call" | custom-call | tf_op jit(solution)/shard_map/attend_forward/pallas_call | solution.py:673
  138.4 0.7 squeeze.44.refs_1_.refs_2_
  139.1 111.0 %feed_forward.2 = (bf16[64,1536]{1,0:T(8,128)(2,1)}, bf16[2,4,4,64,1536]{4,3,2,1,0:T(8,128)(2,1)}, bf16[2,4,256,384]{3,2,1,0:T(8,128)(2,1)}, bf16[2,4,256,384]{3...) custom-call(f32[64,1536]{1,0:T(8,128)} %get-tuple-element.75.refs_0_.r, ...), custom_call_target="tpu_custom_call" | custom-call | tf_op jit(solution)/shard_map/feed_forward/pallas_call | solution.py:673
  250.1 0.7 squeeze.45.refs_1_.refs_2_
  250.8 64.2 %attend_forward.3 = (f32[64,1536]{1,0:T(8,128)}, bf16[4,64,1536]{2,1,0:T(8,128)(2,1)}, bf16[256,384]{1,0:T(8,128)(2,1)}, bf16[4,256,256]{2,1,0:T(8,128)(2,1)}, f...) custom-call(bf16[64,1536]{1,0:T(8,128)(2,1)} %get-tuple-element.80.refs_0_.re, ...), custom_call_target="tpu_custom_call" | custom-call | tf_op jit(solution)/shard_map/attend_forward/pallas_call | solution.py:673
  315.0 0.7 squeeze.47.refs_1_.refs_2_
  315.6 87.0 %feed_forward.3 = (bf16[64,1536]{1,0:T(8,128)(2,1)}, bf16[2,4,4,64,1536]{4,3,2,1,0:T(8,128)(2,1)}, bf16[2,4,256,384]{3,2,1,0:T(8,128)(2,1)}, bf16[2,4,256,384]{3,2,1,0:T(8,128)(2,1)}, bf16[2,4,256,384]{3,2,1,0:T(8,128)(2,1)}) custom-call(f32[64,1536]{1,0:T(8,128)} %get-tuple-element.82.refs_0_.refs_1_, f32[1,1536]{1,0:T(1,128)} %squeeze.47.refs_1_.refs_2_, ...), custom_call_target="tpu_custom_call" | custom-call | tf_op jit(solution)/shard_map/feed_forward/pallas_call | solution.py:673
  402.7 90.5 %feed_backward.2 = (f32[64,1536]{1,0:T(8,128)}, bf16[3,1536,384]{2,1,0:T(8,128)(2,1)}, f32[1,1536]{1,0:T(1,128)}) custom-call(bf16[64,1536]{1,0:T(8,128)(2,1)} %get-tuple-element.70.refs_0_, f32[64,1536]{1,0:T(8,128)} %get-tuple-element.82.refs_0_.refs_1_, f32[1,1536]{1,0:T(1,128)} %squeeze.47.refs_1_.refs_2_, ...), custom_call_target="tpu_custom_call" | custom-call | tf_op jit(solution)/shard_map/feed_backward/pallas_call | solution.py:673
  493.2 76.5 %attend_backward.2 = (bf16[64,1536]{1,0:T(8,128)(2,1)}, bf16[1536,1024]{1,0:T(8,128)(2,1)}, f32[1,1536]{1,0:T(1,128)}, f32[1,640]{1,0:T(1,128)}, bf16[96,8960]{1,0:T(8,128)(2,1)}, /*index=5*/bf16[96,8960]{1,0:T(8,128)(2,1)}) custom-call(f32[64,1536]{1,0:T(8,128)} %get-tuple-element.90.refs_0_, bf16[64,1536]{1,0:T(8,128)(2,1)} %get-tuple-element.80.refs_0_.refs_1_, ...), custom_call_target="tpu_custom_call" | custom-call | tf_op jit(solution)/shard_map/attend_backward/pallas_call | solution.py:673
  569.7 152.7 %feed_backward.3 = (f32[64,1536]{1,0:T(8,128)}, bf16[3,1536,384]{2,1,0:T(8,128)(2,1)}, f32[1,1536]{1,0:T(1,128)}, bf16[16,96,1024]{2,1,0:T(8,128)(2,1)}, bf16[96,8960]{1,0:T(8,128)(2,1)}) custom-call(bf16[64,1536]{1,0:T(8,128)(2,1)} %get-tuple-element.97.refs_0_.refs_4_, f32[64,1536]{1,0:T(8,128)} %get-tuple-element.75.refs_0_.refs_1_, ...), custom_call_target="tpu_custom_call" | custom-call | tf_op jit(solution)/shard_map/feed_backward/pallas_call | solution.py:673
  722.4 82.8 %attend_backward.3 = (bf16[64,1536]{1,0:T(8,128)(2,1)}, bf16[1536,1024]{1,0:T(8,128)(2,1)}, f32[1,1536]{1,0:T(1,128)}, f32[1,640]{1,0:T(1,128)}, bf16[96,8960]{1...) custom-call(f32[64,1536]{1,0:T(8,128)} %get-tuple-element.103.refs_0_, ...), custom_call_target="tpu_custom_call" | custom-call | tf_op jit(solution)/shard_map/attend_backward/pallas_call | solution.py:673
  805.3 2.0 bitcast_convert_fusion
  807.3 1.2 copy-done.4
  808.4 0.5 copy-done.6
  809.0 0.5 copy-done.7
  809.5 0.3 broadcast_select_fusion.1
  809.9 3.5 fusion
  813.6 0.1 reshape.113
  814.0 0.1 reshape.117
  814.5 0.1 concatenate.29
  814.6 0.7 pad_maximum_fusion.1.refs_0_
  815.2 80.2 %collect_gradients.1 = (f32[32,8,128]{2,1,0:T(8,128)}, bf16[2,64,1536]{2,1,0:T(8,128)(2,1)}, bf16[2,64,1536]{2,1,0:T(8,128)(2,1)}, bf16[16,96,1024]{2,1,0:T(8,128)(2,1)}) custom-call(f32[32,8,128]{2,1,0:T(8,128)} %pad_maximum_fusion.1.refs_0_, bf16[64,1536]{1,0:T(8,128)(2,1)} %get-tuple-element.80.refs_0_.refs_1_, ...), custom_call_target="tpu_custom_call" | custom-call | tf_op jit(solution)/shard_map/collect_gradients/pallas_call | solution.py:673
  895.5 1.7 convert_reduce_fusion
  897.1 0.1 slice_bitcast_fusion
  897.3 0.2 reshape.121
  897.5 0.3 reduce_sum.29
  897.9 0.2 copy.54
  898.0 0.2 reshape.122
  898.2 0.9 maximum_bitcast_fusion.1
  899.2 0.4 copy.55
  899.5 1.1 reshape.123
  900.6 0.5 fusion.10
  901.2 0.5 slice.104
  901.7 0.5 slice.105
  902.2 0.7 copy.81
  902.9 0.7 copy.82
  (78 shorter events, 1.2 us)
Async XLA Ops:
  0.6 77.0 %copy-start = (s32[2,1024]{1,0:T(2,128)S(1)}, s32[2,1024]{1,0:T(2,128)}, u32[]{:S(2)}) copy-start(s32[2,1024]{1,0:T(2,128)} %param.11) | copy-start | bytes 24580
  722.4 82.8 %copy-start.5 = (bf16[96,8960]{1,0:T(8,128)(2,1)S(1)}, bf16[96,8960]{1,0:T(8,128)(2,1)}, u32[]{:S(2)}) copy-start(bf16[96,8960]{1,0:T(8,128)(2,1)} %get-tuple-element.129) | copy-start | bytes 5160964
  805.2 2.0 copy-start.3
  805.2 3.2 copy-start.4
  805.2 3.7 copy-start.6
  805.3 4.2 copy-start.7
  809.8 3.6 copy-start.16
  809.8 3.7 copy-start.15
  809.8 3.9 copy-start.14
  809.9 4.0 copy-start.13
  809.9 4.4 copy-start.12
  809.9 4.5 copy-start.11
  815.2 80.2 %copy-start.2 = (bf16[16,96,1024]{2,1,0:T(8,128)(2,1)S(1)}, bf16[16,96,1024]{2,1,0:T(8,128)(2,1)}, u32[]{:S(2)}) copy-start(bf16[16,96,1024]{2,1,0:T(8,128)(2,1)} %get-tuple-element.123) | copy-start | bytes 9437188
  898.2 2.4 copy-start.10
  898.2 4.0 copy-start.9
  899.2 3.8 copy-start.8
  899.2 4.5 copy-start.1

commit v3 on v2

--- a/solution.py
+++ b/solution.py
@@ -567,9 +567,10 @@
         self.ff = down.shape[2]
         self.owned = self.width // self.group
         self.blocks = self.ff // HB
-        self.most = -(-self.blocks // self.total)
-        self.least = self.blocks // self.total
-        self.extra = self.blocks % self.total
+        self.plane = self.blocks // 2
+        self.most = -(-self.plane // self.group)
+        self.least = self.plane // self.group
+        self.extra = self.plane % self.group
         self.hidden = self.most * HB
         self.per_group = QUERY_HEADS // 4
         self.qcols = self.per_group * HEAD_WIDTH_SIZE
@@ -582,7 +583,8 @@
         return (
             self.batches == 2
             and gathered * 3 < VMEM_LIMIT // 2
-            and self.ff % HB == 0
+            and self.ff % (2 * HB) == 0
+            and self.ctx % 2 == 0
             and self.least >= 1
             and self.owned % 16 == 0
             and self.rows % 32 == 0
@@ -594,14 +596,29 @@
     return (index // group, inside // ctx, lax.rem(inside, ctx))
 
 
+def block_rank(sz, inside):
+    head, z = (inside // sz.ctx, lax.rem(inside, sz.ctx))
+    y, k = (head // 2, lax.rem(head, 2))
+    turn = jnp.where(z < sz.ctx // 2, 2 * z, 2 * (sz.ctx - 1 - z) + 1)
+    return turn + sz.ctx * (2 * k + lax.rem(y + z, 2))
+
+
 def first_column(sz, owner):
-    return pl.multiple_of((owner * sz.least + jnp.minimum(owner, sz.extra)) * HB, HB)
-
-
-def plane_blocks(sz, plane):
-    start = plane * sz.group * sz.least + min(plane * sz.group, sz.extra)
-    stop = (plane + 1) * sz.group * sz.least + min((plane + 1) * sz.group, sz.extra)
-    return (start, stop - start)
+    rank = block_rank(sz, lax.rem(owner, sz.group))
+    plane = owner // sz.group * sz.plane
+    return pl.multiple_of((plane + rank * sz.least + jnp.minimum(rank, sz.extra)) * HB, HB)
+
+
+def has_more(sz, owner):
+    return block_rank(sz, lax.rem(owner, sz.group)) < sz.extra
+
+
+def extras_of_head(sz, head):
+    count = 0
+    for z in range(sz.ctx):
+        turn = 2 * z if z < sz.ctx // 2 else 2 * (sz.ctx - 1 - z) + 1
+        count += turn + sz.ctx * (2 * (head % 2) + (head // 2 + z) % 2) < sz.extra
+    return count
 
 
 def half_turn(values):
@@ -732,7 +749,7 @@
             if own:
                 first = pl.multiple_of(base + first_column(sz, owner) + offset, HB)
                 return (self.source.at[:, pl.ds(first, width)], target)
-            first = first_column(sz, owner) - first_column(sz, x * sz.group) + offset
+            first = first_column(sz, owner) - x * sz.plane * HB + offset
             first = pl.multiple_of(first, HB)
             return (self.staged.at[self.part, :, pl.ds(first, width)], target)
 
@@ -748,7 +765,7 @@
                     remote(source, target, self.send.at[0], self.recv.at[0], device).start()
                     if sz.extra:
 
-                        @pl.when(owner < sz.extra)
+                        @pl.when(has_more(sz, owner))
                         def _():
                             source, target = pair(owner, wide, HB, own)
                             remote(source, target, self.send.at[1], self.recv.at[1], device).start()
@@ -759,7 +776,7 @@
                 pltpu.make_async_copy(source, target, self.send.at[0]).start()
                 if sz.extra:
 
-                    @pl.when(me < sz.extra)
+                    @pl.when(has_more(sz, me))
                     def _():
                         source, target = pair(me, wide, HB, own)
                         pltpu.make_async_copy(source, target, self.send.at[1]).start()
@@ -774,20 +791,14 @@
         wide = sz.least * HB
         arrived(self.target.at[pl.ds(0, sz.width - sz.owned), pl.ds(0, wide)], self.recv.at[0])
         arrived(self.target.at[:, pl.ds(0, wide)], self.send.at[0])
-        for plane in range(2):
-            count = min(max(sz.extra - plane * sz.group, 0), sz.group)
-            if count:
-
-                @pl.when(x == plane)
-                def _():
-                    arrived(self.target.at[pl.ds(0, count * sz.owned), pl.ds(0, HB)], self.send.at[1])
-
-                    @pl.when(me < sz.extra)
-                    def _():
-                        arrived(
-                            self.target.at[pl.ds(0, sz.width - sz.owned), pl.ds(0, HB)],
-                            self.recv.at[1],
-                        )
+        if sz.extra:
+            arrived(self.target.at[pl.ds(0, sz.extra * sz.owned), pl.ds(0, HB)], self.send.at[1])
+
+            @pl.when(has_more(sz, me))
+            def _():
+                arrived(
+                    self.target.at[pl.ds(0, sz.width - sz.owned), pl.ds(0, HB)], self.recv.at[1]
+                )
 
 
 def head_columns(sz, g, qkv, out_w):
@@ -869,123 +880,207 @@
             arrived(span, self.s_core.at[part])
 
 
-class Returned:
-    reach = 2
-
-    def __init__(self, sz, section, parts, grads):
-        self.sz, self.section, self.parts = sz, section, parts
-        self.ins = [(grads, None)]
-        self.outs = [jax.ShapeDtypeStruct((sz.owned, sz.ff), BF) for _ in parts]
-        self.scratch = [DMA((2, len(parts))), DMA((2, len(parts)))]
+class LineShares:
+    reach = 0
+
+    def __init__(self, sz, part, grads=None):
+        self.sz, self.part = sz, part
+        self.ins = [] if grads is None else [(grads, None)]
+        self.outs = [jax.ShapeDtypeStruct((sz.ctx, 4, sz.owned, sz.hidden), BF)]
+        self.scratch = [DMA((2, sz.ctx)), DMA((2, sz.ctx))]
 
     def bind(self, ins, outs, scratch):
-        self.source, self.targets = ins[0], outs
+        if ins:
+            self.source = ins[0]
+        self.target = outs[0]
         self.send, self.recv = scratch
 
-    def begin(self, place, low=0.0, high=1.0):
+    def moves(self, place, step, offset, width):
+        sz = self.sz
+        x, y, k, z = place
+        ctx = lax.rem(z + step, sz.ctx)
+        for head in range(4):
+            rows = pl.ds(pl.multiple_of((head * sz.ctx + ctx) * sz.owned, 16), sz.owned)
+            cols = pl.ds(offset, width)
+            yield (self.source.at[self.part, rows, cols], self.target.at[z, head, :, cols])
+
+    def begin(self, place):
         sz = self.sz
         n = sz.ctx
         x, y, k, z = place
-        inside = (y * 2 + k) * n + z
-        me = x * sz.group + inside
-        first, stop = span_of(sz.group, low, high)
+        me = x * sz.group + (y * 2 + k) * n + z
         wide = sz.least * HB
-        cols = pl.ds(first_column(sz, me), wide)
-        more = pl.ds(pl.multiple_of(first_column(sz, me) + wide, HB), HB)
-
-        def moves(device, slot):
-            rows = pl.ds(pl.multiple_of(device * sz.owned, 16), sz.owned)
-            source = self.source.at[self.parts[slot], rows]
-            base = (source.at[:, pl.ds(0, wide)], self.targets[slot].at[:, cols])
-            last = (source.at[:, pl.ds(wide, HB)], self.targets[slot].at[:, more])
-            return (base, last)
-
-        def go(device, local):
-            for slot in range(len(self.parts)):
-                base, last = moves(device, slot)
-
-                def start(pair, kind):
-                    if local:
-                        pltpu.make_async_copy(*pair, self.send.at[kind, slot]).start()
+
+        def go(kind, offset, width):
+            for step in list(range(1, n)) + [0]:
+                for source, target in self.moves(place, step, offset, width):
+                    if step:
+                        remote(
+                            source,
+                            target,
+                            self.send.at[kind, step],
+                            self.recv.at[kind, step],
+                            at(x, y, k, lax.rem(z + step, n)),
+                        ).start()
                     else:
-                        remote(
-                            *pair,
-                            self.send.at[kind, slot],
-                            self.recv.at[kind, slot],
-                            (self.section, device // n, lax.rem(device, n)),
-                        ).start()
-
-                start(base, 0)
-                if sz.extra:
-
-                    @pl.when(me < sz.extra)
-                    def _():
-                        start(last, 1)
-
-        @pl.loop(first, min(stop, sz.group - 1))
-        def _(step):
-            go(plane_order(n, place, step), False)
-
-        if stop < sz.group:
-            return
-        for own in (True, False):
-
-            @pl.when((x == self.section) == own)
+                        pltpu.make_async_copy(source, target, self.send.at[kind, 0]).start()
+
+        go(0, 0, wide)
+        if sz.extra:
+
+            @pl.when(has_more(sz, me))
             def _():
-                go(inside, own)
-
-    def middle(self, place):
-        pass
+                go(1, wide, HB)
 
     def finish(self, place):
         sz = self.sz
+        n = sz.ctx
         x, y, k, z = place
-        me = x * sz.group + (y * 2 + k) * sz.ctx + z
+        first = x * sz.group + (y * 2 + k) * n
         wide = sz.least * HB
-        for slot, target in enumerate(self.targets):
-            arrived(target.at[:, pl.ds(0, sz.group * wide)], self.send.at[0, slot])
+        for step in range(n):
+            ctx = lax.rem(z + n - step, n)
+            arrived(self.target.at[ctx, :, :, pl.ds(0, wide)], self.send.at[0, step])
+            if step:
+                arrived(self.target.at[ctx, :, :, pl.ds(0, wide)], self.recv.at[0, step])
             if sz.extra:
 
-                @pl.when(me < sz.extra)
+                @pl.when(has_more(sz, first + z))
                 def _():
-                    arrived(target.at[:, pl.ds(0, sz.group * HB)], self.send.at[1, slot])
-
-            @pl.when(x == self.section)
-            def _():
-                arrived(target.at[:, pl.ds(0, (sz.total - 1) * wide)], self.recv.at[0, slot])
+                    arrived(self.target.at[ctx, :, :, pl.ds(wide, HB)], self.send.at[1, step])
+
+                if step:
+
+                    @pl.when(has_more(sz, first + ctx))
+                    def _():
+                        arrived(self.target.at[ctx, :, :, pl.ds(wide, HB)], self.recv.at[1, step])
+
+
+class PlaneShares:
+    def __init__(self, sz, section, part, source, target, sems):
+        self.sz, self.section, self.part = sz, section, part
+        self.source, self.target = source, target
+        self.send, self.recv, self.local, self.s_over, self.r_over = sems
+
+    def begin(self, place):
+        sz = self.sz
+        n = sz.ctx
+        x, y, k, z = place
+        head = y * 2 + k
+        wide = sz.least * HB
+        slot = jnp.where(x == self.section, 0, 1)
+
+        def go(to, device, local):
+            for ctx in range(n):
+                owner = x * sz.group + head * n + ctx
+                first = first_column(sz, owner)
+
+                def one(kind, offset, width):
+                    source = self.source.at[ctx, to, :, pl.ds(offset, width)]
+                    cols = pl.ds(pl.multiple_of(first + offset, HB), width)
+                    target = self.target.at[slot, self.part, :, cols]
+                    if local:
+                        pltpu.make_async_copy(source, target, self.local.at[kind]).start()
+                    else:
+                        recv = self.recv.at[0] if kind == 0 else self.recv.at[1 + head]
+                        remote(source, target, self.send.at[kind], recv, device).start()
+
+                one(0, 0, wide)
                 if sz.extra:
 
-                    @pl.when(me >= sz.extra)
+                    @pl.when(has_more(sz, owner))
                     def _():
-                        arrived(target.at[:, pl.ds(0, sz.extra * HB)], self.recv.at[1, slot])
-
-                    if sz.extra > 1:
-
-                        @pl.when(me < sz.extra)
-                        def _():
-                            arrived(target.at[:, pl.ds(0, (sz.extra - 1) * HB)], self.recv.at[1, slot])
+                        one(1, wide, HB)
+
+        for step in range(1, 4):
+            to = lax.rem(head + step, 4)
+            go(to, (x, to, z), False)
+        go(head, None, True)
+
+    def cross(self, place):
+        sz = self.sz
+        n = sz.ctx
+        x, y, k, z = place
+        head = y * 2 + k
+        wide = sz.least * HB
+        row = self.target.at[0, self.part]
+        arrived(row.at[:, pl.ds(0, 3 * n * wide)], self.recv.at[0])
+        arrived(row.at[:, pl.ds(0, 3 * n * wide)], self.send.at[0])
+        arrived(row.at[:, pl.ds(0, n * wide)], self.local.at[0])
+        for other in range(4):
+            count = extras_of_head(sz, other)
+            if count:
+
+                @pl.when(head != other)
+                def _():
+                    arrived(row.at[:, pl.ds(0, count * HB)], self.recv.at[1 + other])
+
+                @pl.when(head == other)
+                def _():
+                    arrived(row.at[:, pl.ds(0, 3 * count * HB)], self.send.at[1])
+                    arrived(row.at[:, pl.ds(0, count * HB)], self.local.at[1])
+
+        @pl.when(x != self.section)
+        def _():
+            self.over(place).start()
+
+    def over(self, place):
+        x, y, k, z = place
+        plane = 1 - self.section
+        cols = pl.ds(plane * self.sz.plane * HB, self.sz.plane * HB)
+        return remote(
+            self.target.at[1, self.part, :, cols],
+            self.target.at[0, self.part, :, cols],
+            self.s_over,
+            self.r_over,
+            at(1 - x, y, k, z),
+        )
+
+    def finish(self, place):
+        x = place[0]
+
+        @pl.when(x != self.section)
+        def _():
+            self.over(place).wait_send()
+
+        @pl.when(x == self.section)
+        def _():
+            self.over(place).wait_recv()
 
 
 class ReturnedHeads:
-    reach = 2
+    reach = 0
 
     def __init__(self, sz, section, grads):
         self.sz, self.section = sz, section
         stretch = sz.width // 4
         self.ins = [(grads, vmem())]
-        self.outs = [jax.ShapeDtypeStruct((sz.group, sz.owned, sz.atot), BF)]
+        self.outs = [jax.ShapeDtypeStruct((4, sz.owned, sz.atot), BF)]
         self.scratch = [
             pltpu.VMEM((2, stretch, sz.atot), BF),
             pltpu.VMEM((2, stretch, sz.atot), BF),
+            pltpu.VMEM((sz.ctx, 2, sz.owned, sz.atot), BF),
             DMA((2,)),
             DMA((2,)),
-            DMA,
-            DMA,
+            DMA((sz.ctx,)),
+            DMA((sz.ctx,)),
+            DMA((2,)),
+            DMA((4,)),
         ]
 
     def bind(self, ins, outs, scratch):
         self.source, self.target = ins[0], outs[0]
-        self.got, self.summed, self.s_core, self.r_core, self.send, self.recv = scratch
+        (
+            self.got,
+            self.summed,
+            self.lined,
+            self.s_core,
+            self.r_core,
+            self.s_line,
+            self.r_line,
+            self.send,
+            self.recv,
+        ) = scratch
 
     def rows(self, part, k):
         stretch = self.sz.width // 4
@@ -1001,51 +1096,79 @@
             at(x, y, 1 - k, z),
         )
 
-    def begin(self, place, low=0.0, high=1.0):
+    def own(self, ctx):
+        return pl.ds(pl.multiple_of(ctx * self.sz.owned, 16), self.sz.owned)
+
+    def line(self, place, step):
+        x, y, k, z = place
+        ctx = lax.rem(z + step, self.sz.ctx)
+        return remote(
+            self.summed.at[:, self.own(ctx)],
+            self.lined.at[step],
+            self.s_line.at[step],
+            self.r_line.at[step],
+            at(x, y, k, ctx),
+        )
+
+    def begin(self, place):
         for part in range(2):
             self.core(place, part).start()
 
     def middle(self, place):
-        sz = self.sz
-        n = sz.ctx
-        x, y, k, z = place
+        k = place[2]
         for part in range(2):
             self.core(place, part).wait_recv()
             total = self.source[self.rows(part, k)].astype(F32) + self.got[part].astype(F32)
             self.summed[part] = total.astype(BF)
-        slot = (2 * x + y) * n + z
-        mine = y * n + z
-
-        def pair(index):
-            rows = pl.ds(pl.multiple_of(lax.rem(index, n) * sz.owned, 16), sz.owned)
-            return (self.summed.at[index // n, rows], self.target.at[slot])
-
-        def go(index):
-            device = at(self.section, index // n, k, lax.rem(index, n))
-            remote(*pair(index), self.send, self.recv, device).start()
-
-        @pl.loop(1, 2 * n)
-        def _(step):
-            go(lax.rem(mine + step, 2 * n))
-
-        @pl.when(x == self.section)
-        def _():
-            pltpu.make_async_copy(*pair(mine), self.send).start()
-
-        @pl.when(x != self.section)
-        def _():
-            go(mine)
+        for step in range(1, self.sz.ctx):
+            self.line(place, step).start()
+
+    def home(self, place, part):
+        x, y, k, z = place
+        group = 2 * x + y
+        device = at(self.section, part, k, z)
+        return (self.lined.at[0, part], self.target.at[group], self.send.at[part], self.recv.at[group], device)
+
+    def homes(self, place, starting):
+        x, y, k, z = place
+        for part in range(2):
+            own = jnp.logical_and(x == self.section, y == part)
+
+            @pl.when(jnp.logical_not(own))
+            def _():
+                copy = remote(*self.home(place, part))
+                copy.start() if starting else copy.wait_send()
+
+            @pl.when(own)
+            def _():
+                source, target, send, _, _ = self.home(place, part)
+                copy = pltpu.make_async_copy(source, target, send)
+                copy.start() if starting else copy.wait()
+
+    def late(self, place):
+        x, y, k, z = place
+        total = self.summed[:, self.own(z)].astype(F32)
+        for step in range(1, self.sz.ctx):
+            self.line(place, step).wait_recv()
+            total = total + self.lined[step].astype(F32)
+        self.lined[0] = total.astype(BF)
+        self.homes(place, True)
 
     def finish(self, place):
-        sz = self.sz
         x, y, k, z = place
         for part in range(2):
             self.core(place, part).wait_send()
-        arrived(self.target.at[pl.ds(0, 2 * sz.ctx)], self.send)
+        for step in range(1, self.sz.ctx):
+            self.line(place, step).wait_send()
+        self.homes(place, False)
 
         @pl.when(x == self.section)
         def _():
-            arrived(self.target.at[pl.ds(0, sz.group - 1)], self.recv)
+            for group in range(4):
+
+                @pl.when(group != 2 * x + y)
+                def _():
+                    arrived(self.target.at[group], self.recv.at[group])
 
 
 def begin(jobs, place, low=0.0, high=1.0):
@@ -1344,8 +1467,7 @@
 
 def spread(sz, small, tokens, cotangent, qkv, out_w, gate_up, down):
     n = sz.ctx
-    counts = [plane_blocks(sz, plane) for plane in range(2)]
-    staged_cols = max(count for _, count in counts) * HB
+    half = sz.plane * HB
 
     def body(ins, outs, scratch, jobs):
         small, tokens, cotangent, qkv, out_w, gate_up, down = ins
@@ -1404,20 +1526,10 @@
 
         pltpu.make_async_copy(small, small_all.at[me], s_small).start()
 
-        def columns_over(plane, part):
-            start, count = counts[1 - plane]
-            base = (sz.ff if part == 1 else 0) + start * HB
-            source = (down if part == 2 else gate_up).at[:, pl.ds(base, count * HB)]
-            target = cols_x.at[part, :, pl.ds(0, count * HB)]
-            return remote(source, target, s_cx.at[part], r_cx.at[part], across)
-
-        def for_plane(act):
-            for plane in range(2):
-
-                @pl.when(x == plane)
-                def _():
-                    for part in range(3):
-                        act(plane, part)
+        def columns_over(part):
+            base = (sz.ff if part == 1 else 0) + (1 - x) * half
+            source = (down if part == 2 else gate_up).at[:, pl.ds(pl.multiple_of(base, HB), half)]
+            return remote(source, cols_x.at[part], s_cx.at[part], r_cx.at[part], across)
 
         heads, first = jobs
         heads.use(ins, outs)
@@ -1427,23 +1539,15 @@
         def _():
             heads.begin(place)
 
-        for_plane(lambda plane, part: columns_over(plane, part).start())
+        for part in range(3):
+            columns_over(part).start()
         arrived(heads_x, r_hx)
 
         @pl.when(x != heads.section)
         def _():
             heads.begin(place)
 
-        def came(plane, part):
-            width = counts[plane][1] * HB
-            arrived(cols_x.at[part, :, pl.ds(0, width)], r_cx.at[part])
-
-        for plane in range(2):
-
-            @pl.when(x == plane)
-            def _():
-                came(plane, 0)
-
+        columns_over(0).wait_recv()
         first.begin(place)
         heads.middle(place)
         arrived(small_all.at[pl.ds(0, sz.total - 1)], r_small)
@@ -1453,12 +1557,10 @@
         owns(False)
         heads.finish(place)
 
-        def rest(plane, part):
+        for part in range(3):
             if part:
-                came(plane, part)
-            columns_over(plane, part).wait_send()
-
-        for_plane(rest)
+                columns_over(part).wait_recv()
+            columns_over(part).wait_send()
         arrived(heads_x, s_hx)
         first.finish(place)
 
@@ -1468,7 +1570,7 @@
         (shape((sz.rows, sz.width), BF), hbm()),
         (shape((sz.rows, sz.width), BF), hbm()),
         (shape((2, sz.owned, sz.atot), BF), hbm()),
-        (shape((3, sz.owned, staged_cols), BF), hbm()),
+        (shape((3, sz.owned, half), BF), hbm()),
     ]
     arrays = (small, tokens, cotangent, qkv, out_w, gate_up, down)
     scratch = [DMA, DMA, DMA((2, 2)), DMA((2,)), DMA, DMA, DMA((3,)), DMA((3,))]
@@ -1655,7 +1757,7 @@
         group = 2 * x + y
         dh_all[group] = dh1[...].astype(BF)
         copies = gather_pair(dh_all, place, s_in, r_in)
-        begin(jobs, place, 0.0, 0.4)
+        jobs[0].begin(place)
         load.wait()
         gathered_pair(dh_all, place, copies, r_in)
         dh = dh_all[...].reshape(rows, sz.width)
@@ -1693,7 +1795,7 @@
                 )
             )
             kv_copies[-1].start()
-        begin(jobs, place, 0.4, 1.0)
+        jobs[1].begin(place)
         dw_out[:, sz.acols :] = mm(dh, o_in[...].astype(BF), TN).astype(BF)
         total = dkv[z].astype(F32)
         for step in range(n - 1):
@@ -1706,7 +1808,6 @@
         back = scatter_pair(parts, landed, place, s_back, r_back)
         dw_out[:, : sz.acols] = mm(n1_all[...].reshape(rows, sz.width), da[...], TN).astype(BF)
         bias_grad[...] = jnp.sum(da[...].astype(F32), axis=0, keepdims=True)
-        middle(jobs, place)
         for copy in copies + kv_copies:
             copy.wait_send()
         dn1 = parts[group].astype(F32)
@@ -1763,7 +1864,7 @@
     def __init__(self, sz, place, sources, w, sems):
         x, y, k, z = place
         self.sz, self.sources, self.w, self.sems = sz, sources, w, sems
-        self.more = x * sz.group + (y * 2 + k) * sz.ctx + z < sz.extra
+        self.more = has_more(sz, x * sz.group + (y * 2 + k) * sz.ctx + z)
         self.wide = sz.least * HB
 
     def copies(self, offset, width, kind):
@@ -1800,9 +1901,11 @@
                     copy.wait()
 
 
-def meet_tree(sz, place, jobs):
+def meet_tree(sz, place, jobs, diagonal=False):
     x, y, k, z = place
     peers = tree_peers(sz.ctx, x, y, k, z)
+    if diagonal:
+        peers.append(at(1 - x, 1 - y, k, z))
     meet(sz, place, peers, peers[:1], jobs)
 
 
@@ -1891,15 +1994,18 @@
         x, y, k, z = place
         hidden_weights = HiddenWeights(sz, place, sources, w, w_sems)
         hidden_weights.start()
-        meet_tree(sz, place, jobs)
+        meet_tree(sz, place, jobs, len(jobs) > 1)
         gather = Gather(n, sz.rows, dy_all, place, refs[:12])
         scatter = Scatter(n, sz.rows, place, refs[12:])
         dy_all[k, gather.groups[0], z] = dy[...]
         gather.begin()
-        begin(jobs[:1], place)
+        down_share, *heads = jobs
+        down_share.source = dw_out
+        for job in heads:
+            job.begin(place)
         hidden_weights.wait()
-        middle(jobs, place)
-        begin(jobs[1:], place)
+        for job in heads:
+            job.middle(place)
         rows = n * sz.rows
 
         def column(core, which):
@@ -1930,13 +2036,16 @@
                 side = left[:, :, :, :, cols].reshape(total, tile)
                 dw_out[slot, cols] = mm(side, grads, TN).astype(BF)
 
-        dn2 = scatter.run(
-            (
-                lambda: weight_grad(0, n2_all, dgate_all),
-                lambda: weight_grad(1, n2_all, dup_all),
-                lambda: weight_grad(2, dy_all, hm_in),
-            )
-        )
+        def down_first():
+            weight_grad(2, dy_all, hm_in)
+            down_share.begin(place)
+
+        def last():
+            weight_grad(1, n2_all, dup_all)
+            for job in heads:
+                job.late(place)
+
+        dn2 = scatter.run((down_first, lambda: weight_grad(0, n2_all, dgate_all), last))
         values = h1[...]
         inverse = row_norm(values)
         weighted = dn2 * gain[...]
@@ -1979,18 +2088,31 @@
     )
 
 
-def collect(sz, small, acts, grads, jobs):
+def collect(sz, small, acts, grads, shares, heads):
     n = sz.ctx
+    order = [(section, part) for part in (2, 0, 1) for section in (1, 0)]
 
     def body(ins, outs, scratch, jobs):
-        small, act0, act1, grad0, grad1 = ins
-        small_in, act_out, grad_out = outs
-        s_small, r_small, s_out, r_out = scratch
+        small, act0, act1, grad0, grad1, *shares = ins
+        small_in, act_out, grad_out, w_out = outs
+        s_small, r_small, s_out, r_out, send, recv, local, s_over, r_over = scratch
+        (heads,) = jobs
         place = where_am_i()
         x, y, k, z = place
         me = x * sz.group + (y * 2 + k) * n + z
-        meet(sz, place, [], [], jobs)
-        begin(jobs, place)
+        greet_all(me, sz.total, lambda index: flat_place(index, sz.group, n))
+        heads.begin(place)
+        moves = []
+        for number, (section, part) in enumerate(order):
+            sems = (
+                send.at[number],
+                recv.at[number],
+                local.at[number],
+                s_over.at[number],
+                r_over.at[number],
+            )
+            moves.append(PlaneShares(sz, section, part, shares[number], w_out, sems))
+            moves[-1].begin(place)
 
         @pl.loop(1, sz.total)
         def _(step):
@@ -2025,7 +2147,12 @@
                         def _():
                             pltpu.make_async_copy(source, target.at[k], r_out.at[slot, k]).start()
 
-        middle(jobs, place)
+        heads.middle(place)
+        for move in moves[:4]:
+            move.cross(place)
+        heads.late(place)
+        for move in moves[4:]:
+            move.cross(place)
         results(True)
         results(False)
         for slot, target in enumerate((act_out, grad_out)):
@@ -2033,19 +2160,34 @@
                 arrived(target.at[batch], r_out.at[slot, batch])
         arrived(small_in.at[pl.ds(0, sz.total - 1)], r_small)
         arrived(small_in, s_small)
-        finish(jobs, place)
+        heads.finish(place)
+        for move in moves:
+            move.finish(place)
 
     shapes = (
         jax.ShapeDtypeStruct((sz.total, 8, LANES), F32),
         jax.ShapeDtypeStruct((2, sz.rows, sz.width), BF),
         jax.ShapeDtypeStruct((2, sz.rows, sz.width), BF),
-    )
+        jax.ShapeDtypeStruct((2, 3, sz.owned, sz.ff), BF),
+    )
+    arrays = (small, *acts, *grads, *[shares[section][part] for section, part in order])
+    many = len(order)
     return run_call(
         body,
-        [(array, hbm()) for array in (small, *acts, *grads)],
+        [(array, hbm()) for array in arrays],
         [(shape, hbm()) for shape in shapes],
-        [DMA, DMA, DMA((2, 2)), DMA((2, 2))],
-        jobs,
+        [
+            DMA,
+            DMA,
+            DMA((2, 2)),
+            DMA((2, 2)),
+            DMA((many, 2)),
+            DMA((many, 5)),
+            DMA((many, 2)),
+            DMA((many,)),
+            DMA((many,)),
+        ],
+        [heads],
         2,
         "collect_gradients",
     )
@@ -2136,19 +2278,19 @@
         acts.append(act)
         inputs.append(act)
     grads, das, smalls = [None, None], [None, None], [None, None]
-    came = [[None] * 3, [None] * 3]
+    shares = [[None] * 3, [None] * 3]
     came_heads = [None, None]
     dy = cot_own
     for section in (1, 0):
-        jobs = []
+        jobs = [LineShares(sz, 2)]
         if section == 0:
-            jobs = [ReturnedHeads(sz, 1, das[1]), Returned(sz, 1, (2,), dw)]
-        (dh1, dw, gain2_grad), more = feed_back(
+            jobs.append(ReturnedHeads(sz, 1, das[1]))
+        (dh1, dw, gain2_grad), ((shares[section][2],), *more) = feed_back(
             sz, section, dy, middles[section], gain2[section], weights[section], kept_feed[section], jobs
         )
         if section == 0:
-            (came_heads[1],), (came[1][2],) = more
-        (dy, das[section], gain1_grad, bias_grad), (returned,) = attend_back(
+            ((came_heads[1],),) = more
+        (dy, das[section], gain1_grad, bias_grad), ((shares[section][0],), (shares[section][1],)) = attend_back(
             sz,
             section,
             dh1,
@@ -2159,10 +2301,8 @@
             qpos,
             kpos,
             kept_att[section],
-            [Returned(sz, section, (0, 1) if section else (0, 1, 2), dw)],
+            [LineShares(sz, 0, dw), LineShares(sz, 1, dw)],
         )
-        for part, grad in enumerate(returned):
-            came[section][part] = grad
         grads[section] = dy
         whole_bias = jnp.zeros((1, query_columns + 2 * key_columns), F32)
         offset = 0
@@ -2176,20 +2316,13 @@
         rows = [line(row.reshape(group, -1))[:, None] for row in rows]
         smalls[section] = jnp.concatenate(rows + [jnp.zeros((group, 4, LANES), F32)], axis=1)
     small_out = jnp.concatenate(smalls, axis=0)
-    (small_in, act_out, grad_out), ((came_heads[0],),) = collect(
-        sz, small_out, acts, grads, [ReturnedHeads(sz, 0, das[0])]
-    )
-
-    def own(parts):
-        return jnp.where(x == 0, parts[0], parts[1])
-
+    (small_in, act_out, grad_out, w_out), ((came_heads[0],),) = collect(
+        sz, small_out, acts, grads, shares, ReturnedHeads(sz, 0, das[0])
+    )
     small_sum = jnp.sum(small_in, axis=0)
-    gate_up_grad = jnp.concatenate(
-        [own((came[0][part], came[1][part])).astype(F32) for part in range(2)], axis=1
-    )[None]
-    down_grad = own((came[0][2], came[1][2])).astype(F32)[None]
-    att_in = own(came_heads)
-    att_sum = jnp.sum(att_in.astype(F32).reshape(4, n, sz.owned, sz.atot), axis=1)
+    gate_up_grad = jnp.concatenate([w_out[0, 0], w_out[0, 1]], axis=1).astype(F32)[None]
+    down_grad = w_out[0, 2].astype(F32)[None]
+    att_sum = jnp.where(x == 0, came_heads[0], came_heads[1]).astype(F32)
     q_grad = att_sum[:, :, : sz.qcols].transpose(1, 0, 2).reshape(sz.owned, query_columns)
     kv_grad = jnp.sum(
         att_sum[:, :, sz.qcols : sz.acols].reshape(

time: 914 us -> 839 us (0.918)
  Pallas kernels: 876 us -> 801 us
    pallas_call x10, Pallas kernels: 876 us -> 801 us  [run_call(): pl.pallas_call(kernel, out_shape=tuple((shape for shape, _ in outs)), in_...]
where the time goes in v3:
time: 839 us; the launch traced here: 830 us
  Pallas kernels  801 us (95%)
  other arithmetic  14.7 us (2%)
  local copies, waits for them, and re-layouts  13.2 us (2%)
    pallas_call x10, Pallas kernels, run_call(): pl.pallas_call(kernel, out_shape=tuple((shape for shape, _ in outs)), in_...  801 us

profile of v3, /device:TPU:14, one launch (start us, length us, event | category | flops | bytes accessed | tf_op | source)
XLA Modules:
  0.0 830.1 jit_solution(11716851124396865574)
XLA Ops:
  0.7 0.1 pad.58.clone
  0.8 1.4 fusion.6.refs_0_
  2.1 71.0 %spread_weights.1 = (bf16[32,16,128]{2,1,0:T(8,128)(2,1)}, bf16[64,1536]{1,0:T(8,128)(2,1)}, bf16[64,1536]{1,0:T(8,128)(2,1)}, bf16[2,96,1024]{2,1,0:T(8,128)(2,...) custom-call(bf16[16,128]{1,0:T(8,128)(2,1)} %fusion.6.refs_0_, ...), custom_call_target="tpu_custom_call" | custom-call | tf_op jit(solution)/shard_map/spread_weights/pallas_call | solution.py:690
  73.2 0.9 bitcast_convert_fusion.1
  74.2 0.6 slice_bitcast_fusion.4
  74.9 0.1 reshape.144
  75.0 0.1 convert_element_type.66
  75.1 0.1 broadcast_multiply_fusion
  75.2 1.2 sine_multiply_fusion
  76.5 0.8 reshape.161.refs_6_
  77.3 0.7 reshape.146.refs_7_
  78.0 0.7 squeeze.45.refs_1_.refs_2_
  78.6 56.9 %attend_forward.2 = (f32[64,1536]{1,0:T(8,128)}, bf16[4,64,1536]{2,1,0:T(8,128)(2,1)}, bf16[256,384]{1,0:T(8,128)(2,1)}, bf16[4,256,256]{2,1,0:T(8,128)(2,1)}, f...) custom-call(bf16[64,1536]{1,0:T(8,128)(2,1)} %get-tuple-element.72.refs_0_.re, ...), custom_call_target="tpu_custom_call" | custom-call | tf_op jit(solution)/shard_map/attend_forward/pallas_call | solution.py:690
  135.6 0.7 squeeze.47.refs_1_.refs_2_
  136.2 107.9 %feed_forward.2 = (bf16[64,1536]{1,0:T(8,128)(2,1)}, bf16[2,4,4,64,1536]{4,3,2,1,0:T(8,128)(2,1)}, bf16[2,4,256,384]{3,2,1,0:T(8,128)(2,1)}, bf16[2,4,256,384]{3...) custom-call(f32[64,1536]{1,0:T(8,128)} %get-tuple-element.76.refs_0_.r, ...), custom_call_target="tpu_custom_call" | custom-call | tf_op jit(solution)/shard_map/feed_forward/pallas_call | solution.py:690
  244.1 0.7 squeeze.48.refs_1_.refs_2_
  244.8 58.1 %attend_forward.3 = (f32[64,1536]{1,0:T(8,128)}, bf16[4,64,1536]{2,1,0:T(8,128)(2,1)}, bf16[256,384]{1,0:T(8,128)(2,1)}, bf16[4,256,256]{2,1,0:T(8,128)(2,1)}, f...) custom-call(bf16[64,1536]{1,0:T(8,128)(2,1)} %get-tuple-element.81.refs_0_.re, ...), custom_call_target="tpu_custom_call" | custom-call | tf_op jit(solution)/shard_map/attend_forward/pallas_call | solution.py:690
  302.9 0.7 squeeze.50.refs_1_.refs_2_
  303.6 86.8 %feed_forward.3 = (bf16[64,1536]{1,0:T(8,128)(2,1)}, bf16[2,4,4,64,1536]{4,3,2,1,0:T(8,128)(2,1)}, bf16[2,4,256,384]{3,2,1,0:T(8,128)(2,1)}, bf16[2,4,256,384]{3,2,1,0:T(8,128)(2,1)}, bf16[2,4,256,384]{3,2,1,0:T(8,128)(2,1)}) custom-call(f32[64,1536]{1,0:T(8,128)} %get-tuple-element.83.refs_0_.refs_1_, f32[1,1536]{1,0:T(1,128)} %squeeze.50.refs_1_.refs_2_, ...), custom_call_target="tpu_custom_call" | custom-call | tf_op jit(solution)/shard_map/feed_forward/pallas_call | solution.py:690
  390.4 94.2 %feed_backward.2 = (f32[64,1536]{1,0:T(8,128)}, bf16[3,1536,384]{2,1,0:T(8,128)(2,1)}, f32[1,1536]{1,0:T(1,128)}, bf16[4,4,96,384]{3,2,1,0:T(8,128)(2,1)}) custom-call(bf16[64,1536]{1,0:T(8,128)(2,1)} %get-tuple-element.71.refs_0_, f32[64,1536]{1,0:T(8,128)} %get-tuple-element.83.refs_0_.refs_1_, f32[1,1536]{1,0:T(1,128)} %squeeze.50.refs_1_.refs_2_, ...), custom_call_target="tpu_custom_call" | custom-call | tf_op jit(solution)/shard_map/feed_backward/pallas_call | solution.py:690
  484.7 57.0 %attend_backward.2 = (bf16[64,1536]{1,0:T(8,128)(2,1)}, bf16[1536,1024]{1,0:T(8,128)(2,1)}, f32[1,1536]{1,0:T(1,128)}, f32[1,640]{1,0:T(1,128)}, bf16[4,4,96,384...) custom-call(f32[64,1536]{1,0:T(8,128)} %get-tuple-element.91.refs_0_, ...), custom_call_target="tpu_custom_call" | custom-call | tf_op jit(solution)/shard_map/attend_backward/pallas_call | solution.py:690
  541.6 107.1 %feed_backward.3 = (f32[64,1536]{1,0:T(8,128)}, bf16[3,1536,384]{2,1,0:T(8,128)(2,1)}, f32[1,1536]{1,0:T(1,128)}, bf16[4,4,96,384]{3,2,1,0:T(8,128)(2,1)}, bf16[4,96,1024]{2,1,0:T(8,128)(2,1)}) custom-call(bf16[64,1536]{1,0:T(8,128)(2,1)} %get-tuple-element.98.refs_0_.refs_4_, f32[64,1536]{1,0:T(8,128)} %get-tuple-element.76.refs_0_.refs_1_, ...), custom_call_target="tpu_custom_call" | custom-call | tf_op jit(solution)/shard_map/feed_backward/pallas_call | solution.py:690
  648.8 57.7 %attend_backward.3 = (bf16[64,1536]{1,0:T(8,128)(2,1)}, bf16[1536,1024]{1,0:T(8,128)(2,1)}, f32[1,1536]{1,0:T(1,128)}, f32[1,640]{1,0:T(1,128)}, bf16[4,4,96,384...) custom-call(f32[64,1536]{1,0:T(8,128)} %get-tuple-element.104.refs_0_, ...), custom_call_target="tpu_custom_call" | custom-call | tf_op jit(solution)/shard_map/attend_backward/pallas_call | solution.py:690
  706.5 0.7 constant_dynamic-update-slice_fusion.5
  707.2 0.6 constant_dynamic-update-slice_fusion.4
  707.8 0.6 constant_dynamic-update-slice_fusion.3
  708.6 0.1 reshape.150
  708.7 0.7 reduce.4
  709.7 0.1 reshape.154
  710.1 0.1 concatenate.39
  710.2 0.7 pad_maximum_fusion.1.refs_0_
  710.9 104.1 %collect_gradients.1 = (f32[32,8,128]{2,1,0:T(8,128)}, bf16[2,64,1536]{2,1,0:T(8,128)(2,1)}, bf16[2,64,1536]{2,1,0:T(8,128)(2,1)}, bf16[2,3,96,8960]{3,2,1,0:T(8,128)(2,1)}, bf16[4,96,1024]{2,1,0:T(8,128)(2,1)}) custom-call(f32[32,8,128]{2,1,0:T(8,128)} %pad_maximum_fusion.1.refs_0_, bf16[64,1536]{1,0:T(8,128)(2,1)} %get-tuple-element.81.refs_0_.refs_1_, ...), custom_call_target="tpu_custom_call" | custom-call | tf_op jit(solution)/shard_map/collect_gradients/pallas_call | solution.py:690
  815.0 4.7 bitcast_convert_fusion
  819.7 3.5 maximum_convert_fusion
  823.2 0.1 select_convert_fusion
  823.3 0.1 slice_bitcast_fusion.2
  823.5 0.2 reshape.156
  823.7 0.3 reduce_sum.19
  824.1 0.2 copy.56
  824.2 0.2 reshape.157
  824.4 0.9 maximum_bitcast_fusion
  825.4 0.4 copy.57
  825.7 1.1 reshape.158
  826.8 0.5 fusion.9
  827.4 0.5 slice.113
  827.9 0.5 slice.114
  828.4 0.7 copy.81
  829.1 0.7 copy.82
  (65 shorter events, 1.1 us)
Async XLA Ops:
  0.6 74.2 %copy-start = (s32[2,1024]{1,0:T(2,128)S(1)}, s32[2,1024]{1,0:T(2,128)}, u32[]{:S(2)}) copy-start(s32[2,1024]{1,0:T(2,128)} %param.11) | copy-start | bytes 24580
  648.8 59.8 %copy-start.10 = (f32[1,640]{1,0:T(1,128)S(1)}, f32[1,640]{1,0:T(1,128)}, u32[]{:S(2)}) copy-start(f32[1,640]{1,0:T(1,128)} %get-tuple-element.116) | copy-start | bytes 7684
  648.8 60.7 %copy-start.9 = (f32[1,1536]{1,0:T(1,128)S(1)}, f32[1,1536]{1,0:T(1,128)}, u32[]{:S(2)}) copy-start(f32[1,1536]{1,0:T(1,128)} %get-tuple-element.112) | copy-start | bytes 18436
  648.8 61.1 %copy-start.8 = (f32[1,1536]{1,0:T(1,128)S(1)}, f32[1,1536]{1,0:T(1,128)}, u32[]{:S(2)}) copy-start(f32[1,1536]{1,0:T(1,128)} %get-tuple-element.114) | copy-start | bytes 18436
  648.8 61.2 %copy-start.7 = (f32[1,1536]{1,0:T(1,128)S(1)}, f32[1,1536]{1,0:T(1,128)}, u32[]{:S(2)}) copy-start(f32[1,1536]{1,0:T(1,128)} %get-tuple-element.115) | copy-start | bytes 18436
  819.7 3.5 copy-start.2
  819.7 3.5 copy-start.3
  824.4 2.4 copy-start.6
  824.4 4.0 copy-start.5
  825.3 3.8 copy-start.4
  825.4 4.5 copy-start.1

commit v4 on v3

--- a/solution.py
+++ b/solution.py
@@ -904,7 +904,7 @@
             cols = pl.ds(offset, width)
             yield (self.source.at[self.part, rows, cols], self.target.at[z, head, :, cols])
 
-    def begin(self, place):
+    def begin(self, place, steps=None):
         sz = self.sz
         n = sz.ctx
         x, y, k, z = place
@@ -912,7 +912,7 @@
         wide = sz.least * HB
 
         def go(kind, offset, width):
-            for step in list(range(1, n)) + [0]:
+            for step in list(range(1, n)) + [0] if steps is None else steps:
                 for source, target in self.moves(place, step, offset, width):
                     if step:
                         remote(
@@ -961,6 +961,10 @@
         self.sz, self.section, self.part = sz, section, part
         self.source, self.target = source, target
         self.send, self.recv, self.local, self.s_over, self.r_over = sems
+        self.row = target.at[0, part]
+
+    def place_in(self, slot):
+        return self.target.at[slot, self.part]
 
     def begin(self, place):
         sz = self.sz
@@ -978,7 +982,7 @@
                 def one(kind, offset, width):
                     source = self.source.at[ctx, to, :, pl.ds(offset, width)]
                     cols = pl.ds(pl.multiple_of(first + offset, HB), width)
-                    target = self.target.at[slot, self.part, :, cols]
+                    target = self.place_in(slot).at[:, cols]
                     if local:
                         pltpu.make_async_copy(source, target, self.local.at[kind]).start()
                     else:
@@ -997,13 +1001,13 @@
             go(to, (x, to, z), False)
         go(head, None, True)
 
-    def cross(self, place):
+    def settled(self, place):
         sz = self.sz
         n = sz.ctx
         x, y, k, z = place
         head = y * 2 + k
         wide = sz.least * HB
-        row = self.target.at[0, self.part]
+        row = self.row
         arrived(row.at[:, pl.ds(0, 3 * n * wide)], self.recv.at[0])
         arrived(row.at[:, pl.ds(0, 3 * n * wide)], self.send.at[0])
         arrived(row.at[:, pl.ds(0, n * wide)], self.local.at[0])
@@ -1020,7 +1024,10 @@
                     arrived(row.at[:, pl.ds(0, 3 * count * HB)], self.send.at[1])
                     arrived(row.at[:, pl.ds(0, count * HB)], self.local.at[1])
 
-        @pl.when(x != self.section)
+    def cross(self, place):
+        self.settled(place)
+
+        @pl.when(place[0] != self.section)
         def _():
             self.over(place).start()
 
@@ -1048,32 +1055,56 @@
             self.over(place).wait_recv()
 
 
+class ReadyShares(PlaneShares):
+    reach = 0
+
+    def __init__(self, sz, section, part, source):
+        self.sz, self.section, self.part = sz, section, part
+        self.ins = [(source, None)]
+        self.outs = [jax.ShapeDtypeStruct((sz.owned, sz.ff), BF)]
+        self.scratch = [DMA((2,)), DMA((5,)), DMA((2,))]
+
+    def bind(self, ins, outs, scratch):
+        self.source, self.row = ins[0], outs[0]
+        self.send, self.recv, self.local = scratch
+
+    def place_in(self, slot):
+        return self.row
+
+    def finish(self, place):
+        self.settled(place)
+
+
 class ReturnedHeads:
     reach = 0
 
-    def __init__(self, sz, section, grads):
-        self.sz, self.section = sz, section
+    def __init__(self, sz, section, part, grads):
+        self.sz, self.section, self.part = sz, section, part
         stretch = sz.width // 4
-        self.ins = [(grads, vmem())]
+        self.ins = [] if grads is None else [(grads, None)]
         self.outs = [jax.ShapeDtypeStruct((4, sz.owned, sz.atot), BF)]
         self.scratch = [
-            pltpu.VMEM((2, stretch, sz.atot), BF),
-            pltpu.VMEM((2, stretch, sz.atot), BF),
-            pltpu.VMEM((sz.ctx, 2, sz.owned, sz.atot), BF),
-            DMA((2,)),
-            DMA((2,)),
+            pltpu.VMEM((stretch, sz.atot), BF),
+            pltpu.VMEM((stretch, sz.atot), BF),
+            pltpu.VMEM((sz.ctx, sz.owned, sz.atot), BF),
+            DMA,
+            DMA,
+            DMA,
             DMA((sz.ctx,)),
             DMA((sz.ctx,)),
-            DMA((2,)),
+            DMA,
             DMA((4,)),
         ]
 
     def bind(self, ins, outs, scratch):
-        self.source, self.target = ins[0], outs[0]
+        if ins:
+            self.source = ins[0]
+        self.target = outs[0]
         (
             self.got,
             self.summed,
             self.lined,
+            self.load,
             self.s_core,
             self.r_core,
             self.s_line,
@@ -1082,18 +1113,17 @@
             self.recv,
         ) = scratch
 
-    def rows(self, part, k):
+    def rows(self, k):
         stretch = self.sz.width // 4
-        return pl.ds(pl.multiple_of((part * 2 + k) * stretch, 16), stretch)
-
-    def core(self, place, part):
+        return pl.ds(pl.multiple_of((self.part * 2 + k) * stretch, 16), stretch)
+
+    def own_rows(self, place):
+        return pltpu.make_async_copy(self.source.at[self.rows(place[2])], self.summed, self.load)
+
+    def core(self, place):
         x, y, k, z = place
         return remote(
-            self.source.at[self.rows(part, 1 - k)],
-            self.got.at[part],
-            self.s_core.at[part],
-            self.r_core.at[part],
-            at(x, y, 1 - k, z),
+            self.source.at[self.rows(1 - k)], self.got, self.s_core, self.r_core, at(x, y, 1 - k, z)
         )
 
     def own(self, ctx):
@@ -1103,7 +1133,7 @@
         x, y, k, z = place
         ctx = lax.rem(z + step, self.sz.ctx)
         return remote(
-            self.summed.at[:, self.own(ctx)],
+            self.summed.at[self.own(ctx)],
             self.lined.at[step],
             self.s_line.at[step],
             self.r_line.at[step],
@@ -1111,43 +1141,35 @@
         )
 
     def begin(self, place):
-        for part in range(2):
-            self.core(place, part).start()
+        self.own_rows(place).start()
+        self.core(place).start()
 
     def middle(self, place):
-        k = place[2]
-        for part in range(2):
-            self.core(place, part).wait_recv()
-            total = self.source[self.rows(part, k)].astype(F32) + self.got[part].astype(F32)
-            self.summed[part] = total.astype(BF)
+        self.own_rows(place).wait()
+        self.core(place).wait_recv()
+        self.summed[...] = (self.summed[...].astype(F32) + self.got[...].astype(F32)).astype(BF)
         for step in range(1, self.sz.ctx):
             self.line(place, step).start()
 
-    def home(self, place, part):
-        x, y, k, z = place
-        group = 2 * x + y
-        device = at(self.section, part, k, z)
-        return (self.lined.at[0, part], self.target.at[group], self.send.at[part], self.recv.at[group], device)
-
     def homes(self, place, starting):
         x, y, k, z = place
-        for part in range(2):
-            own = jnp.logical_and(x == self.section, y == part)
-
-            @pl.when(jnp.logical_not(own))
-            def _():
-                copy = remote(*self.home(place, part))
-                copy.start() if starting else copy.wait_send()
-
-            @pl.when(own)
-            def _():
-                source, target, send, _, _ = self.home(place, part)
-                copy = pltpu.make_async_copy(source, target, send)
-                copy.start() if starting else copy.wait()
+        own = jnp.logical_and(x == self.section, y == self.part)
+        target = self.target.at[2 * x + y]
+
+        @pl.when(jnp.logical_not(own))
+        def _():
+            device = at(self.section, self.part, k, z)
+            copy = remote(self.lined.at[0], target, self.send, self.recv.at[2 * x + y], device)
+            copy.start() if starting else copy.wait_send()
+
+        @pl.when(own)
+        def _():
+            copy = pltpu.make_async_copy(self.lined.at[0], target, self.send)
+            copy.start() if starting else copy.wait()
 
     def late(self, place):
         x, y, k, z = place
-        total = self.summed[:, self.own(z)].astype(F32)
+        total = self.summed[self.own(z)].astype(F32)
         for step in range(1, self.sz.ctx):
             self.line(place, step).wait_recv()
             total = total + self.lined[step].astype(F32)
@@ -1156,13 +1178,12 @@
 
     def finish(self, place):
         x, y, k, z = place
-        for part in range(2):
-            self.core(place, part).wait_send()
+        self.core(place).wait_send()
         for step in range(1, self.sz.ctx):
             self.line(place, step).wait_send()
         self.homes(place, False)
 
-        @pl.when(x == self.section)
+        @pl.when(jnp.logical_and(x == self.section, y == self.part))
         def _():
             for group in range(4):
 
@@ -1288,27 +1309,40 @@
             for which in range(4):
                 self.core(which, step).wait_send()
 
-    def run(self, column, nearly):
+    def stages(self, column, nearly):
         k, steps = self.k, range(self.n)
-        for step in range(1, self.n):
-            self.spread(step)
-        column(k, 0)
-        for step in steps:
-            self.second(step)
-        self.other(0)
-        column(1 - k, 0)
-        column(k, 1)
-        column(k, 2)
-        for step in steps:
-            self.third(step)
-        self.other(1)
-        column(1 - k, 1)
-        self.other(2)
-        column(1 - k, 2)
-        nearly()
-        column(k, 3)
-        self.other(3)
-        column(1 - k, 3)
+
+        def spread():
+            for step in range(1, self.n):
+                self.spread(step)
+
+        def second():
+            for step in steps:
+                self.second(step)
+
+        def near():
+            self.other(0)
+            column(1 - k, 0)
+            column(k, 1)
+            column(k, 2)
+
+        def third():
+            for step in steps:
+                self.third(step)
+
+        def far():
+            self.other(1)
+            column(1 - k, 1)
+            self.other(2)
+            column(1 - k, 2)
+            nearly()
+
+        def last():
+            column(k, 3)
+            self.other(3)
+            column(1 - k, 3)
+
+        return [self.begin, spread, lambda: column(k, 0), second, near, third, far, last]
 
 
 class Scatter:
@@ -1409,14 +1443,14 @@
             for step in self.order():
                 self.close(direction, part, step).start()
 
-    def run(self, fill):
-        fill = list(fill) + [lambda: None] * 3
+    def open(self):
         self.add_core(3)
         for step in self.order():
             self.diag(1, step).start()
             self.diag(0, step).start()
         self.add_core(0)
-        fill[0]()
+
+    def late(self):
         for step in self.order():
             slot = self.slot(step)
             for direction, part in ((0, 0), (1, 1)):
@@ -1429,9 +1463,9 @@
                     + self.from_diag[came, step].astype(F32)
                 ).astype(BF)
                 self.close(direction, part, step).start()
-        fill[1]()
+
+    def along(self):
         group = self.groups[0]
-        result = None
         for step in self.order():
             slot = self.slot(step)
             for direction in range(2):
@@ -1446,12 +1480,17 @@
                 self.parts[self.k, group, slot] = total.astype(BF)
                 self.line(step).start()
             else:
-                result = total
-        fill[2]()
+                self.own = total
+
+    def result(self):
+        result = self.own
         for step in range(1, self.n):
             self.line(step).wait_recv()
             result = result + self.from_line[step].astype(F32)
         return result
+
+    def stages(self):
+        return [self.open, self.late, self.along]
 
     def finish(self):
         for which in range(4):
@@ -1463,6 +1502,21 @@
                     self.close(direction, part, step).wait_send()
             if step:
                 self.line(step).wait_send()
+
+
+CHUNKS = 2
+A, B = 0, 1
+TOGETHER = (
+    (A, 0), (B, 0), (A, 1), (A, 2), (A, 3), (A, 4), (B, 1), (A, 5), (B, 2), (A, 6), (B, 3), (A, 7),
+    (A, 8), (B, 4), (B, 5), (A, 9), (B, 6), (B, 7), (B, 8), (A, 10), (B, 9), (B, 10),
+)
+
+
+def run_together(first, second, after):
+    for stream, number in TOGETHER:
+        (first, second)[stream][number]()
+        if (stream, number) in after:
+            after[stream, number]()
 
 
 def spread(sz, small, tokens, cotangent, qkv, out_w, gate_up, down):
@@ -1608,6 +1662,49 @@
         self.source, self.staged = ins[source], outs[staged]
 
 
+class Part:
+    def __init__(self, body, ins, outs, scratch):
+        self.body, self.ins, self.outs, self.scratch = body, ins, outs, scratch
+
+
+def joined(sz, first, first_jobs, second, second_jobs, link, cores, collective_id, name):
+    a, b, c = len(first.ins), len(first.outs), len(first.scratch)
+    count = len(first_jobs)
+
+    def body(ins, outs, scratch, jobs):
+        place = where_am_i()
+        x, y, k, z = place
+        peers = pair_peers(x, y, k, z)
+        near = list(peers) + line_peers(sz.ctx, x, y, k, z) + [at(x, y, 1 - k, z)]
+        if cores:
+            near.append(at(x, 1 - y, 1 - k, z))
+        meet(sz, place, near, [peers[0], peers[2]], jobs)
+        own, later = (jobs[:count], jobs[count:])
+        first.body(ins[:a], outs[:b], scratch[:c], own, place)
+        second.body(link(outs[:b], ins[a:], own, later), outs[b:], scratch[c:], later, place, own)
+
+    results, extra = run_call(
+        body,
+        first.ins + second.ins,
+        first.outs + second.outs,
+        first.scratch + second.scratch,
+        list(first_jobs) + list(second_jobs),
+        collective_id,
+        name,
+    )
+    return (results[:b], results[b:], extra[:count], extra[count:])
+
+
+def alone(sz, part, jobs, meeting, collective_id, name):
+    def body(ins, outs, scratch, jobs):
+        place = where_am_i()
+        meeting(place, jobs)
+        part.body(ins, outs, scratch, jobs, place)
+        finish(jobs, place)
+
+    return run_call(body, part.ins, part.outs, part.scratch, jobs, collective_id, name)
+
+
 def gather_pair(buffer, place, send, recv):
     x, y, k, z = place
     own = buffer.at[2 * x + y]
@@ -1638,24 +1735,25 @@
     return copies
 
 
-def meet_pair(sz, place, jobs):
+def meet_pair(sz, place, jobs, cores=False):
     x, y, k, z = place
     peers = pair_peers(x, y, k, z)
-    meet(sz, place, list(peers) + line_peers(sz.ctx, x, y, k, z), [peers[0], peers[2]], jobs)
-
-
-def attend(sz, section, x_own, gain, bias, watt, tables, qpos, kpos, jobs):
+    near = list(peers) + line_peers(sz.ctx, x, y, k, z)
+    if cores:
+        near += [at(x, y, 1 - k, z), at(x, 1 - y, 1 - k, z)]
+    meet(sz, place, near, [peers[0], peers[2]], jobs)
+
+
+def attend(sz, x_own, gain, bias, watt, tables, qpos, kpos):
     n, rows = sz.ctx, 4 * sz.rows
 
-    def body(ins, outs, scratch, jobs):
+    def body(ins, outs, scratch, jobs, place):
         x_ref, gain, bias, watt, cosine, sine, qpos, kpos = ins
         h1_out, n1_all, q_out, kv_all, o_out, lse_out = outs
         w, parts, landed, w_sem, s_in, r_in, s_kv, r_kv, s_back, r_back = scratch
-        place = where_am_i()
         x, y, k, z = place
         load = pltpu.make_async_copy(watt, w, w_sem)
         load.start()
-        meet_pair(sz, place, jobs)
         group = 2 * x + y
         values = x_ref[...].astype(F32)
         n1_all[group] = (values * row_norm(values) * gain[...]).astype(BF)
@@ -1707,7 +1805,6 @@
         h1_out[...] = out
         for copy in back:
             copy.wait_send()
-        finish(jobs, place)
 
     shapes = (
         jax.ShapeDtypeStruct((sz.rows, sz.width), F32),
@@ -1731,35 +1828,27 @@
         DMA((3,)),
         DMA((3,)),
     ]
-    return run_call(
-        body,
-        list(zip(arrays, specs)),
-        [(shape, vmem()) for shape in shapes],
-        scratch,
-        jobs,
-        3 + section,
-        "attend_forward",
-    )
-
-
-def attend_back(sz, section, dh1, x_own, gain, watt, tables, qpos, kpos, kept, jobs):
+    return Part(body, list(zip(arrays, specs)), [(shape, vmem()) for shape in shapes], scratch)
+
+
+def attend_back(sz, dh1, x_own, gain, watt, tables, qpos, kpos, kept, part_later=False):
     n, rows = sz.ctx, 4 * sz.rows
 
-    def body(ins, outs, scratch, jobs):
+    def body(ins, outs, scratch, jobs, place):
         dh1, x_ref, gain, watt, cosine, sine, qpos, kpos, n1_all, q_in, kv_all, o_in, lse_in = ins
         dx_out, dw_out, gain_grad, bias_grad = outs
         w, dh_all, dkv, dkv_in, da, parts, landed, w_sem, s_in, r_in, s_kv, r_kv, s_back, r_back = scratch
-        place = where_am_i()
         x, y, k, z = place
         load = pltpu.make_async_copy(watt, w, w_sem)
         load.start()
-        meet_pair(sz, place, jobs)
         group = 2 * x + y
         dh_all[group] = dh1[...].astype(BF)
         copies = gather_pair(dh_all, place, s_in, r_in)
         jobs[0].begin(place)
         load.wait()
         gathered_pair(dh_all, place, copies, r_in)
+        for job in jobs[2:]:
+            job.begin(place)
         dh = dh_all[...].reshape(rows, sz.width)
         dout = mm(dh, w[:, sz.acols :]).astype(BF)
         keys = kv_all[:, :, : sz.kcols].reshape(n * rows, sz.kcols)
@@ -1795,7 +1884,7 @@
                 )
             )
             kv_copies[-1].start()
-        jobs[1].begin(place)
+        jobs[1].begin(place, (1,) if part_later else None)
         dw_out[:, sz.acols :] = mm(dh, o_in[...].astype(BF), TN).astype(BF)
         total = dkv[z].astype(F32)
         for step in range(n - 1):
@@ -1823,7 +1912,6 @@
         gain_grad[...] = jnp.sum(dn1 * values * inverse, axis=0, keepdims=True)
         for copy in back:
             copy.wait_send()
-        finish(jobs, place)
 
     shapes = (
         jax.ShapeDtypeStruct((sz.rows, sz.width), BF),
@@ -1849,15 +1937,7 @@
         DMA((3,)),
         DMA((3,)),
     ]
-    return run_call(
-        body,
-        list(zip(arrays, specs)),
-        [(shape, vmem()) for shape in shapes],
-        scratch,
-        jobs,
-        5 + section,
-        "attend_backward",
-    )
+    return Part(body, list(zip(arrays, specs)), [(shape, vmem()) for shape in shapes], scratch)
 
 
 class HiddenWeights:
@@ -1867,167 +1947,206 @@
         self.more = has_more(sz, x * sz.group + (y * 2 + k) * sz.ctx + z)
         self.wide = sz.least * HB
 
-    def copies(self, offset, width, kind):
+    def copies(self, offset, width, kind, parts):
         cols = pl.ds(offset, width)
         return [
             pltpu.make_async_copy(
                 self.sources[part].at[:, cols], self.w.at[part, :, cols], self.sems.at[kind, part]
             )
-            for part in range(3)
+            for part in parts
         ]
 
-    def start(self):
-        for copy in self.copies(0, self.wide, 0):
+    def start(self, parts=(0, 1, 2)):
+        for copy in self.copies(0, self.wide, 0, parts):
             copy.start()
         if self.sz.extra:
 
             @pl.when(self.more)
             def _():
-                for copy in self.copies(self.wide, HB, 1):
+                for copy in self.copies(self.wide, HB, 1, parts):
                     copy.start()
 
             @pl.when(jnp.logical_not(self.more))
             def _():
-                self.w[:, :, self.wide :] = jnp.zeros((3, self.sz.width, HB), BF)
-
-    def wait(self):
-        for copy in self.copies(0, self.wide, 0):
+                for part in parts:
+                    self.w[part, :, self.wide :] = jnp.zeros((self.sz.width, HB), BF)
+
+    def wait(self, parts=(0, 1, 2)):
+        for copy in self.copies(0, self.wide, 0, parts):
             copy.wait()
         if self.sz.extra:
 
             @pl.when(self.more)
             def _():
-                for copy in self.copies(self.wide, HB, 1):
+                for copy in self.copies(self.wide, HB, 1, parts):
                     copy.wait()
 
 
-def meet_tree(sz, place, jobs, diagonal=False):
-    x, y, k, z = place
-    peers = tree_peers(sz.ctx, x, y, k, z)
-    if diagonal:
-        peers.append(at(1 - x, 1 - y, k, z))
-    meet(sz, place, peers, peers[:1], jobs)
-
-
-def feed(sz, section, h1, gain, weights, jobs):
+def halves(n, rows, gathered, place, refs):
+    count = len(Gather.scratch(n)) + len(Scatter.scratch(n, rows, 0))
+    made = []
+    for chunk in range(CHUNKS):
+        own = refs[chunk * count : (chunk + 1) * count]
+        made.append(
+            (Gather(n, rows, gathered.at[chunk], place, own[:12]), Scatter(n, rows, place, own[12:]))
+        )
+    return made
+
+
+def halves_scratch(n, rows, width):
+    return (Gather.scratch(n) + Scatter.scratch(n, rows, width)) * CHUNKS
+
+
+def feed(sz, gain, gate):
     n = sz.ctx
-
-    def body(ins, outs, scratch, jobs):
+    rows = sz.rows // CHUNKS
+
+    def body(ins, outs, scratch, jobs, place, pending):
         h1, gain, *sources = ins
-        act_out, n2_all, gate_out, up_out, hm_out = outs
-        w, w_sems, *refs = scratch
-        place = where_am_i()
+        act_out, *kept_out = outs
+        w, n2_all, gate_out, up_out, hm_out, w_sems, kept_sems, *refs = scratch
         x, y, k, z = place
         hidden_weights = HiddenWeights(sz, place, sources, w, w_sems)
-        hidden_weights.start()
-        meet_tree(sz, place, jobs)
-        gather = Gather(n, sz.rows, n2_all, place, refs[:12])
-        scatter = Scatter(n, sz.rows, place, refs[12:])
+        pairs = halves(n, rows, n2_all, place, refs)
         values = h1[...]
-        n2_all[k, gather.groups[0], z] = (values * row_norm(values) * gain[...]).astype(BF)
-        gather.begin()
-        begin(jobs[:1], place)
-        begin(jobs[1:], place, 0.0, 0.75)
-        hidden_weights.wait()
-        rows = n * sz.rows
-
-        def column(core, which):
-            group = gather.groups[which]
-            normed = n2_all[core, group].reshape(rows, sz.width)
+        normed = (values * row_norm(values) * gain[...]).astype(BF)
+        for chunk in range(CHUNKS):
+            n2_all[chunk, k, 2 * x + y, z] = normed[chunk * rows : (chunk + 1) * rows]
+
+        def columns(chunk):
+            gather, scatter = pairs[chunk]
+
+            def column(core, which):
+                group = gather.groups[which]
+                normed = n2_all[chunk, core, group].reshape(n * rows, sz.width)
+                gate = mm(normed, w[0])
+                up = mm(normed, w[1])
+                hidden = (gate * jax.nn.sigmoid(gate) * up).astype(BF)
+                gate_out[chunk, core, group] = gate.astype(BF)
+                up_out[chunk, core, group] = up.astype(BF)
+                hm_out[chunk, core, group] = hidden
+                scatter.parts[core, group] = (
+                    mm(hidden, w[2], NT).astype(BF).reshape(n, rows, sz.width)
+                )
+                if core is not k:
+                    scatter.core(which).start()
+
+            return gather.stages(column, scatter.early) + scatter.stages()
+
+        def started():
+            for job in jobs[:1]:
+                job.begin(place)
+            begin(jobs[1:], place, 0.0, 0.75)
+            finish(pending, place)
+            hidden_weights.start()
+            hidden_weights.wait()
+
+        keep = [
+            pltpu.make_async_copy(source, target, kept_sems.at[i])
+            for i, (source, target) in enumerate(zip((n2_all, gate_out, up_out, hm_out), kept_out))
+        ]
+
+        def later():
+            for copy in keep:
+                copy.start()
+            begin(jobs[1:], place, 0.75, 1.0)
+            middle(jobs, place)
+
+        run_together(columns(0), columns(1), {(B, 0): started, (B, 8): later})
+        for chunk, (gather, scatter) in enumerate(pairs):
+            span = slice(chunk * rows, (chunk + 1) * rows)
+            act_out[span] = (values[span] + scatter.result()).astype(BF)
+        for gather, scatter in pairs:
+            gather.finish()
+            scatter.finish()
+        for copy in keep:
+            copy.wait()
+        finish(jobs, place)
+
+    kept = jax.ShapeDtypeStruct((CHUNKS, 2, 4, n * rows, sz.hidden), BF)
+    shapes = (
+        jax.ShapeDtypeStruct((sz.rows, sz.width), BF),
+        jax.ShapeDtypeStruct((CHUNKS, 2, 4, n, rows, sz.width), BF),
+        kept,
+        kept,
+        kept,
+    )
+    scratch = [pltpu.VMEM((3, sz.width, sz.hidden), BF)]
+    scratch += [pltpu.VMEM(shape.shape, BF) for shape in shapes[1:]]
+    scratch += [DMA((2, 3)), DMA((4,))] + halves_scratch(n, rows, sz.width)
+    outs = [(shape, hbm() if i else vmem()) for i, shape in enumerate(shapes)]
+    return Part(body, [(gain, vmem()), (gate, hbm())], outs, scratch)
+
+
+def both(sz, dy, gain, gate):
+    n, rows = sz.ctx, sz.rows
+
+    def body(ins, outs, scratch, jobs, place, pending):
+        dy, h1, gain, *sources = ins
+        act_out, dh1_out, dw_out, gain_grad = outs
+        w, n2_all, dy_all, gate_all, up_all, hm_all, w_sems, *refs = scratch
+        x, y, k, z = place
+        hidden_weights = HiddenWeights(sz, place, sources, w, w_sems)
+        count = len(refs) // 2
+        (gather_f, scatter_f), (gather_b, scatter_b) = [
+            (Gather(n, rows, buffer, place, own[:12]), Scatter(n, rows, place, own[12:]))
+            for buffer, own in ((n2_all, refs[:count]), (dy_all, refs[count:]))
+        ]
+        values = h1[...]
+        inverse = row_norm(values)
+        n2_all[k, 2 * x + y, z] = (values * inverse * gain[...]).astype(BF)
+        dy_all[k, 2 * x + y, z] = dy[...]
+
+        waiting = []
+
+        def down_product(core, which):
+            group = gather_f.groups[which]
+            partial = mm(hm_all[core, group], w[2], NT)
+            scatter_f.parts[core, group] = partial.astype(BF).reshape(n, rows, sz.width)
+            if core is not k:
+                scatter_f.core(which).start()
+
+        def down_here():
+            nonlocal waiting
+            finish(jobs, place)
+            hidden_weights.start((2,))
+            hidden_weights.wait((2,))
+            for core, which in waiting:
+                down_product(core, which)
+            waiting = None
+
+        def forward(core, which):
+            group = gather_f.groups[which]
+            normed = n2_all[core, group].reshape(n * rows, sz.width)
             gate = mm(normed, w[0])
             up = mm(normed, w[1])
             hidden = (gate * jax.nn.sigmoid(gate) * up).astype(BF)
-            gate_out[core, group] = gate.astype(BF)
-            up_out[core, group] = up.astype(BF)
-            hm_out[core, group] = hidden
-            scatter.parts[core, group] = (
-                mm(hidden, w[2], NT).astype(BF).reshape(n, sz.rows, sz.width)
-            )
-            if core is not k:
-                scatter.core(which).start()
-
-        gather.run(column, scatter.early)
-
-        def later():
-            begin(jobs[1:], place, 0.75, 1.0)
-            middle(jobs, place)
-
-        result = scatter.run((later,))
-        act_out[...] = (values + result).astype(BF)
-        gather.finish()
-        scatter.finish()
-        finish(jobs, place)
-
-    kept = jax.ShapeDtypeStruct((2, 4, n * sz.rows, sz.hidden), BF)
-    shapes = (
-        jax.ShapeDtypeStruct((sz.rows, sz.width), BF),
-        jax.ShapeDtypeStruct((2, 4, n, sz.rows, sz.width), BF),
-        kept,
-        kept,
-        kept,
-    )
-    scratch = (
-        [pltpu.VMEM((3, sz.width, sz.hidden), BF), DMA((2, 3))]
-        + Gather.scratch(n)
-        + Scatter.scratch(n, sz.rows, sz.width)
-    )
-    return run_call(
-        body,
-        [(h1, vmem()), (gain, vmem())] + [(w, hbm()) for w in weights],
-        [(shape, vmem()) for shape in shapes],
-        scratch,
-        jobs,
-        7 + section,
-        "feed_forward",
-    )
-
-
-def feed_back(sz, section, dy, h1, gain, weights, kept, jobs):
-    n = sz.ctx
-
-    def body(ins, outs, scratch, jobs):
-        dy, h1, gain, *sources = ins[:6]
-        n2_all, gate_in, up_in, hm_in = ins[6:]
-        dh1_out, dw_out, gain_grad = outs
-        w, dy_all, dgate_all, dup_all, w_sems, *refs = scratch
-        place = where_am_i()
-        x, y, k, z = place
-        hidden_weights = HiddenWeights(sz, place, sources, w, w_sems)
-        hidden_weights.start()
-        meet_tree(sz, place, jobs, len(jobs) > 1)
-        gather = Gather(n, sz.rows, dy_all, place, refs[:12])
-        scatter = Scatter(n, sz.rows, place, refs[12:])
-        dy_all[k, gather.groups[0], z] = dy[...]
-        gather.begin()
-        down_share, *heads = jobs
-        down_share.source = dw_out
-        for job in heads:
-            job.begin(place)
-        hidden_weights.wait()
-        for job in heads:
-            job.middle(place)
-        rows = n * sz.rows
-
-        def column(core, which):
-            group = gather.groups[which]
-            dhidden = mm(dy_all[core, group].reshape(rows, sz.width), w[2])
-            gate = gate_in[core, group].astype(F32)
-            up = up_in[core, group].astype(F32)
+            gate_all[core, group] = gate.astype(BF)
+            up_all[core, group] = up.astype(BF)
+            hm_all[core, group] = hidden
+            if waiting is None:
+                down_product(core, which)
+            else:
+                waiting.append((core, which))
+
+        def backward(core, which):
+            group = gather_b.groups[which]
+            dhidden = mm(dy_all[core, group].reshape(n * rows, sz.width), w[2])
+            gate = gate_all[core, group].astype(F32)
+            up = up_all[core, group].astype(F32)
             sigmoid = jax.nn.sigmoid(gate)
             dgate = (dhidden * up * sigmoid * (1.0 + gate * (1.0 - sigmoid))).astype(BF)
             dup = (dhidden * gate * sigmoid).astype(BF)
-            dgate_all[core, group] = dgate
-            dup_all[core, group] = dup
+            gate_all[core, group] = dgate
+            up_all[core, group] = dup
             partial = mm(dgate, w[0], NT) + mm(dup, w[1], NT)
-            scatter.parts[core, group] = partial.astype(BF).reshape(n, sz.rows, sz.width)
+            scatter_b.parts[core, group] = partial.astype(BF).reshape(n, rows, sz.width)
             if core is not k:
-                scatter.core(which).start()
-
-        gather.run(column, scatter.early)
-        total = 8 * rows
-        tile = 256 if sz.width % 256 == 0 else 128
+                scatter_b.core(which).start()
 
         def weight_grad(slot, left, right):
+            total = 8 * n * rows
+            tile = 256 if sz.width % 256 == 0 else 128
             grads = right[...].reshape(total, sz.hidden)
 
             @pl.loop(0, sz.width // tile)
@@ -2036,16 +2155,28 @@
                 side = left[:, :, :, :, cols].reshape(total, tile)
                 dw_out[slot, cols] = mm(side, grads, TN).astype(BF)
 
-        def down_first():
-            weight_grad(2, dy_all, hm_in)
-            down_share.begin(place)
-
-        def last():
-            weight_grad(1, n2_all, dup_all)
-            for job in heads:
-                job.late(place)
-
-        dn2 = scatter.run((down_first, lambda: weight_grad(0, n2_all, dgate_all), last))
+        def result():
+            act_out[...] = (h1[...] + scatter_f.result()).astype(BF)
+
+        def started():
+            finish(pending, place)
+            hidden_weights.start((0, 1))
+            hidden_weights.wait((0, 1))
+
+        run_together(
+            gather_f.stages(forward, scatter_f.early) + scatter_f.stages(),
+            gather_b.stages(backward, scatter_b.early) + scatter_b.stages(),
+            {
+                (A, 0): lambda: begin(jobs, place),
+                (B, 0): started,
+                (A, 5): down_here,
+                (B, 8): lambda: weight_grad(2, dy_all, hm_all),
+                (B, 9): lambda: weight_grad(0, n2_all, gate_all),
+                (B, 10): lambda: weight_grad(1, n2_all, up_all),
+            },
+        )
+        result()
+        dn2 = scatter_b.result()
         values = h1[...]
         inverse = row_norm(values)
         weighted = dn2 * gain[...]
@@ -2054,8 +2185,132 @@
             dy[...].astype(F32) + inverse * weighted - values * (inverse * inverse * inverse) * inner
         )
         gain_grad[...] = jnp.sum(dn2 * values * inverse, axis=0, keepdims=True)
-        gather.finish()
-        scatter.finish()
+        for job in (gather_f, scatter_f, gather_b, scatter_b):
+            job.finish()
+
+    shapes = (
+        jax.ShapeDtypeStruct((sz.rows, sz.width), BF),
+        jax.ShapeDtypeStruct((sz.rows, sz.width), F32),
+        jax.ShapeDtypeStruct((3, sz.width, sz.hidden), BF),
+        jax.ShapeDtypeStruct((1, sz.width), F32),
+    )
+    gathered = pltpu.VMEM((2, 4, n, rows, sz.width), BF)
+    inner = pltpu.VMEM((2, 4, n * rows, sz.hidden), BF)
+    scratch = [
+        pltpu.VMEM((3, sz.width, sz.hidden), BF),
+        gathered,
+        gathered,
+        inner,
+        inner,
+        inner,
+        DMA((2, 3)),
+    ] + (Gather.scratch(n) + Scatter.scratch(n, rows, sz.width)) * 2
+    ins = [(dy, vmem()), (gain, vmem()), (gate, hbm())]
+    return Part(body, ins, [(shape, vmem()) for shape in shapes], scratch)
+
+
+def feed_back(sz, h1, gain, weights, kept):
+    n = sz.ctx
+    rows = sz.rows // CHUNKS
+
+    def body(ins, outs, scratch, jobs, place, pending):
+        dy, h1, gain, *sources = ins[:6]
+        dh1_out, dw_out, gain_grad = outs
+        w, dy_all, dgate_all, dup_all, *scratch = scratch
+        n2_all, gate_in, up_in, hm_in, w_sems, kept_sems, *refs = scratch
+        kept = [
+            pltpu.make_async_copy(source, target, kept_sems.at[i])
+            for i, (source, target) in enumerate(zip(ins[6:], (n2_all, gate_in, up_in, hm_in)))
+        ]
+        x, y, k, z = place
+        hidden_weights = HiddenWeights(sz, place, sources, w, w_sems)
+        hidden_weights.start()
+        for copy in kept[1:] + kept[:1]:
+            copy.start()
+        pairs = halves(n, rows, dy_all, place, refs)
+        for chunk in range(CHUNKS):
+            dy_all[chunk, k, 2 * x + y, z] = dy[chunk * rows : (chunk + 1) * rows]
+        line_jobs = [job for job in jobs if isinstance(job, LineShares)]
+        heads = [job for job in jobs if isinstance(job, ReturnedHeads)]
+
+        def columns(chunk):
+            gather, scatter = pairs[chunk]
+
+            def column(core, which):
+                group = gather.groups[which]
+                dhidden = mm(dy_all[chunk, core, group].reshape(n * rows, sz.width), w[2])
+                gate = gate_in[chunk, core, group].astype(F32)
+                up = up_in[chunk, core, group].astype(F32)
+                sigmoid = jax.nn.sigmoid(gate)
+                dgate = (dhidden * up * sigmoid * (1.0 + gate * (1.0 - sigmoid))).astype(BF)
+                dup = (dhidden * gate * sigmoid).astype(BF)
+                dgate_all[chunk, core, group] = dgate
+                dup_all[chunk, core, group] = dup
+                partial = mm(dgate, w[0], NT) + mm(dup, w[1], NT)
+                scatter.parts[core, group] = partial.astype(BF).reshape(n, rows, sz.width)
+                if core is not k:
+                    scatter.core(which).start()
+
+            return gather.stages(column, scatter.early) + scatter.stages()
+
+        total = 8 * n * sz.rows
+        tile = 256 if sz.width % 256 == 0 else 128
+
+        def weight_grad(slot, left, right):
+            grads = right[...].reshape(total, sz.hidden)
+
+            @pl.loop(0, sz.width // tile)
+            def _(step):
+                cols = pl.ds(pl.multiple_of(step * tile, tile), tile)
+                side = left[:, :, :, :, :, cols].reshape(total, tile)
+                dw_out[slot, cols] = mm(side, grads, TN).astype(BF)
+
+        def started():
+            for job in heads:
+                job.begin(place)
+            pending[1].begin(place, range(2, n))
+            pending[1].begin(place, (0,))
+            for job in line_jobs:
+                job.begin(place)
+            hidden_weights.wait()
+            kept[1].wait()
+            kept[2].wait()
+            for job in heads:
+                job.middle(place)
+
+        def down_grad():
+            kept[3].wait()
+            kept[0].wait()
+            weight_grad(2, dy_all, hm_in)
+
+        def last():
+            weight_grad(1, n2_all, dup_all)
+            for job in heads:
+                job.late(place)
+
+        run_together(
+            columns(0),
+            columns(1),
+            {
+                (B, 0): started,
+                (B, 8): down_grad,
+                (B, 9): lambda: weight_grad(0, n2_all, dgate_all),
+                (B, 10): last,
+            },
+        )
+        dn2 = jnp.concatenate([scatter.result() for _, scatter in pairs], axis=0)
+        values = h1[...]
+        inverse = row_norm(values)
+        weighted = dn2 * gain[...]
+        inner = jnp.mean(weighted * values, axis=-1, keepdims=True)
+        dh1_out[...] = (
+            dy[...].astype(F32) + inverse * weighted - values * (inverse * inverse * inverse) * inner
+        )
+        gain_grad[...] = jnp.sum(dn2 * values * inverse, axis=0, keepdims=True)
+        for gather, scatter in pairs:
+            gather.finish()
+            scatter.finish()
+        finish(pending, place)
         finish(jobs, place)
 
     shapes = (
@@ -2063,47 +2318,45 @@
         jax.ShapeDtypeStruct((3, sz.width, sz.hidden), BF),
         jax.ShapeDtypeStruct((1, sz.width), F32),
     )
-    inner = pltpu.VMEM((2, 4, n * sz.rows, sz.hidden), BF)
-    scratch = (
-        [
-            pltpu.VMEM((3, sz.width, sz.hidden), BF),
-            pltpu.VMEM((2, 4, n, sz.rows, sz.width), BF),
-            inner,
-            inner,
-            DMA((2, 3)),
-        ]
-        + Gather.scratch(n)
-        + Scatter.scratch(n, sz.rows, sz.width)
-    )
-    arrays = (dy, h1, gain, *weights, *kept)
-    specs = [vmem()] * 3 + [hbm()] * 3 + [vmem()] * 4
-    return run_call(
-        body,
-        list(zip(arrays, specs)),
-        [(shape, vmem()) for shape in shapes],
-        scratch,
-        jobs,
-        9 + section,
-        "feed_backward",
-    )
-
-
-def collect(sz, small, acts, grads, shares, heads):
+    inner = pltpu.VMEM((CHUNKS, 2, 4, n * rows, sz.hidden), BF)
+    scratch = [
+        pltpu.VMEM((3, sz.width, sz.hidden), BF),
+        pltpu.VMEM((CHUNKS, 2, 4, n, rows, sz.width), BF),
+        inner,
+        inner,
+        pltpu.VMEM((CHUNKS, 2, 4, n, rows, sz.width), BF),
+        inner,
+        inner,
+        inner,
+        DMA((2, 3)),
+        DMA((4,)),
+    ] + halves_scratch(n, rows, sz.width)
+    arrays = (h1, gain, *weights, *kept)
+    specs = [vmem()] * 2 + [hbm()] * 7
+    return Part(body, list(zip(arrays, specs)), [(shape, vmem()) for shape in shapes], scratch)
+
+
+def collect(sz, small, acts, grads, shares, ready, jobs):
     n = sz.ctx
-    order = [(section, part) for part in (2, 0, 1) for section in (1, 0)]
+    order = [(0, 2), (1, 1), (0, 0)]
+    last = (0, 1)
+    early = [2, 0]
 
     def body(ins, outs, scratch, jobs):
         small, act0, act1, grad0, grad1, *shares = ins
+        shares, ready = (shares[: len(order)], shares[len(order) :])
         small_in, act_out, grad_out, w_out = outs
-        s_small, r_small, s_out, r_out, send, recv, local, s_over, r_over = scratch
-        (heads,) = jobs
+        s_small, r_small, s_out, r_out, send, recv, local, s_over, r_over, s_ready, r_ready = scratch
+        line_job, *heads = jobs
         place = where_am_i()
         x, y, k, z = place
         me = x * sz.group + (y * 2 + k) * n + z
         greet_all(me, sz.total, lambda index: flat_place(index, sz.group, n))
-        heads.begin(place)
+        line_job.begin(place)
+        for job in heads:
+            job.begin(place)
         moves = []
-        for number, (section, part) in enumerate(order):
+        for number, (section, part) in enumerate(order + [last]):
             sems = (
                 send.at[number],
                 recv.at[number],
@@ -2111,8 +2364,26 @@
                 s_over.at[number],
                 r_over.at[number],
             )
-            moves.append(PlaneShares(sz, section, part, shares[number], w_out, sems))
-            moves[-1].begin(place)
+            source = shares[number] if number < len(order) else line_job.target
+            moves.append(PlaneShares(sz, section, part, source, w_out, sems))
+        def over(number):
+            part = early[number]
+            cols = pl.ds(0, sz.plane * HB)
+            return remote(
+                ready[number].at[:, cols],
+                w_out.at[0, part, :, cols],
+                s_ready.at[number],
+                r_ready.at[number],
+                at(1 - x, y, k, z),
+            )
+
+        @pl.when(x == 0)
+        def _():
+            for number in range(len(early)):
+                over(number).start()
+
+        for move in moves[:-1]:
+            move.begin(place)
 
         @pl.loop(1, sz.total)
         def _(step):
@@ -2147,22 +2418,39 @@
                         def _():
                             pltpu.make_async_copy(source, target.at[k], r_out.at[slot, k]).start()
 
-        heads.middle(place)
-        for move in moves[:4]:
-            move.cross(place)
-        heads.late(place)
-        for move in moves[4:]:
-            move.cross(place)
+        for job in heads:
+            job.middle(place)
+        moves[0].cross(place)
+        line_job.finish(place)
+        moves[-1].begin(place)
         results(True)
+        moves[1].cross(place)
+        moves[2].cross(place)
+        heads[0].late(place)
+        moves[3].cross(place)
+        for job in heads[1:]:
+            job.late(place)
         results(False)
+
+        @pl.when(x == 0)
+        def _():
+            for number in range(len(early)):
+                over(number).wait_send()
+
+        @pl.when(x == 1)
+        def _():
+            for number in range(len(early)):
+                over(number).wait_recv()
+
         for slot, target in enumerate((act_out, grad_out)):
             for batch in range(2):
                 arrived(target.at[batch], r_out.at[slot, batch])
         arrived(small_in.at[pl.ds(0, sz.total - 1)], r_small)
         arrived(small_in, s_small)
-        heads.finish(place)
         for move in moves:
             move.finish(place)
+        for job in heads:
+            job.finish(place)
 
     shapes = (
         jax.ShapeDtypeStruct((sz.total, 8, LANES), F32),
@@ -2170,8 +2458,8 @@
         jax.ShapeDtypeStruct((2, sz.rows, sz.width), BF),
         jax.ShapeDtypeStruct((2, 3, sz.owned, sz.ff), BF),
     )
-    arrays = (small, *acts, *grads, *[shares[section][part] for section, part in order])
-    many = len(order)
+    arrays = (small, *acts, *grads, *[shares[section][part] for section, part in order], *ready)
+    many = len(order) + 1
     return run_call(
         body,
         [(array, hbm()) for array in arrays],
@@ -2186,8 +2474,10 @@
             DMA((many, 2)),
             DMA((many,)),
             DMA((many,)),
+            DMA((len(early),)),
+            DMA((len(early),)),
         ],
-        [heads],
+        jobs,
         2,
         "collect_gradients",
     )
@@ -2250,60 +2540,75 @@
     def columns(section, part):
         return Columns(sz, section, part, gate_up_weight, down_weight, cols_x)
 
-    att, gates, weights = [att0, None], [gate0, None], []
-    inputs, acts, kept_att, kept_feed, middles = [tok_own], [], [], [], []
-    for section in range(2):
-        (h1, *kept), ((up,), (down,)) = attend(
-            sz,
-            section,
-            inputs[section],
-            gain1[section],
-            own_bias[section],
-            att[section],
-            tables,
-            qpos,
-            kpos,
-            [columns(section, 1), columns(section, 2)],
+    def attention(section, x_own, watt):
+        return attend(sz, x_own, gain1[section], own_bias[section], watt, tables, qpos, kpos)
+
+    (mid0, *kept_att0), (act0, *kept_feed), ((up0,), (down0,)), ((att1,), (gate1,)) = joined(
+        sz,
+        attention(0, tok_own, att0),
+        [columns(0, 1), columns(0, 2)],
+        feed(sz, gain2[0], gate0),
+        [Heads(sz, 1, qkv_weight, out_weight, heads_x), columns(1, 0)],
+        lambda made, given, own, later: (made[0], *given, own[0].target, own[1].target),
+        False,
+        3,
+        "layer_forward",
+    )
+    (_, *kept_att1), (act1, dh1, dw1, gain2_grad1), _, _ = joined(
+        sz,
+        attention(1, act0, att1),
+        [columns(1, 1)],
+        both(sz, cot_own, gain2[1], gate1),
+        [columns(1, 2)],
+        lambda made, given, own, later: (given[0], made[0], *given[1:], own[0].target, later[0].target),
+        False,
+        4,
+        "layer_turn",
+    )
+    acts = [act0, act1]
+
+    def attention_back(section, dh1, x_own, watt, kept):
+        return attend_back(
+            sz, dh1, x_own, gain1[section], watt, tables, qpos, kpos, kept, part_later=section == 1
         )
-        kept_att.append(kept)
-        middles.append(h1)
-        weights.append((gates[section], up, down))
-        jobs = []
-        if section == 0:
-            jobs = [Heads(sz, 1, qkv_weight, out_weight, heads_x), columns(1, 0)]
-        (act, *kept), more = feed(sz, section, h1, gain2[section], weights[section], jobs)
-        if section == 0:
-            (att[1],), (gates[1],) = more
-        kept_feed.append(kept)
-        acts.append(act)
-        inputs.append(act)
-    grads, das, smalls = [None, None], [None, None], [None, None]
-    shares = [[None] * 3, [None] * 3]
-    came_heads = [None, None]
-    dy = cot_own
-    for section in (1, 0):
-        jobs = [LineShares(sz, 2)]
-        if section == 0:
-            jobs.append(ReturnedHeads(sz, 1, das[1]))
-        (dh1, dw, gain2_grad), ((shares[section][2],), *more) = feed_back(
-            sz, section, dy, middles[section], gain2[section], weights[section], kept_feed[section], jobs
-        )
-        if section == 0:
-            ((came_heads[1],),) = more
-        (dy, das[section], gain1_grad, bias_grad), ((shares[section][0],), (shares[section][1],)) = attend_back(
-            sz,
-            section,
-            dh1,
-            inputs[section],
-            gain1[section],
-            att[section],
-            tables,
-            qpos,
-            kpos,
-            kept_att[section],
-            [LineShares(sz, 0, dw), LineShares(sz, 1, dw)],
-        )
-        grads[section] = dy
+
+    def heads_linked(made, given, own, later):
+        later[1].source = made[1]
+        return (made[0], *given)
+
+    (
+        (grad1, da1, gain1_grad1, bias_grad1),
+        (dh1, dw0, gain2_grad0),
+        ((down_share1,), (gate_share1,)),
+        ((up_share1,), (heads10,)),
+    ) = joined(
+        sz,
+        attention_back(1, dh1, act0, att1, kept_att1),
+        [LineShares(sz, 2, dw1), LineShares(sz, 0, dw1)],
+        feed_back(sz, mid0, gain2[0], (gate0, up0, down0), kept_feed),
+        [LineShares(sz, 1, dw1), ReturnedHeads(sz, 1, 0, None)],
+        heads_linked,
+        False,
+        5,
+        "layer_backward",
+    )
+    (grad0, da0, gain1_grad0, bias_grad0), ((down_share0,), (gate_share0,), *ready) = alone(
+        sz,
+        attention_back(0, dh1, tok_own, att0, kept_att0),
+        [LineShares(sz, 2, dw0), LineShares(sz, 0, dw0)]
+        + [ReadyShares(sz, 1, part, share) for part, share in ((2, down_share1), (0, gate_share1))],
+        lambda place, jobs: meet_pair(sz, place, jobs, True),
+        6,
+        "attend_backward",
+    )
+    grads = [grad0, grad1]
+    shares = [[gate_share0, None, down_share0], [gate_share1, up_share1, down_share1]]
+    came_heads = [[None, None], [heads10, None]]
+    smalls = []
+    for gain1_grad, gain2_grad, bias_grad in (
+        (gain1_grad0, gain2_grad0, bias_grad0),
+        (gain1_grad1, gain2_grad1, bias_grad1),
+    ):
         whole_bias = jnp.zeros((1, query_columns + 2 * key_columns), F32)
         offset = 0
         for start, size in starts:
@@ -2314,15 +2619,24 @@
         split = query_columns + key_columns
         rows = [gain1_grad, gain2_grad, whole_bias[:, :split], whole_bias[:, split:]]
         rows = [line(row.reshape(group, -1))[:, None] for row in rows]
-        smalls[section] = jnp.concatenate(rows + [jnp.zeros((group, 4, LANES), F32)], axis=1)
+        smalls.append(jnp.concatenate(rows + [jnp.zeros((group, 4, LANES), F32)], axis=1))
     small_out = jnp.concatenate(smalls, axis=0)
-    (small_in, act_out, grad_out, w_out), ((came_heads[0],),) = collect(
-        sz, small_out, acts, grads, shares, ReturnedHeads(sz, 0, das[0])
-    )
+    jobs = [LineShares(sz, 1, dw0)]
+    jobs += [
+        ReturnedHeads(sz, section, part, da) for section, part, da in ((1, 1, da1), (0, 0, da0), (0, 1, da0))
+    ]
+    (small_in, act_out, grad_out, w_out), more = collect(
+        sz, small_out, acts, grads, shares, [array for (array,) in ready], jobs
+    )
+    (came_heads[1][1],), (came_heads[0][0],), (came_heads[0][1],) = more[1:]
     small_sum = jnp.sum(small_in, axis=0)
-    gate_up_grad = jnp.concatenate([w_out[0, 0], w_out[0, 1]], axis=1).astype(F32)[None]
-    down_grad = w_out[0, 2].astype(F32)[None]
-    att_sum = jnp.where(x == 0, came_heads[0], came_heads[1]).astype(F32)
+    here = jnp.logical_and(x == 1, jnp.arange(sz.ff) >= sz.plane * HB)
+    (down_ready,), (gate_ready,) = ready
+    gate = jnp.where(here, gate_ready, w_out[0, 0])
+    gate_up_grad = jnp.concatenate([gate, w_out[0, 1]], axis=1).astype(F32)[None]
+    down_grad = jnp.where(here, down_ready, w_out[0, 2]).astype(F32)[None]
+    by_y = [jnp.where(y == 0, parts[0], parts[1]) for parts in came_heads]
+    att_sum = jnp.where(x == 0, by_y[0], by_y[1]).astype(F32)
     q_grad = att_sum[:, :, : sz.qcols].transpose(1, 0, 2).reshape(sz.owned, query_columns)
     kv_grad = jnp.sum(
         att_sum[:, :, sz.qcols : sz.acols].reshape(

time: 839 us -> 753 us (0.90)
  Pallas kernels: 801 us -> 713 us
    pallas_call x10 -> x6, Pallas kernels: 801 us -> 713 us  [run_call(): pl.pallas_call(kernel, out_shape=tuple((shape for shape, _ in outs)), in_...]
where the time goes in v4:
time: 753 us; the launch traced here: 744 us
  Pallas kernels  713 us (95%)
  local copies, waits for them, and re-layouts  14.9 us (2%)
  other arithmetic  14.2 us (2%)
    pallas_call x6, Pallas kernels, run_call(): pl.pallas_call(kernel, out_shape=tuple((shape for shape, _ in outs)), in_...  713 us

profile of v4, /device:TPU:14, one launch (start us, length us, event | category | flops | bytes accessed | tf_op | source)
XLA Modules:
  0.0 743.6 jit_solution(14201036373718165962)
XLA Ops:
  0.7 0.1 pad.58.clone
  0.8 1.4 fusion.8.refs_0_
  2.1 71.0 %spread_weights.1 = (bf16[32,16,128]{2,1,0:T(8,128)(2,1)}, bf16[64,1536]{1,0:T(8,128)(2,1)}, bf16[64,1536]{1,0:T(8,128)(2,1)}, bf16[2,96,1024]{2,1,0:T(8,128)(2,...) custom-call(bf16[16,128]{1,0:T(8,128)(2,1)} %fusion.8.refs_0_, ...), custom_call_target="tpu_custom_call" | custom-call | tf_op jit(solution)/shard_map/spread_weights/pallas_call | solution.py:690
  73.2 0.9 bitcast_convert_fusion.1
  74.2 0.6 slice_bitcast_fusion.3
  74.9 0.1 reshape.131
  75.0 0.1 convert_element_type.54
  75.1 0.1 broadcast_multiply_fusion
  75.2 1.2 sine_multiply_fusion
  76.5 0.8 reshape.148.refs_6_
  77.3 0.7 reshape.133.refs_7_
  78.0 0.7 squeeze.48.refs_1_.refs_2_
  78.6 0.7 squeeze.50.refs_8_.refs_14_
  79.3 149.8 %layer_forward.1 = (f32[64,1536]{1,0:T(8,128)}, bf16[4,64,1536]{2,1,0:T(8,128)(2,1)}, bf16[256,384]{1,0:T(8,128)(2,1)}, bf16[4,256,256]{2,1,0:T(8,128)(2,1)}, f3...) custom-call(bf16[64,1536]{1,0:T(8,128)(2,1)} %get-tuple-element.67.r, ...), custom_call_target="tpu_custom_call" | custom-call | tf_op jit(solution)/shard_map/layer_forward/pallas_call | solution.py:690
  229.1 0.7 squeeze.51.refs_1_.refs_2_
  229.8 0.7 squeeze.53.refs_9_
  230.5 193.8 %layer_turn.1 = (f32[64,1536]{1,0:T(8,128)}, bf16[4,64,1536]{2,1,0:T(8,128)(2,1)}, bf16[256,384]{1,0:T(8,128)(2,1)}, bf16[4,256,256]{2,1,0:T(8,128)(2,1)}, f32[2...) custom-call(bf16[64,1536]{1,0:T(8,128)(2,1)} %get-tuple-element.73.r, ...), custom_call_target="tpu_custom_call" | custom-call | tf_op jit(solution)/shard_map/layer_turn/pallas_call | solution.py:690
  424.3 142.3 %layer_backward.1 = (bf16[64,1536]{1,0:T(8,128)(2,1)}, bf16[1536,1024]{1,0:T(8,128)(2,1)}, f32[1,1536]{1,0:T(1,128)}, f32[1,640]{1,0:T(1,128)}, f32[64,1536]{1,0...) custom-call(f32[64,1536]{1,0:T(8,128)} %get-tuple-element.77.refs_0_, ...), custom_call_target="tpu_custom_call" | custom-call | tf_op jit(solution)/shard_map/layer_backward/pallas_call | solution.py:690
  566.7 61.9 %attend_backward.1 = (bf16[64,1536]{1,0:T(8,128)(2,1)}, bf16[1536,1024]{1,0:T(8,128)(2,1)}, f32[1,1536]{1,0:T(1,128)}, f32[1,640]{1,0:T(1,128)}, bf16[4,4,96,384...) custom-call(f32[64,1536]{1,0:T(8,128)} %get-tuple-element.91.refs_0_, ...), custom_call_target="tpu_custom_call" | custom-call | tf_op jit(solution)/shard_map/attend_backward/pallas_call | solution.py:690
  628.6 0.7 constant_dynamic-update-slice_fusion.5
  629.3 0.7 constant_dynamic-update-slice_fusion.4
  630.0 0.6 constant_dynamic-update-slice_fusion.3
  630.6 0.1 reshape.136
  630.8 0.1 reshape.137
  630.9 0.7 reduce.4
  631.8 0.1 concatenate.38
  631.9 0.1 reshape.141
  632.0 0.1 reshape.140
  632.3 0.1 concatenate.39
  632.4 0.7 pad_maximum_fusion.1.refs_0_
  633.1 94.0 %collect_gradients.1 = (f32[32,8,128]{2,1,0:T(8,128)}, bf16[2,64,1536]{2,1,0:T(8,128)(2,1)}, bf16[2,64,1536]{2,1,0:T(8,128)(2,1)}, bf16[2,3,96,8960]{3,2,1,0:T(8...) custom-call(f32[32,8,128]{2,1,0:T(8,128)} %pad_maximum_fusion.1.refs, ...), custom_call_target="tpu_custom_call" | custom-call | tf_op jit(solution)/shard_map/collect_gradients/pallas_call | solution.py:690
  727.1 4.2 bitcast_convert_fusion
  731.3 1.6 slice_bitcast_fusion
  732.9 3.5 maximum_convert_fusion
  736.4 0.2 select_convert_fusion
  736.6 0.1 slice_bitcast_fusion.1
  736.8 0.2 reshape.143
  737.0 0.3 reduce_sum.19
  737.3 0.2 copy.56
  737.5 0.2 reshape.144
  737.7 0.9 maximum_bitcast_fusion
  738.6 0.4 copy.57
  739.0 1.1 reshape.145
  740.1 0.5 fusion.11
  740.6 0.5 slice.112
  741.1 0.5 slice.113
  741.6 0.7 copy.81
  742.4 0.7 copy.82
  (71 shorter events, 0.9 us)
Async XLA Ops:
  0.6 74.2 %copy-start = (s32[2,1024]{1,0:T(2,128)S(1)}, s32[2,1024]{1,0:T(2,128)}, u32[]{:S(2)}) copy-start(s32[2,1024]{1,0:T(2,128)} %param.11) | copy-start | bytes 24580
  566.6 64.1 %copy-start.14 = (f32[1,640]{1,0:T(1,128)S(1)}, f32[1,640]{1,0:T(1,128)}, u32[]{:S(2)}) copy-start(f32[1,640]{1,0:T(1,128)} %get-tuple-element.105) | copy-start | bytes 7684
  566.6 65.1 %copy-start.13 = (f32[1,1536]{1,0:T(1,128)S(1)}, f32[1,1536]{1,0:T(1,128)}, u32[]{:S(2)}) copy-start(f32[1,1536]{1,0:T(1,128)} %get-tuple-element.101) | copy-start | bytes 18436
  566.6 65.5 %copy-start.12 = (f32[1,1536]{1,0:T(1,128)S(1)}, f32[1,1536]{1,0:T(1,128)}, u32[]{:S(2)}) copy-start(f32[1,1536]{1,0:T(1,128)} %get-tuple-element.103) | copy-start | bytes 18436
  566.6 65.6 %copy-start.11 = (f32[1,1536]{1,0:T(1,128)S(1)}, f32[1,1536]{1,0:T(1,128)}, u32[]{:S(2)}) copy-start(f32[1,1536]{1,0:T(1,128)} %get-tuple-element.104) | copy-start | bytes 18436
  633.1 94.0 %copy-start.2 = (bf16[96,8960]{1,0:T(8,128)(2,1)S(1)}, bf16[96,8960]{1,0:T(8,128)(2,1)}, u32[]{:S(2)}) copy-start(bf16[96,8960]{1,0:T(8,128)(2,1)} %get-tuple-element.112.refs_8_) | copy-start | bytes 5160964
  633.1 94.0 %copy-start.3 = (bf16[96,8960]{1,0:T(8,128)(2,1)S(1)}, bf16[96,8960]{1,0:T(8,128)(2,1)}, u32[]{:S(2)}) copy-start(bf16[96,8960]{1,0:T(8,128)(2,1)} %get-tuple-element.113.refs_9_) | copy-start | bytes 5160964
  732.9 3.5 copy-start.4
  732.9 3.5 copy-start.5
  732.9 3.5 copy-start.6
  732.9 3.5 copy-start.7
  737.6 2.4 copy-start.10
  737.6 4.0 copy-start.9
  738.6 3.8 copy-start.8
  738.6 4.5 copy-start.1

commit v5 on v4

--- a/solution.py
+++ b/solution.py
@@ -814,6 +814,27 @@
     )
 
 
+RELAYED = 4
+
+
+def ends(n, z, ctx):
+    if n != RELAYED:
+        return z < 0
+    return jnp.abs(z - ctx) == n - 1
+
+
+def relay_of(n, z, ctx):
+    if n != RELAYED:
+        return z < 0
+    return jnp.logical_or(
+        jnp.logical_and(z == 0, ctx == n - 2), jnp.logical_and(z == n - 1, ctx == 1)
+    )
+
+
+def inner(n, z):
+    return jnp.logical_and(z > 0, z < n - 1)
+
+
 class Heads:
     reach = 1
 
@@ -821,12 +842,12 @@
         self.sz, self.section = sz, section
         self.ins = [(qkv, None), (out_w, None), (staged, None)]
         self.outs = [jax.ShapeDtypeStruct((sz.width, sz.atot), BF)]
-        self.scratch = [DMA, DMA, DMA((2,)), DMA((2,))]
+        self.scratch = [DMA, DMA((2,)), DMA((2,)), DMA((2,)), DMA]
 
     def bind(self, ins, outs, scratch):
         self.qkv, self.out_w, self.staged = ins
         self.target = outs[0]
-        self.send, self.recv, self.s_core, self.r_core = scratch
+        self.send, self.recv, self.s_core, self.r_core, self.s_relay = scratch
 
     def begin(self, place, low=0.0, high=1.0):
         sz = self.sz
@@ -850,10 +871,14 @@
                 @pl.loop(1, 2 * n)
                 def _(step):
                     index = lax.rem(mine + step, 2 * n)
-                    for source, target in pairs(index // n, own):
-                        remote(
-                            source, target, self.send, self.recv, at(x, index // n, k, lax.rem(index, n))
-                        ).start()
+                    ctx = lax.rem(index, n)
+
+                    @pl.when(jnp.logical_not(ends(n, z, ctx)))
+                    def _():
+                        recv = self.recv.at[jnp.where(relay_of(n, z, ctx), 1, 0)]
+                        for source, target in pairs(index // n, own):
+                            device = at(x, index // n, k, ctx)
+                            remote(source, target, self.send, recv, device).start()
 
                 for source, target in pairs(y, own):
                     pltpu.make_async_copy(source, target, self.send).start()
@@ -861,13 +886,42 @@
     def span(self, part, k):
         stretch = self.sz.width // 4
         return self.target.at[pl.ds(pl.multiple_of((part * 2 + k) * stretch, 16), stretch)]
+
+    def relay(self, place):
+        sz = self.sz
+        n = sz.ctx
+        x, y, k, z = place
+        if n != RELAYED:
+            return
+
+        @pl.when(inner(n, z))
+        def _():
+            arrived(self.target.at[pl.ds(0, 2 * sz.owned)], self.recv.at[1])
+            source = jnp.where(z == 1, n - 1, 0)
+            for head in range(2):
+                rows = ((head * 2 + k) * n + source) * sz.owned
+                span = self.target.at[pl.ds(pl.multiple_of(rows, 16), sz.owned)]
+                device = at(x, y, k, n - 1 - source)
+                remote(span, span, self.s_relay, self.recv.at[0], device).start()
 
     def middle(self, place):
         sz = self.sz
         x, y, k, z = place
         half = sz.width // 2
-        arrived(self.target.at[pl.ds(0, half - sz.owned)], self.recv)
-        arrived(self.target.at[pl.ds(0, half)], self.send)
+        two = 2 * sz.owned if sz.ctx == RELAYED else 0
+
+        @pl.when(inner(sz.ctx, z))
+        def _():
+            arrived(self.target.at[pl.ds(0, half - sz.owned - two)], self.recv.at[0])
+            arrived(self.target.at[pl.ds(0, half)], self.send)
+            if two:
+                arrived(self.target.at[pl.ds(0, two)], self.s_relay)
+
+        @pl.when(jnp.logical_not(inner(sz.ctx, z)))
+        def _():
+            arrived(self.target.at[pl.ds(0, half - sz.owned)], self.recv.at[0])
+            arrived(self.target.at[pl.ds(0, half - two)], self.send)
+
         for part in range(2):
             span = self.span(part, k)
             remote(span, span, self.s_core.at[part], self.r_core.at[part], at(x, y, 1 - k, z)).start()
@@ -1055,26 +1109,6 @@
             self.over(place).wait_recv()
 
 
-class ReadyShares(PlaneShares):
-    reach = 0
-
-    def __init__(self, sz, section, part, source):
-        self.sz, self.section, self.part = sz, section, part
-        self.ins = [(source, None)]
-        self.outs = [jax.ShapeDtypeStruct((sz.owned, sz.ff), BF)]
-        self.scratch = [DMA((2,)), DMA((5,)), DMA((2,))]
-
-    def bind(self, ins, outs, scratch):
-        self.source, self.row = ins[0], outs[0]
-        self.send, self.recv, self.local = scratch
-
-    def place_in(self, slot):
-        return self.row
-
-    def finish(self, place):
-        self.settled(place)
-
-
 class ReturnedHeads:
     reach = 0
 
@@ -1087,6 +1121,9 @@
             pltpu.VMEM((stretch, sz.atot), BF),
             pltpu.VMEM((stretch, sz.atot), BF),
             pltpu.VMEM((sz.ctx, sz.owned, sz.atot), BF),
+            pltpu.VMEM((sz.owned, sz.atot), BF),
+            pltpu.VMEM((sz.owned, sz.atot), F32),
+            DMA,
             DMA,
             DMA,
             DMA,
@@ -1104,7 +1141,10 @@
             self.got,
             self.summed,
             self.lined,
+            self.taken,
+            self.sum,
             self.load,
+            self.r_taken,
             self.s_core,
             self.r_core,
             self.s_line,
@@ -1148,8 +1188,46 @@
         self.own_rows(place).wait()
         self.core(place).wait_recv()
         self.summed[...] = (self.summed[...].astype(F32) + self.got[...].astype(F32)).astype(BF)
-        for step in range(1, self.sz.ctx):
-            self.line(place, step).start()
+        x, y, k, z = place
+        n = self.sz.ctx
+        for step in range(1, n):
+            ctx = lax.rem(z + step, n)
+            if n != RELAYED:
+                self.line(place, step).start()
+                continue
+
+            @pl.when(ends(n, z, ctx))
+            def _():
+                remote(
+                    self.summed.at[self.own(ctx)],
+                    self.taken,
+                    self.s_line.at[step],
+                    self.r_taken,
+                    at(x, y, k, jnp.where(z == 0, 1, n - 2)),
+                ).start()
+
+            @pl.when(jnp.logical_not(jnp.logical_or(ends(n, z, ctx), self.held(z, ctx))))
+            def _():
+                self.line(place, step).start()
+
+    def held(self, z, ctx):
+        n = self.sz.ctx
+        return jnp.logical_or(
+            jnp.logical_and(z == 1, ctx == n - 1), jnp.logical_and(z == n - 2, ctx == 0)
+        )
+
+    def relay(self, place):
+        n = self.sz.ctx
+        z = place[3]
+        if n != RELAYED:
+            return
+
+        @pl.when(inner(n, z))
+        def _():
+            arrived(self.taken, self.r_taken)
+            rows = self.own(jnp.where(z == 1, n - 1, 0))
+            self.summed[rows] = (self.summed[rows].astype(F32) + self.taken[...].astype(F32)).astype(BF)
+            self.line(place, 2).start()
 
     def homes(self, place, starting):
         x, y, k, z = place
@@ -1169,11 +1247,16 @@
 
     def late(self, place):
         x, y, k, z = place
-        total = self.summed[self.own(z)].astype(F32)
-        for step in range(1, self.sz.ctx):
-            self.line(place, step).wait_recv()
-            total = total + self.lined[step].astype(F32)
-        self.lined[0] = total.astype(BF)
+        n = self.sz.ctx
+        self.sum[...] = self.summed[self.own(z)].astype(F32)
+        for step in range(1, n):
+
+            @pl.when(jnp.logical_not(ends(n, z, lax.rem(z + n - step, n))))
+            def _():
+                self.line(place, step).wait_recv()
+                self.sum[...] += self.lined[step].astype(F32)
+
+        self.lined[0] = self.sum[...].astype(BF)
         self.homes(place, True)
 
     def finish(self, place):
@@ -1190,6 +1273,45 @@
                 @pl.when(group != 2 * x + y)
                 def _():
                     arrived(self.target.at[group], self.recv.at[group])
+
+
+class Placed:
+    reach = 0
+
+    def __init__(self, sz, first, second):
+        self.ins = [(first, None), (second, None)]
+        self.outs = [jax.ShapeDtypeStruct((2, sz.rows, sz.width), BF)]
+        self.scratch = [DMA((2,)), DMA((2,))]
+
+    def bind(self, ins, outs, scratch):
+        self.sources, self.target = ins, outs[0]
+        self.send, self.recv = scratch
+
+    def each(self, place, starting):
+        x, y, k, z = place
+        for section in range(2):
+            source, target = (self.sources[section], self.target.at[k])
+            own = jnp.logical_and(x == section, jnp.logical_and(x == y, y == k))
+
+            @pl.when(jnp.logical_not(own))
+            def _():
+                device = at(section, x, y, z)
+                copy = remote(source, target, self.send.at[section], self.recv.at[k], device)
+                copy.start() if starting else copy.wait_send()
+
+            if starting:
+
+                @pl.when(own)
+                def _():
+                    pltpu.make_async_copy(source, target, self.recv.at[k]).start()
+
+    def begin(self, place):
+        self.each(place, True)
+
+    def finish(self, place):
+        self.each(place, False)
+        for batch in range(2):
+            arrived(self.target.at[batch], self.recv.at[batch])
 
 
 def begin(jobs, place, low=0.0, high=1.0):
@@ -1602,6 +1724,7 @@
             heads.begin(place)
 
         columns_over(0).wait_recv()
+        heads.relay(place)
         first.begin(place)
         heads.middle(place)
         arrived(small_all.at[pl.ds(0, sz.total - 1)], r_small)
@@ -1640,7 +1763,7 @@
 
     def bind(self, ins, outs, scratch):
         self.target = outs[0]
-        self.send, self.recv, self.s_core, self.r_core = scratch
+        self.send, self.recv, self.s_core, self.r_core, self.s_relay = scratch
 
     def use(self, ins, outs):
         qkv, out_w, staged = self.named
@@ -1667,7 +1790,7 @@
         self.body, self.ins, self.outs, self.scratch = body, ins, outs, scratch
 
 
-def joined(sz, first, first_jobs, second, second_jobs, link, cores, collective_id, name):
+def joined(sz, first, first_jobs, second, second_jobs, link, slab, collective_id, name):
     a, b, c = len(first.ins), len(first.outs), len(first.scratch)
     count = len(first_jobs)
 
@@ -1676,8 +1799,8 @@
         x, y, k, z = place
         peers = pair_peers(x, y, k, z)
         near = list(peers) + line_peers(sz.ctx, x, y, k, z) + [at(x, y, 1 - k, z)]
-        if cores:
-            near.append(at(x, 1 - y, 1 - k, z))
+        if slab:
+            near += [at(x, 1 - y, 1 - k, z), at(1 - x, y, 1 - k, z), at(1 - x, 1 - y, 1 - k, z)]
         meet(sz, place, near, [peers[0], peers[2]], jobs)
         own, later = (jobs[:count], jobs[count:])
         first.body(ins[:a], outs[:b], scratch[:c], own, place)
@@ -1693,16 +1816,6 @@
         name,
     )
     return (results[:b], results[b:], extra[:count], extra[count:])
-
-
-def alone(sz, part, jobs, meeting, collective_id, name):
-    def body(ins, outs, scratch, jobs):
-        place = where_am_i()
-        meeting(place, jobs)
-        part.body(ins, outs, scratch, jobs, place)
-        finish(jobs, place)
-
-    return run_call(body, part.ins, part.outs, part.scratch, jobs, collective_id, name)
 
 
 def gather_pair(buffer, place, send, recv):
@@ -1733,15 +1846,6 @@
     for copy in copies:
         copy.start()
     return copies
-
-
-def meet_pair(sz, place, jobs, cores=False):
-    x, y, k, z = place
-    peers = pair_peers(x, y, k, z)
-    near = list(peers) + line_peers(sz.ctx, x, y, k, z)
-    if cores:
-        near += [at(x, y, 1 - k, z), at(x, 1 - y, 1 - k, z)]
-    meet(sz, place, near, [peers[0], peers[2]], jobs)
 
 
 def attend(sz, x_own, gain, bias, watt, tables, qpos, kpos):
@@ -1831,10 +1935,10 @@
     return Part(body, list(zip(arrays, specs)), [(shape, vmem()) for shape in shapes], scratch)
 
 
-def attend_back(sz, dh1, x_own, gain, watt, tables, qpos, kpos, kept, part_later=False):
+def attend_back(sz, dh1, x_own, gain, watt, tables, qpos, kpos, kept, plan):
     n, rows = sz.ctx, 4 * sz.rows
 
-    def body(ins, outs, scratch, jobs, place):
+    def body(ins, outs, scratch, jobs, place, after=None):
         dh1, x_ref, gain, watt, cosine, sine, qpos, kpos, n1_all, q_in, kv_all, o_in, lse_in = ins
         dx_out, dw_out, gain_grad, bias_grad = outs
         w, dh_all, dkv, dkv_in, da, parts, landed, w_sem, s_in, r_in, s_kv, r_kv, s_back, r_back = scratch
@@ -1843,12 +1947,12 @@
         load.start()
         group = 2 * x + y
         dh_all[group] = dh1[...].astype(BF)
+        after = plan(jobs, place) if after is None else after
         copies = gather_pair(dh_all, place, s_in, r_in)
-        jobs[0].begin(place)
+        after[0]()
         load.wait()
         gathered_pair(dh_all, place, copies, r_in)
-        for job in jobs[2:]:
-            job.begin(place)
+        after[1]()
         dh = dh_all[...].reshape(rows, sz.width)
         dout = mm(dh, w[:, sz.acols :]).astype(BF)
         keys = kv_all[:, :, : sz.kcols].reshape(n * rows, sz.kcols)
@@ -1884,7 +1988,7 @@
                 )
             )
             kv_copies[-1].start()
-        jobs[1].begin(place, (1,) if part_later else None)
+        after[2]()
         dw_out[:, sz.acols :] = mm(dh, o_in[...].astype(BF), TN).astype(BF)
         total = dkv[z].astype(F32)
         for step in range(n - 1):
@@ -1895,6 +1999,7 @@
         da[:, sz.qcols + sz.kcols :] = total[:, sz.kcols :].astype(BF)
         parts[...] = mm(da[...], w[:, : sz.acols], NT).astype(BF).reshape(4, sz.rows, sz.width)
         back = scatter_pair(parts, landed, place, s_back, r_back)
+        after[3]()
         dw_out[:, : sz.acols] = mm(n1_all[...].reshape(rows, sz.width), da[...], TN).astype(BF)
         bias_grad[...] = jnp.sum(da[...].astype(F32), axis=0, keepdims=True)
         for copy in copies + kv_copies:
@@ -2052,7 +2157,11 @@
             begin(jobs[1:], place, 0.75, 1.0)
             middle(jobs, place)
 
-        run_together(columns(0), columns(1), {(B, 0): started, (B, 8): later})
+        run_together(
+            columns(0),
+            columns(1),
+            {(B, 0): started, (A, 6): lambda: jobs[0].relay(place), (B, 8): later},
+        )
         for chunk, (gather, scatter) in enumerate(pairs):
             span = slice(chunk * rows, (chunk + 1) * rows)
             act_out[span] = (values[span] + scatter.result()).astype(BF)
@@ -2279,6 +2388,8 @@
                 job.middle(place)
 
         def down_grad():
+            for job in heads:
+                job.relay(place)
             kept[3].wait()
             kept[0].wait()
             weight_grad(2, dy_all, hm_in)
@@ -2336,54 +2447,76 @@
     return Part(body, list(zip(arrays, specs)), [(shape, vmem()) for shape in shapes], scratch)
 
 
-def collect(sz, small, acts, grads, shares, ready, jobs):
+def finale(sz, part, small, results, shares, line_jobs, head_jobs):
     n = sz.ctx
-    order = [(0, 2), (1, 1), (0, 0)]
-    last = (0, 1)
-    early = [2, 0]
+    a, count = len(part.ins), len(part.scratch)
+    order = [(1, 2), (1, 0), (1, 1), (0, 2), (0, 0), (0, 1)]
+    query_columns = QUERY_HEADS * HEAD_WIDTH_SIZE
+    key_columns = KEY_VALUE_HEADS * HEAD_WIDTH_SIZE
 
     def body(ins, outs, scratch, jobs):
-        small, act0, act1, grad0, grad1, *shares = ins
-        shares, ready = (shares[: len(order)], shares[len(order) :])
-        small_in, act_out, grad_out, w_out = outs
-        s_small, r_small, s_out, r_out, send, recv, local, s_over, r_over, s_ready, r_ready = scratch
-        line_job, *heads = jobs
+        small_given, grad1, *shares = ins[a:]
+        small_in, grad_out, w_out = outs
+        made = scratch[count : count + 4]
+        small, whole_bias, s_small, r_small, s_out, r_out, *sems = scratch[count + 4 :]
+        dx, dw, gain_grad, bias_grad = made
+        down_line, gate_line, up_line, *heads = jobs
         place = where_am_i()
         x, y, k, z = place
         me = x * sz.group + (y * 2 + k) * n + z
+        for job in heads[1:]:
+            job.source = dw
+        sources = [shares[2], shares[0], shares[1], down_line.target, gate_line.target, up_line.target]
+        moves = {
+            where: PlaneShares(sz, *where, source, w_out, [sem.at[number] for sem in sems])
+            for number, (where, source) in enumerate(zip(order, sources))
+        }
         greet_all(me, sz.total, lambda index: flat_place(index, sz.group, n))
-        line_job.begin(place)
-        for job in heads:
+
+        placed = Placed(sz, None, None)
+        placed.bind((dx, grad1), (grad_out,), (s_out, r_out))
+
+        def sent():
+            down_line.begin(place)
+            heads[0].begin(place)
+
+        def gathered():
+            moves[1, 2].begin(place)
+
+        def shared():
+            gate_line.begin(place)
+            up_line.begin(place)
+            down_line.finish(place)
+            moves[0, 2].begin(place)
+
+        def returned():
+            moves[0, 2].cross(place)
+            moves[1, 2].cross(place)
+
+        hooks = (sent, gathered, shared, returned)
+        part.body(ins[:a], made, scratch[:count], jobs, place, hooks)
+        for job in heads[1:]:
             job.begin(place)
-        moves = []
-        for number, (section, part) in enumerate(order + [last]):
-            sems = (
-                send.at[number],
-                recv.at[number],
-                local.at[number],
-                s_over.at[number],
-                r_over.at[number],
-            )
-            source = shares[number] if number < len(order) else line_job.target
-            moves.append(PlaneShares(sz, section, part, source, w_out, sems))
-        def over(number):
-            part = early[number]
-            cols = pl.ds(0, sz.plane * HB)
-            return remote(
-                ready[number].at[:, cols],
-                w_out.at[0, part, :, cols],
-                s_ready.at[number],
-                r_ready.at[number],
-                at(1 - x, y, k, z),
-            )
-
-        @pl.when(x == 0)
-        def _():
-            for number in range(len(early)):
-                over(number).start()
-
-        for move in moves[:-1]:
-            move.begin(place)
+        placed.begin(place)
+
+        small[...] = small_given[...]
+        whole_bias[...] = jnp.zeros_like(whole_bias)
+        starts = (
+            ((2 * x + y) * sz.qcols, sz.qcols),
+            (query_columns + x * sz.kcols, sz.kcols),
+            (query_columns + key_columns + x * sz.kcols, sz.kcols),
+        )
+        offset = 0
+        for start, size in starts:
+            whole_bias[:, pl.ds(pl.multiple_of(start, HB), size)] = bias_grad[:, offset : offset + size]
+            offset += size
+        wide = (query_columns + key_columns) // sz.group
+        thin = key_columns // sz.group
+        for row in range(sz.group):
+            small[row, 0:1, : sz.owned] = gain_grad[:, row * sz.owned : (row + 1) * sz.owned]
+            small[row, 2:3, :wide] = whole_bias[:, row * wide : (row + 1) * wide]
+            base = query_columns + key_columns + row * thin
+            small[row, 3:4, :thin] = whole_bias[:, base : base + thin]
 
         @pl.loop(1, sz.total)
         def _(step):
@@ -2393,61 +2526,28 @@
             ).start()
 
         pltpu.make_async_copy(small.at[me], small_in.at[me], s_small).start()
-
-        def results(starting):
-            for section in range(2):
-                for slot, (source, target) in enumerate(
-                    (((act0, act1)[section], act_out), ((grad0, grad1)[section], grad_out))
-                ):
-                    own = jnp.logical_and(x == section, jnp.logical_and(x == y, y == k))
-
-                    @pl.when(jnp.logical_not(own))
-                    def _():
-                        copy = remote(
-                            source,
-                            target.at[k],
-                            s_out.at[section, slot],
-                            r_out.at[slot, k],
-                            at(section, x, y, z),
-                        )
-                        copy.start() if starting else copy.wait_send()
-
-                    if starting:
-
-                        @pl.when(own)
-                        def _():
-                            pltpu.make_async_copy(source, target.at[k], r_out.at[slot, k]).start()
-
         for job in heads:
             job.middle(place)
-        moves[0].cross(place)
-        line_job.finish(place)
-        moves[-1].begin(place)
-        results(True)
-        moves[1].cross(place)
-        moves[2].cross(place)
+        gate_line.finish(place)
+        moves[0, 0].begin(place)
+        moves[1, 0].begin(place)
+        moves[0, 0].cross(place)
+        up_line.finish(place)
+        moves[0, 1].begin(place)
+        moves[1, 1].begin(place)
+        moves[1, 0].cross(place)
+        heads[0].relay(place)
+        moves[0, 1].cross(place)
+        heads[1].relay(place)
         heads[0].late(place)
-        moves[3].cross(place)
+        moves[1, 1].cross(place)
+        heads[2].relay(place)
         for job in heads[1:]:
             job.late(place)
-        results(False)
-
-        @pl.when(x == 0)
-        def _():
-            for number in range(len(early)):
-                over(number).wait_send()
-
-        @pl.when(x == 1)
-        def _():
-            for number in range(len(early)):
-                over(number).wait_recv()
-
-        for slot, target in enumerate((act_out, grad_out)):
-            for batch in range(2):
-                arrived(target.at[batch], r_out.at[slot, batch])
+        placed.finish(place)
         arrived(small_in.at[pl.ds(0, sz.total - 1)], r_small)
         arrived(small_in, s_small)
-        for move in moves:
+        for move in moves.values():
             move.finish(place)
         for job in heads:
             job.finish(place)
@@ -2455,31 +2555,35 @@
     shapes = (
         jax.ShapeDtypeStruct((sz.total, 8, LANES), F32),
         jax.ShapeDtypeStruct((2, sz.rows, sz.width), BF),
-        jax.ShapeDtypeStruct((2, sz.rows, sz.width), BF),
         jax.ShapeDtypeStruct((2, 3, sz.owned, sz.ff), BF),
     )
-    arrays = (small, *acts, *grads, *[shares[section][part] for section, part in order], *ready)
-    many = len(order) + 1
-    return run_call(
-        body,
-        [(array, hbm()) for array in arrays],
-        [(shape, hbm()) for shape in shapes],
-        [
+    many = len(order)
+    scratch = (
+        part.scratch
+        + [pltpu.VMEM(shape.shape, shape.dtype) for shape, _ in part.outs]
+        + [
+            pltpu.VMEM((sz.total, 8, LANES), F32),
+            pltpu.VMEM((1, query_columns + 2 * key_columns), F32),
             DMA,
             DMA,
-            DMA((2, 2)),
-            DMA((2, 2)),
+            DMA((2,)),
+            DMA((2,)),
             DMA((many, 2)),
             DMA((many, 5)),
             DMA((many, 2)),
             DMA((many,)),
             DMA((many,)),
-            DMA((len(early),)),
-            DMA((len(early),)),
-        ],
-        jobs,
-        2,
-        "collect_gradients",
+        ]
+    )
+    ins = part.ins + [(small, vmem())] + [(array, hbm()) for array in (*results, *shares)]
+    return run_call(
+        body,
+        ins,
+        [(shape, hbm()) for shape in shapes],
+        scratch,
+        line_jobs + head_jobs,
+        6,
+        "layer_last",
     )
 
 
@@ -2565,11 +2669,16 @@
         4,
         "layer_turn",
     )
-    acts = [act0, act1]
-
-    def attention_back(section, dh1, x_own, watt, kept):
-        return attend_back(
-            sz, dh1, x_own, gain1[section], watt, tables, qpos, kpos, kept, part_later=section == 1
+
+    def attention_back(section, dh1, x_own, watt, kept, plan=None):
+        return attend_back(sz, dh1, x_own, gain1[section], watt, tables, qpos, kpos, kept, plan)
+
+    def shares_between(jobs, place):
+        return (
+            lambda: jobs[0].begin(place),
+            lambda: jobs[2].begin(place),
+            lambda: jobs[1].begin(place, (1,)),
+            lambda: None,
         )
 
     def heads_linked(made, given, own, later):
@@ -2579,62 +2688,44 @@
     (
         (grad1, da1, gain1_grad1, bias_grad1),
         (dh1, dw0, gain2_grad0),
-        ((down_share1,), (gate_share1,)),
+        ((down_share1,), (gate_share1,), (act_out,)),
         ((up_share1,), (heads10,)),
     ) = joined(
         sz,
-        attention_back(1, dh1, act0, att1, kept_att1),
-        [LineShares(sz, 2, dw1), LineShares(sz, 0, dw1)],
+        attention_back(1, dh1, act0, att1, kept_att1, shares_between),
+        [LineShares(sz, 2, dw1), LineShares(sz, 0, dw1), Placed(sz, act0, act1)],
         feed_back(sz, mid0, gain2[0], (gate0, up0, down0), kept_feed),
         [LineShares(sz, 1, dw1), ReturnedHeads(sz, 1, 0, None)],
         heads_linked,
-        False,
+        True,
         5,
         "layer_backward",
     )
-    (grad0, da0, gain1_grad0, bias_grad0), ((down_share0,), (gate_share0,), *ready) = alone(
+    whole_bias = jnp.zeros((1, query_columns + 2 * key_columns), F32)
+    offset = 0
+    for start, size in starts:
+        part = bias_grad1[:, offset : offset + size]
+        whole_bias = lax.dynamic_update_slice(whole_bias, part, (0, start))
+        offset += size
+    split = query_columns + key_columns
+    rows = [gain1_grad1, gain2_grad1, whole_bias[:, :split], whole_bias[:, split:]]
+    rows = [line(row.reshape(group, -1))[:, None] for row in rows]
+    small1 = jnp.concatenate(rows + [jnp.zeros((group, 4, LANES), F32)], axis=1)
+    small0 = jnp.pad(line(gain2_grad0.reshape(group, -1))[:, None], ((0, 0), (1, 6), (0, 0)))
+    came_heads = [[None, None], [heads10, None]]
+    (small_in, grad_out, w_out), more = finale(
         sz,
         attention_back(0, dh1, tok_own, att0, kept_att0),
-        [LineShares(sz, 2, dw0), LineShares(sz, 0, dw0)]
-        + [ReadyShares(sz, 1, part, share) for part, share in ((2, down_share1), (0, gate_share1))],
-        lambda place, jobs: meet_pair(sz, place, jobs, True),
-        6,
-        "attend_backward",
-    )
-    grads = [grad0, grad1]
-    shares = [[gate_share0, None, down_share0], [gate_share1, up_share1, down_share1]]
-    came_heads = [[None, None], [heads10, None]]
-    smalls = []
-    for gain1_grad, gain2_grad, bias_grad in (
-        (gain1_grad0, gain2_grad0, bias_grad0),
-        (gain1_grad1, gain2_grad1, bias_grad1),
-    ):
-        whole_bias = jnp.zeros((1, query_columns + 2 * key_columns), F32)
-        offset = 0
-        for start, size in starts:
-            whole_bias = lax.dynamic_update_slice(
-                whole_bias, bias_grad[:, offset : offset + size], (0, start)
-            )
-            offset += size
-        split = query_columns + key_columns
-        rows = [gain1_grad, gain2_grad, whole_bias[:, :split], whole_bias[:, split:]]
-        rows = [line(row.reshape(group, -1))[:, None] for row in rows]
-        smalls.append(jnp.concatenate(rows + [jnp.zeros((group, 4, LANES), F32)], axis=1))
-    small_out = jnp.concatenate(smalls, axis=0)
-    jobs = [LineShares(sz, 1, dw0)]
-    jobs += [
-        ReturnedHeads(sz, section, part, da) for section, part, da in ((1, 1, da1), (0, 0, da0), (0, 1, da0))
-    ]
-    (small_in, act_out, grad_out, w_out), more = collect(
-        sz, small_out, acts, grads, shares, [array for (array,) in ready], jobs
-    )
-    (came_heads[1][1],), (came_heads[0][0],), (came_heads[0][1],) = more[1:]
+        jnp.concatenate([small0, small1], axis=0),
+        (grad1,),
+        (gate_share1, up_share1, down_share1),
+        [LineShares(sz, part, dw0) for part in (2, 0, 1)],
+        [ReturnedHeads(sz, 1, 1, da1), ReturnedHeads(sz, 0, 0, None), ReturnedHeads(sz, 0, 1, None)],
+    )
+    (came_heads[1][1],), (came_heads[0][0],), (came_heads[0][1],) = more[3:]
     small_sum = jnp.sum(small_in, axis=0)
-    here = jnp.logical_and(x == 1, jnp.arange(sz.ff) >= sz.plane * HB)
-    (down_ready,), (gate_ready,) = ready
-    gate = jnp.where(here, gate_ready, w_out[0, 0])
-    gate_up_grad = jnp.concatenate([gate, w_out[0, 1]], axis=1).astype(F32)[None]
-    down_grad = jnp.where(here, down_ready, w_out[0, 2]).astype(F32)[None]
+    gate_up_grad = jnp.concatenate([w_out[0, 0], w_out[0, 1]], axis=1).astype(F32)[None]
+    down_grad = w_out[0, 2].astype(F32)[None]
     by_y = [jnp.where(y == 0, parts[0], parts[1]) for parts in came_heads]
     att_sum = jnp.where(x == 0, by_y[0], by_y[1]).astype(F32)
     q_grad = att_sum[:, :, : sz.qcols].transpose(1, 0, 2).reshape(sz.owned, query_columns)

time: 753 us -> 730 us (0.969)
  Pallas kernels: 713 us -> 694 us
    pallas_call x6 -> x5, Pallas kernels: 713 us -> 694 us  [run_call(): pl.pallas_call(kernel, out_shape=tuple((shape for shape, _ in outs)), in_...]
where the time goes in v5:
time: 730 us; the launch traced here: 724 us
  Pallas kernels  694 us (95%)
  other arithmetic  15.4 us (2%)
  local copies, waits for them, and re-layouts  12.8 us (2%)
    pallas_call x5, Pallas kernels, run_call(): pl.pallas_call(kernel, out_shape=tuple((shape for shape, _ in outs)), in_...  694 us

profile of v5, /device:TPU:14, one launch (start us, length us, event | category | flops | bytes accessed | tf_op | source)
XLA Modules:
  0.0 724.0 jit_solution(11301165144548310739)
XLA Ops:
  0.7 0.1 pad.51.clone
  0.8 1.4 fusion.6.refs_0_
  2.1 71.0 %spread_weights.1 = (bf16[32,16,128]{2,1,0:T(8,128)(2,1)}, bf16[64,1536]{1,0:T(8,128)(2,1)}, bf16[64,1536]{1,0:T(8,128)(2,1)}, bf16[2,96,1024]{2,1,0:T(8,128)(2,...) custom-call(bf16[16,128]{1,0:T(8,128)(2,1)} %fusion.6.refs_0_, ...), custom_call_target="tpu_custom_call" | custom-call | tf_op jit(solution)/shard_map/spread_weights/pallas_call | solution.py:690
  73.2 0.9 bitcast_convert_fusion.1
  74.3 0.6 slice_bitcast_fusion.4
  74.9 0.1 reshape.135
  75.0 0.1 convert_element_type.65
  75.1 0.1 broadcast_multiply_fusion
  75.2 1.2 sine_multiply_fusion
  76.5 0.8 reshape.149.refs_6_
  77.3 0.7 reshape.137.refs_7_
  78.0 0.7 squeeze.44.refs_1_.refs_2_
  78.7 0.7 squeeze.46.refs_8_.refs_14_
  79.3 143.0 %layer_forward.1 = (f32[64,1536]{1,0:T(8,128)}, bf16[4,64,1536]{2,1,0:T(8,128)(2,1)}, bf16[256,384]{1,0:T(8,128)(2,1)}, bf16[4,256,256]{2,1,0:T(8,128)(2,1)}, f3...) custom-call(bf16[64,1536]{1,0:T(8,128)(2,1)} %get-tuple-element.59.r, ...), custom_call_target="tpu_custom_call" | custom-call | tf_op jit(solution)/shard_map/layer_forward/pallas_call | solution.py:690
  222.4 0.7 squeeze.47.refs_1_.refs_2_
  223.0 0.7 squeeze.49.refs_9_
  223.7 189.9 %layer_turn.1 = (f32[64,1536]{1,0:T(8,128)}, bf16[4,64,1536]{2,1,0:T(8,128)(2,1)}, bf16[256,384]{1,0:T(8,128)(2,1)}, bf16[4,256,256]{2,1,0:T(8,128)(2,1)}, f32[2...) custom-call(bf16[64,1536]{1,0:T(8,128)(2,1)} %get-tuple-element.65.r, ...), custom_call_target="tpu_custom_call" | custom-call | tf_op jit(solution)/shard_map/layer_turn/pallas_call | solution.py:690
  413.6 143.0 %layer_backward.1 = (bf16[64,1536]{1,0:T(8,128)(2,1)}, bf16[1536,1024]{1,0:T(8,128)(2,1)}, f32[1,1536]{1,0:T(1,128)}, f32[1,640]{1,0:T(1,128)}, f32[64,1536]{1,0...) custom-call(f32[64,1536]{1,0:T(8,128)} %get-tuple-element.69.refs_0_, ...), custom_call_target="tpu_custom_call" | custom-call | tf_op jit(solution)/shard_map/layer_backward/pallas_call | solution.py:690
  556.6 0.6 constant_dynamic-update-slice_fusion.2
  557.2 0.7 constant_dynamic-update-slice_fusion.1
  557.9 0.6 constant_dynamic-update-slice_fusion
  558.5 0.1 reshape.141
  558.7 0.1 reshape.142
  558.7 0.7 reduce.5
  559.5 0.1 reshape.139
  559.6 0.1 reshape.140
  559.7 0.1 concatenate.35
  559.7 0.7 reduce.4
  560.5 0.1 reshape.138
  560.5 0.7 select_maximum_fusion.refs_13_
  561.2 147.4 %layer_last.1 = (f32[32,8,128]{2,1,0:T(8,128)}, bf16[2,64,1536]{2,1,0:T(8,128)(2,1)}, bf16[2,3,96,8960]{3,2,1,0:T(8,128)(2,1)}, bf16[4,4,96,384]{3,2,1,0:T(8,128...) custom-call(f32[64,1536]{1,0:T(8,128)} %get-tuple-element.85.refs_0_, ...), custom_call_target="tpu_custom_call" | custom-call | tf_op jit(solution)/shard_map/layer_last/pallas_call | solution.py:690
  708.7 4.7 bitcast_convert_fusion
  713.4 3.5 maximum_convert_fusion
  716.9 0.2 select_convert_fusion
  717.1 0.1 slice_bitcast_fusion.2
  717.2 0.1 copy.62
  717.2 0.2 reshape.144
  717.5 0.3 reduce_sum.19
  717.8 0.2 copy.56
  717.9 0.2 reshape.145
  718.1 0.9 maximum_bitcast_fusion
  719.1 0.4 copy.57
  719.5 1.1 reshape.146
  720.5 0.5 fusion.9
  721.1 0.5 slice.92
  721.6 0.5 slice.93
  722.1 0.7 copy.68
  722.8 0.7 copy.69
  (45 shorter events, 0.4 us)
Async XLA Ops:
  0.6 74.2 %copy-start = (s32[2,1024]{1,0:T(2,128)S(1)}, s32[2,1024]{1,0:T(2,128)}, u32[]{:S(2)}) copy-start(s32[2,1024]{1,0:T(2,128)} %param.11) | copy-start | bytes 24580
  413.6 145.9 %copy-start.9 = (f32[1,1536]{1,0:T(1,128)S(1)}, f32[1,1536]{1,0:T(1,128)}, u32[]{:S(2)}) copy-start(f32[1,1536]{1,0:T(1,128)} %get-tuple-element.93) | copy-start | bytes 18436
  713.4 3.5 copy-start.2
  713.4 3.5 copy-start.3
  713.4 3.5 copy-start.4
  713.4 3.5 copy-start.5
  718.1 2.4 copy-start.8
  718.1 4.0 copy-start.6
  719.1 3.8 copy-start.7
  719.1 4.5 copy-start.1

commit v6 on v5

--- a/solution.py
+++ b/solution.py
@@ -1011,14 +1011,11 @@
 
 
 class PlaneShares:
-    def __init__(self, sz, section, part, source, target, sems):
+    def __init__(self, sz, section, part, source, own, other, sems):
         self.sz, self.section, self.part = sz, section, part
-        self.source, self.target = source, target
+        self.source, self.own, self.other = source, own, other
         self.send, self.recv, self.local, self.s_over, self.r_over = sems
-        self.row = target.at[0, part]
-
-    def place_in(self, slot):
-        return self.target.at[slot, self.part]
+        self.base = sz.ff if part == 1 else 0
 
     def begin(self, place):
         sz = self.sz
@@ -1026,17 +1023,16 @@
         x, y, k, z = place
         head = y * 2 + k
         wide = sz.least * HB
-        slot = jnp.where(x == self.section, 0, 1)
-
-        def go(to, device, local):
+
+        def go(to, device, local, result):
             for ctx in range(n):
                 owner = x * sz.group + head * n + ctx
                 first = first_column(sz, owner)
 
                 def one(kind, offset, width):
                     source = self.source.at[ctx, to, :, pl.ds(offset, width)]
-                    cols = pl.ds(pl.multiple_of(first + offset, HB), width)
-                    target = self.place_in(slot).at[:, cols]
+                    cols = pl.ds(pl.multiple_of(self.base + first + offset, HB), width)
+                    target = result.at[:, cols]
                     if local:
                         pltpu.make_async_copy(source, target, self.local.at[kind]).start()
                     else:
@@ -1050,10 +1046,18 @@
                     def _():
                         one(1, wide, HB)
 
-        for step in range(1, 4):
-            to = lax.rem(head + step, 4)
-            go(to, (x, to, z), False)
-        go(head, None, True)
+        for own in (True, False):
+
+            @pl.when((x == self.section) == own)
+            def _():
+                result = self.own if own else self.other
+
+                @pl.loop(1, 4)
+                def _(step):
+                    to = lax.rem(head + step, 4)
+                    go(to, (x, to, z), False, result)
+
+                go(head, None, True, result)
 
     def settled(self, place):
         sz = self.sz
@@ -1061,7 +1065,7 @@
         x, y, k, z = place
         head = y * 2 + k
         wide = sz.least * HB
-        row = self.row
+        row = self.own
         arrived(row.at[:, pl.ds(0, 3 * n * wide)], self.recv.at[0])
         arrived(row.at[:, pl.ds(0, 3 * n * wide)], self.send.at[0])
         arrived(row.at[:, pl.ds(0, n * wide)], self.local.at[0])
@@ -1088,10 +1092,10 @@
     def over(self, place):
         x, y, k, z = place
         plane = 1 - self.section
-        cols = pl.ds(plane * self.sz.plane * HB, self.sz.plane * HB)
+        cols = pl.ds(self.base + plane * self.sz.plane * HB, self.sz.plane * HB)
         return remote(
-            self.target.at[1, self.part, :, cols],
-            self.target.at[0, self.part, :, cols],
+            self.other.at[:, cols],
+            self.own.at[:, cols],
             self.s_over,
             self.r_over,
             at(1 - x, y, k, z),
@@ -1848,11 +1852,12 @@
     return copies
 
 
-def attend(sz, x_own, gain, bias, watt, tables, qpos, kpos):
+def attend(sz, section, x_own, gain, bias, watt, tables, qpos, kpos):
     n, rows = sz.ctx, 4 * sz.rows
 
     def body(ins, outs, scratch, jobs, place):
-        x_ref, gain, bias, watt, cosine, sine, qpos, kpos = ins
+        x_ref, gains, biases, watt, cosine, sine, qpos, kpos = ins
+        gain, bias = (gains[section : section + 1], biases[section : section + 1])
         h1_out, n1_all, q_out, kv_all, o_out, lse_out = outs
         w, parts, landed, w_sem, s_in, r_in, s_kv, r_kv, s_back, r_back = scratch
         x, y, k, z = place
@@ -1860,7 +1865,7 @@
         load.start()
         group = 2 * x + y
         values = x_ref[...].astype(F32)
-        n1_all[group] = (values * row_norm(values) * gain[...]).astype(BF)
+        n1_all[group] = (values * row_norm(values) * gain).astype(BF)
         copies = gather_pair(n1_all, place, s_in, r_in)
         begin(jobs, place, 0.0, 0.3)
         load.wait()
@@ -1935,11 +1940,11 @@
     return Part(body, list(zip(arrays, specs)), [(shape, vmem()) for shape in shapes], scratch)
 
 
-def attend_back(sz, dh1, x_own, gain, watt, tables, qpos, kpos, kept, plan):
+def attend_back(sz, section, dh1, x_own, gain, watt, tables, qpos, kpos, kept, plan):
     n, rows = sz.ctx, 4 * sz.rows
 
     def body(ins, outs, scratch, jobs, place, after=None):
-        dh1, x_ref, gain, watt, cosine, sine, qpos, kpos, n1_all, q_in, kv_all, o_in, lse_in = ins
+        dh1, x_ref, gains, watt, cosine, sine, qpos, kpos, n1_all, q_in, kv_all, o_in, lse_in = ins
         dx_out, dw_out, gain_grad, bias_grad = outs
         w, dh_all, dkv, dkv_in, da, parts, landed, w_sem, s_in, r_in, s_kv, r_kv, s_back, r_back = scratch
         x, y, k, z = place
@@ -2010,7 +2015,7 @@
             dn1 = dn1 + landed[i].astype(F32)
         values = x_ref[...].astype(F32)
         inverse = row_norm(values)
-        weighted = dn1 * gain[...]
+        weighted = dn1 * gains[section : section + 1]
         inner = jnp.mean(weighted * values, axis=-1, keepdims=True)
         dx = dh1[...] + inverse * weighted - values * (inverse * inverse * inverse) * inner
         dx_out[...] = dx.astype(BF)
@@ -2114,7 +2119,7 @@
         hidden_weights = HiddenWeights(sz, place, sources, w, w_sems)
         pairs = halves(n, rows, n2_all, place, refs)
         values = h1[...]
-        normed = (values * row_norm(values) * gain[...]).astype(BF)
+        normed = (values * row_norm(values) * gain[2:3]).astype(BF)
         for chunk in range(CHUNKS):
             n2_all[chunk, k, 2 * x + y, z] = normed[chunk * rows : (chunk + 1) * rows]
 
@@ -2203,7 +2208,7 @@
         ]
         values = h1[...]
         inverse = row_norm(values)
-        n2_all[k, 2 * x + y, z] = (values * inverse * gain[...]).astype(BF)
+        n2_all[k, 2 * x + y, z] = (values * inverse * gain[3:4]).astype(BF)
         dy_all[k, 2 * x + y, z] = dy[...]
 
         waiting = []
@@ -2288,7 +2293,7 @@
         dn2 = scatter_b.result()
         values = h1[...]
         inverse = row_norm(values)
-        weighted = dn2 * gain[...]
+        weighted = dn2 * gain[3:4]
         inner = jnp.mean(weighted * values, axis=-1, keepdims=True)
         dh1_out[...] = (
             dy[...].astype(F32) + inverse * weighted - values * (inverse * inverse * inverse) * inner
@@ -2412,7 +2417,7 @@
         dn2 = jnp.concatenate([scatter.result() for _, scatter in pairs], axis=0)
         values = h1[...]
         inverse = row_norm(values)
-        weighted = dn2 * gain[...]
+        weighted = dn2 * gain[2:3]
         inner = jnp.mean(weighted * values, axis=-1, keepdims=True)
         dh1_out[...] = (
             dy[...].astype(F32) + inverse * weighted - values * (inverse * inverse * inverse) * inner
@@ -2447,7 +2452,7 @@
     return Part(body, list(zip(arrays, specs)), [(shape, vmem()) for shape in shapes], scratch)
 
 
-def finale(sz, part, small, results, shares, line_jobs, head_jobs):
+def finale(sz, part, vectors, results, shares, line_jobs, head_jobs):
     n = sz.ctx
     a, count = len(part.ins), len(part.scratch)
     order = [(1, 2), (1, 0), (1, 1), (0, 2), (0, 0), (0, 1)]
@@ -2455,8 +2460,8 @@
     key_columns = KEY_VALUE_HEADS * HEAD_WIDTH_SIZE
 
     def body(ins, outs, scratch, jobs):
-        small_given, grad1, *shares = ins[a:]
-        small_in, grad_out, w_out = outs
+        gain1_grad1, bias_grad1, gain2_grad0, gain2_grad1, grad1, *shares = ins[a:]
+        small_in, grad_out, gate_up_out, down_out, gate_up_other, down_other = outs
         made = scratch[count : count + 4]
         small, whole_bias, s_small, r_small, s_out, r_out, *sems = scratch[count + 4 :]
         dx, dw, gain_grad, bias_grad = made
@@ -2468,7 +2473,13 @@
             job.source = dw
         sources = [shares[2], shares[0], shares[1], down_line.target, gate_line.target, up_line.target]
         moves = {
-            where: PlaneShares(sz, *where, source, w_out, [sem.at[number] for sem in sems])
+            where: PlaneShares(
+                sz,
+                *where,
+                source,
+                *((down_out, down_other) if where[1] == 2 else (gate_up_out, gate_up_other)),
+                [sem.at[number] for sem in sems],
+            )
             for number, (where, source) in enumerate(zip(order, sources))
         }
         greet_all(me, sz.total, lambda index: flat_place(index, sz.group, n))
@@ -2499,24 +2510,31 @@
             job.begin(place)
         placed.begin(place)
 
-        small[...] = small_given[...]
-        whole_bias[...] = jnp.zeros_like(whole_bias)
         starts = (
             ((2 * x + y) * sz.qcols, sz.qcols),
             (query_columns + x * sz.kcols, sz.kcols),
             (query_columns + key_columns + x * sz.kcols, sz.kcols),
         )
-        offset = 0
-        for start, size in starts:
-            whole_bias[:, pl.ds(pl.multiple_of(start, HB), size)] = bias_grad[:, offset : offset + size]
-            offset += size
         wide = (query_columns + key_columns) // sz.group
         thin = key_columns // sz.group
-        for row in range(sz.group):
-            small[row, 0:1, : sz.owned] = gain_grad[:, row * sz.owned : (row + 1) * sz.owned]
-            small[row, 2:3, :wide] = whole_bias[:, row * wide : (row + 1) * wide]
-            base = query_columns + key_columns + row * thin
-            small[row, 3:4, :thin] = whole_bias[:, base : base + thin]
+        small[...] = jnp.zeros_like(small)
+        for section, (gain1, gain2, bias) in enumerate(
+            ((gain_grad, gain2_grad0, bias_grad), (gain1_grad1, gain2_grad1, bias_grad1))
+        ):
+            whole_bias[...] = jnp.zeros_like(whole_bias)
+            offset = 0
+            for start, size in starts:
+                cols = pl.ds(pl.multiple_of(start, HB), size)
+                whole_bias[:, cols] = bias[:, offset : offset + size]
+                offset += size
+            for owner in range(sz.group):
+                row = section * sz.group + owner
+                own = slice(owner * sz.owned, (owner + 1) * sz.owned)
+                small[row, 0:1, : sz.owned] = gain1[:, own]
+                small[row, 1:2, : sz.owned] = gain2[:, own]
+                small[row, 2:3, :wide] = whole_bias[:, owner * wide : (owner + 1) * wide]
+                base = query_columns + key_columns + owner * thin
+                small[row, 3:4, :thin] = whole_bias[:, base : base + thin]
 
         @pl.loop(1, sz.total)
         def _(step):
@@ -2555,7 +2573,10 @@
     shapes = (
         jax.ShapeDtypeStruct((sz.total, 8, LANES), F32),
         jax.ShapeDtypeStruct((2, sz.rows, sz.width), BF),
-        jax.ShapeDtypeStruct((2, 3, sz.owned, sz.ff), BF),
+        jax.ShapeDtypeStruct((sz.owned, 2 * sz.ff), BF),
+        jax.ShapeDtypeStruct((sz.owned, sz.ff), BF),
+        jax.ShapeDtypeStruct((sz.owned, 2 * sz.ff), BF),
+        jax.ShapeDtypeStruct((sz.owned, sz.ff), BF),
     )
     many = len(order)
     scratch = (
@@ -2575,7 +2596,7 @@
             DMA((many,)),
         ]
     )
-    ins = part.ins + [(small, vmem())] + [(array, hbm()) for array in (*results, *shares)]
+    ins = part.ins + [(vector, vmem()) for vector in vectors] + [(array, hbm()) for array in (*results, *shares)]
     return run_call(
         body,
         ins,
@@ -2617,8 +2638,7 @@
         sz, small, tokens, cotangent, qkv_weight, out_weight, gate_up_weight, down_weight
     )
     per_section = small_all.reshape(2, group, 16, LANES).astype(F32)
-    gain1 = per_section[:, :, 0, : sz.owned].reshape(2, 1, sz.width)
-    gain2 = per_section[:, :, 1, : sz.owned].reshape(2, 1, sz.width)
+    gains = per_section[:, :, :2, : sz.owned].transpose(2, 0, 1, 3).reshape(4, sz.width)
     bias = per_section[:, :, 2, :bias_owned].reshape(2, 1, group * bias_owned)
     query_columns = QUERY_HEADS * HEAD_WIDTH_SIZE
     key_columns = KEY_VALUE_HEADS * HEAD_WIDTH_SIZE
@@ -2630,7 +2650,7 @@
     )
     own_bias = jnp.concatenate(
         [lax.dynamic_slice_in_dim(bias, start, size, 2) for start, size in starts], axis=2
-    )
+    )[:, 0]
     ordered = lax.dynamic_index_in_dim(positions, k, 0, keepdims=False)
     ordered = ordered.reshape(4, n, sz.rows).transpose(1, 0, 2)
     own_pos = lax.dynamic_index_in_dim(ordered, z, 0, keepdims=False).reshape(4 * sz.rows)
@@ -2645,13 +2665,13 @@
         return Columns(sz, section, part, gate_up_weight, down_weight, cols_x)
 
     def attention(section, x_own, watt):
-        return attend(sz, x_own, gain1[section], own_bias[section], watt, tables, qpos, kpos)
+        return attend(sz, section, x_own, gains, own_bias, watt, tables, qpos, kpos)
 
     (mid0, *kept_att0), (act0, *kept_feed), ((up0,), (down0,)), ((att1,), (gate1,)) = joined(
         sz,
         attention(0, tok_own, att0),
         [columns(0, 1), columns(0, 2)],
-        feed(sz, gain2[0], gate0),
+        feed(sz, gains, gate0),
         [Heads(sz, 1, qkv_weight, out_weight, heads_x), columns(1, 0)],
         lambda made, given, own, later: (made[0], *given, own[0].target, own[1].target),
         False,
@@ -2662,7 +2682,7 @@
         sz,
         attention(1, act0, att1),
         [columns(1, 1)],
-        both(sz, cot_own, gain2[1], gate1),
+        both(sz, cot_own, gains, gate1),
         [columns(1, 2)],
         lambda made, given, own, later: (given[0], made[0], *given[1:], own[0].target, later[0].target),
         False,
@@ -2671,7 +2691,9 @@
     )
 
     def attention_back(section, dh1, x_own, watt, kept, plan=None):
-        return attend_back(sz, dh1, x_own, gain1[section], watt, tables, qpos, kpos, kept, plan)
+        return attend_back(
+            sz, section, dh1, x_own, gains, watt, tables, qpos, kpos, kept, plan
+        )
 
     def shares_between(jobs, place):
         return (
@@ -2694,29 +2716,18 @@
         sz,
         attention_back(1, dh1, act0, att1, kept_att1, shares_between),
         [LineShares(sz, 2, dw1), LineShares(sz, 0, dw1), Placed(sz, act0, act1)],
-        feed_back(sz, mid0, gain2[0], (gate0, up0, down0), kept_feed),
+        feed_back(sz, mid0, gains, (gate0, up0, down0), kept_feed),
         [LineShares(sz, 1, dw1), ReturnedHeads(sz, 1, 0, None)],
         heads_linked,
         True,
         5,
         "layer_backward",
     )
-    whole_bias = jnp.zeros((1, query_columns + 2 * key_columns), F32)
-    offset = 0
-    for start, size in starts:
-        part = bias_grad1[:, offset : offset + size]
-        whole_bias = lax.dynamic_update_slice(whole_bias, part, (0, start))
-        offset += size
-    split = query_columns + key_columns
-    rows = [gain1_grad1, gain2_grad1, whole_bias[:, :split], whole_bias[:, split:]]
-    rows = [line(row.reshape(group, -1))[:, None] for row in rows]
-    small1 = jnp.concatenate(rows + [jnp.zeros((group, 4, LANES), F32)], axis=1)
-    small0 = jnp.pad(line(gain2_grad0.reshape(group, -1))[:, None], ((0, 0), (1, 6), (0, 0)))
     came_heads = [[None, None], [heads10, None]]
-    (small_in, grad_out, w_out), more = finale(
+    (small_in, grad_out, gate_up_out, down_out, _, _), more = finale(
         sz,
         attention_back(0, dh1, tok_own, att0, kept_att0),
-        jnp.concatenate([small0, small1], axis=0),
+        (gain1_grad1, bias_grad1, gain2_grad0, gain2_grad1),
         (grad1,),
         (gate_share1, up_share1, down_share1),
         [LineShares(sz, part, dw0) for part in (2, 0, 1)],
@@ -2724,8 +2735,8 @@
     )
     (came_heads[1][1],), (came_heads[0][0],), (came_heads[0][1],) = more[3:]
     small_sum = jnp.sum(small_in, axis=0)
-    gate_up_grad = jnp.concatenate([w_out[0, 0], w_out[0, 1]], axis=1).astype(F32)[None]
-    down_grad = w_out[0, 2].astype(F32)[None]
+    gate_up_grad = gate_up_out.astype(F32)[None]
+    down_grad = down_out.astype(F32)[None]
     by_y = [jnp.where(y == 0, parts[0], parts[1]) for parts in came_heads]
     att_sum = jnp.where(x == 0, by_y[0], by_y[1]).astype(F32)
     q_grad = att_sum[:, :, : sz.qcols].transpose(1, 0, 2).reshape(sz.owned, query_columns)

time: 730 us -> 725 us (level)
    convert_element_type x3 -> x0, other arithmetic: 9.11 us -> none  [the longest x1 4.7 us: local_columns(): down_grad = w_out[0, 2].astype(F32)[None]]
where the time goes in v6:
time: 725 us; the launch traced here: 719 us
  Pallas kernels  694 us (96%)
  other arithmetic  12.5 us (2%)
  local copies, waits for them, and re-layouts  10.9 us (2%)
    pallas_call x5, Pallas kernels, run_call(): pl.pallas_call(kernel, out_shape=tuple((shape for shape, _ in outs)), in_...  694 us

profile of v6, /device:TPU:14, one launch (start us, length us, event | category | flops | bytes accessed | tf_op | source)
XLA Modules:
  0.0 719.1 jit_solution(9966105397325991232)
XLA Ops:
  0.6 0.0 copy-start
  0.7 0.1 pad.19.clone
  0.8 1.4 fusion.6.refs_0_
  2.2 0.0 copy-done
  2.2 0.1 reshape.73
  2.3 0.1 convert_element_type.34
  2.4 0.7 reshape.75.refs_7_
  3.1 0.8 reshape.83.refs_6_
  3.9 0.1 broadcast_multiply_fusion
  4.0 1.2 sine_multiply_fusion
  5.2 71.1 %spread_weights.1 = (bf16[32,16,128]{2,1,0:T(8,128)(2,1)}, bf16[64,1536]{1,0:T(8,128)(2,1)}, bf16[64,1536]{1,0:T(8,128)(2,1)}, bf16[2,96,1024]{2,1,0:T(8,128)(2,...) custom-call(bf16[16,128]{1,0:T(8,128)(2,1)} %fusion.6.refs_0_, ...), custom_call_target="tpu_custom_call" | custom-call | tf_op jit(solution)/shard_map/spread_weights/pallas_call | solution.py:690
  76.3 0.9 slice.37
  77.2 0.9 slice.36
  78.0 0.7 reshape.72.refs_1_.refs_8_.refs_9_.refs_2_.refs_14_
  78.8 0.6 maximum_bitcast_fusion.1.refs_2_
  79.4 143.1 %layer_forward.1 = (f32[64,1536]{1,0:T(8,128)}, bf16[4,64,1536]{2,1,0:T(8,128)(2,1)}, bf16[256,384]{1,0:T(8,128)(2,1)}, bf16[4,256,256]{2,1,0:T(8,128)(2,1)}, f3...) custom-call(bf16[64,1536]{1,0:T(8,128)(2,1)} %get-tuple-element.60.r, ...), custom_call_target="tpu_custom_call" | custom-call | tf_op jit(solution)/shard_map/layer_forward/pallas_call | solution.py:690
  222.5 189.5 %layer_turn.1 = (f32[64,1536]{1,0:T(8,128)}, bf16[4,64,1536]{2,1,0:T(8,128)(2,1)}, bf16[256,384]{1,0:T(8,128)(2,1)}, bf16[4,256,256]{2,1,0:T(8,128)(2,1)}, f32[2...) custom-call(bf16[64,1536]{1,0:T(8,128)(2,1)} %get-tuple-element.66.r, ...), custom_call_target="tpu_custom_call" | custom-call | tf_op jit(solution)/shard_map/layer_turn/pallas_call | solution.py:690
  412.0 143.4 %layer_backward.1 = (bf16[64,1536]{1,0:T(8,128)(2,1)}, bf16[1536,1024]{1,0:T(8,128)(2,1)}, f32[1,1536]{1,0:T(1,128)}, f32[1,640]{1,0:T(1,128)}, f32[64,1536]{1,0...) custom-call(f32[64,1536]{1,0:T(8,128)} %get-tuple-element.70.refs_0_, ...), custom_call_target="tpu_custom_call" | custom-call | tf_op jit(solution)/shard_map/layer_backward/pallas_call | solution.py:690
  555.4 0.0 copy-start.4
  555.4 147.3 %layer_last.1 = (f32[32,8,128]{2,1,0:T(8,128)}, bf16[2,64,1536]{2,1,0:T(8,128)(2,1)}, bf16[96,17920]{1,0:T(8,128)(2,1)}, bf16[96,8960]{1,0:T(8,128)(2,1)}, bf16[...) custom-call(f32[64,1536]{1,0:T(8,128)} %get-tuple-element.86.refs_0_, ...), custom_call_target="tpu_custom_call" | custom-call | tf_op jit(solution)/shard_map/layer_last/pallas_call | solution.py:690
  702.8 0.9 reduce_sum.18
  703.7 0.5 slice.31
  704.2 0.5 slice.30
  704.7 0.5 fusion.8
  705.2 0.0 copy-done.4
  705.2 1.5 select_convert_fusion
  706.8 0.1 slice_bitcast_fusion
  706.9 0.4 copy.49
  707.3 1.1 reshape.79
  708.4 0.2 reshape.77
  708.6 0.3 reduce_sum.19
  708.9 0.0 copy-start.3
  708.9 0.2 copy.48
  709.1 0.2 reshape.78
  709.2 0.1 copy.52
  709.3 0.9 maximum_bitcast_fusion
  710.2 0.2 copy-done.3
  710.5 0.0 copy-start.2
  710.5 2.0 bitcast_convert_fusion.1
  712.5 1.2 copy-done.2
  713.7 0.0 copy-start.5
  713.7 0.0 copy-start.6
  713.7 3.5 bitcast_convert_fusion
  717.2 0.0 copy-done.5
  717.2 0.7 copy.57
  717.9 0.0 copy-done.6
  717.9 0.7 copy.58
  718.7 0.0 copy-done.1
  (13 shorter events, 0.2 us)
Async XLA Ops:
  0.6 1.5 copy-start
  555.4 149.8 %copy-start.4 = (bf16[4,96,1024]{2,1,0:T(8,128)(2,1)S(1)}, bf16[4,96,1024]{2,1,0:T(8,128)(2,1)}, u32[]{:S(2)}) copy-start(bf16[4,96,1024]{2,1,0:T(8,128)(2,1)} %get-tuple-element.106) | copy-start | bytes 2359300
  708.9 1.6 copy-start.3
  710.5 3.2 copy-start.2
  713.7 3.5 copy-start.5
  713.7 4.2 copy-start.6
  713.7 5.0 copy-start.1
